TPU v7x, 512 devices: a whole 4x8x8 slice. The times are simulated.
512 devices in a mesh: rep: 32 (over z, x), bn: 16 (over y, core).
Axes of the slice: x: 4, y: 8, z: 8, core: 2. Of those that a mesh axis runs over, the one named last changes fastest.
Arguments:
- block_input: bfloat16 [200704, 2048], P(('rep', 'bn')), may hold values from -6 to 6
- activations: bfloat16 [200704, 512], P(('rep', 'bn')), as said below
- conv_weight: bfloat16 [512, 2048], P('bn'), may hold values from -6 to 6
- bn_gain: float32 [2048], replicated, may hold values from 0.5 to 1.5
- bn_shift: float32 [2048], replicated, may hold values from -3 to 3
- out_grad: bfloat16 [200704, 2048], P(('rep', 'bn')), may hold values from -6 to 6
- velocity: float32 [512, 2048], P('bn'), may hold values from -6 to 6
Outputs:
- act_grad: bfloat16 [200704, 512], P(('rep', 'bn'))
- gain_grad: float32 [2048], replicated
- shift_grad: float32 [2048], replicated
- new_velocity: float32 [512, 2048], P('bn')
Inputs may be any that keep to these rules, and one draw needn't show every extreme that they name: `activations`: entries are nonnegative.
All inputs are finite; a program needn't handle non-finite values.
Results may differ from a plain program's by a relative error of at most 0.015.
Values may be sent and summed in bfloat16 or wider, within the bound.
No kernel may reach another device: no remote copies, remote signals or barrier semaphores. Data moves between devices by JAX's collectives and lax.ppermute only.
A program may use at most 64 MiB of HBM per device.

v0:
```python
import jax
import jax.numpy as jnp
from jax import lax
from jax.sharding import PartitionSpec as P

epsilon = 1e-05
weight_decay = 5e-05
momentum = 0.9


def local(block_input, activations, conv_weight, bn_gain, bn_shift, out_grad, velocity):
    rows = activations.shape[0]
    group_rows = rows * lax.axis_size("bn")
    full_weight = lax.all_gather(conv_weight, "bn", axis=0, tiled=True)
    conv_out = jnp.dot(activations, full_weight, preferred_element_type=jnp.float32)
    chan_total = lax.psum(jnp.sum(conv_out, axis=0), "bn")
    chan_mean = chan_total / group_rows
    centered = conv_out - chan_mean
    variance = lax.psum(jnp.sum(centered * centered, axis=0), "bn") / group_rows
    inv_std = lax.rsqrt(variance + epsilon)
    normed = centered * inv_std
    summed = bn_gain * normed + bn_shift + block_input.astype(jnp.float32)
    grad_pre = jnp.where(summed > 0.0, out_grad.astype(jnp.float32), jnp.zeros_like(summed))
    sum_grad, sum_cross = lax.psum(
        (jnp.sum(grad_pre, axis=0), jnp.sum(grad_pre * normed, axis=0)), "bn"
    )
    grad_conv = (
        bn_gain * inv_std * (grad_pre - sum_grad / group_rows - normed * (sum_cross / group_rows))
    ).astype(jnp.bfloat16)
    gain_grad, shift_grad = lax.psum((sum_cross, sum_grad), "rep")
    act_wide = lax.dot_general(
        grad_conv, full_weight, (((1,), (1,)), ((), ())), preferred_element_type=jnp.float32
    )
    act_grad = act_wide.astype(jnp.bfloat16)
    group_grad = lax.psum_scatter(
        lax.dot_general(
            activations, grad_conv, (((0,), (0,)), ((), ())), preferred_element_type=jnp.float32
        ),
        "bn",
        scatter_dimension=0,
        tiled=True,
    )
    weight_grad = lax.psum(group_grad.astype(jnp.bfloat16), "rep").astype(jnp.float32)
    weight_f = conv_weight.astype(jnp.float32)
    weight_sq, grad_sq = lax.psum(
        (jnp.sum(weight_f * weight_f), jnp.sum(weight_grad * weight_grad)), "bn"
    )
    weight_norm = jnp.sqrt(weight_sq)
    grad_norm = jnp.sqrt(grad_sq)
    ratio = weight_norm / (grad_norm + weight_decay * weight_norm)
    new_velocity = momentum * velocity + ratio * (weight_grad + weight_decay * weight_f)
    return (act_grad, gain_grad, shift_grad, new_velocity)


def solution(mesh):
    return jax.shard_map(
        local,
        mesh=mesh,
        in_specs=(
            P(("rep", "bn"), None),
            P(("rep", "bn"), None),
            P("bn", None),
            P(),
            P(),
            P(("rep", "bn"), None),
            P("bn", None),
        ),
        out_specs=(P(("rep", "bn"), None), P(), P(), P("bn", None)),
        check_vma=False,
    )
```

profile of v0, /device:TPU:1, one launch (start us, length us, event | category | flops | bytes accessed | tf_op | source)
XLA Modules:
  0.0 580.2 jit_solution(10221857778204602345)
XLA Ops:
  7.2 0.0 copy-start
  7.2 0.0 all-gather.2.cloned.1.call-start
  7.2 0.7 all-gather.2.cloned.1.call-update
  7.9 0.0 reduce-scatter.4.cloned.1.call-start
  8.0 50.0 %all-gather.2.cloned.1.call-done = bf16[512,2048]{1,0:T(8,128)(2,1)} async-done(((bf16[32,2048]{1,0:T(8,128)(2,1)}), bf16[512,2048]{1,0:T(8,128)(2,1)}) %all-gather.2.cloned.1.call-update) | async-done | bytes 2097168 | tf_op jit(solution)/shard_map/all_gather | solution.py:14
  58.0 0.0 copy-done
  58.0 4.3 fusion.6
  62.2 23.7 %psum.63 = f32[2048]{0:T(1024)S(1)} all-reduce(f32[2048]{0:T(1024)S(1)} %get-tuple-element.23), channel_id=1, replica_groups=mesh['rep'=32,'bn'=16] {'bn'}, use_global_device_ids=true, to_apply=%region_1.0 | all-reduce | flops 2048 | bytes 16384 | tf_op jit(solution)/shard_map/psum | solution.py:16
  86.0 2.3 multiply_reduce_fusion.1
  88.3 25.8 %psum.64 = f32[2048]{0:T(1024)S(1)} all-reduce(f32[2048]{0:T(1024)S(1)} %multiply_reduce_fusion.1), channel_id=1, replica_groups=mesh['rep'=32,'bn'=16] {'bn'}, use_global_device_ids=true, to_apply=%region_3.0 | all-reduce | flops 2048 | bytes 16384 | tf_op jit(solution)/shard_map/psum | solution.py:19
  114.1 0.0 copy-done.4
  114.1 4.1 fusion
  118.2 42.9 %all-reduce.2 = (f32[2048]{0:T(1024)S(1)}, f32[2048]{0:T(1024)S(1)}) all-reduce(f32[2048]{0:T(1024)S(1)} %get-tuple-element.13, f32[2048]{0:T(1024)S(1)} %get-tuple-element.12), channel_id=1, replica_groups=mesh['rep'=32,'bn'=16] {'bn'}, use_global_device_ids=true, to_apply=%region_7.8 | all-reduce | flops 4096 | bytes 32768 | tf_op jit(solution)/shard_map/psum | solution.py:24
  161.0 3.6 multiply_convert_fusion
  164.6 3.3 convolution_bitcast_fusion
  167.9 5.4 copy.17
  173.3 0.0 reduce-scatter.4.cloned.1.call-update
  173.3 0.0 all-reduce.5.cloned.1.call-start
  173.4 0.8 copy-done.2
  174.2 0.3 copy.15
  174.5 1.3 copy.14
  175.8 0.9 fusion.1
  176.7 62.5 %reduce-scatter.4.cloned.1.call-done = f32[32,2048]{1,0:T(8,128)} async-done(((f32[512,2048]{1,0:T(8,128)}), f32[32,2048]{1,0:T(8,128)}) %reduce-scatter.4.cloned.1.call-update) | async-done | bytes 262160
  239.2 2.0 copy.18
  241.1 0.0 all-reduce.5.cloned.1.call-update
  241.2 3.4 convolution_convert_fusion
  244.6 153.8 %all-reduce.5.cloned.1.call-done = bf16[32,2048]{0,1:T(8,128)(2,1)} async-done(((bf16[32,2048]{0,1:T(8,128)(2,1)}), bf16[32,2048]{0,1:T(8,128)(2,1)}) %all-reduce.5.cloned.1.call-update) | async-done | bytes 131088 | tf_op jit(solution)/shard_map/psum | solution.py:43
  398.4 2.0 fusion.2
  400.4 112.7 %all-reduce = (f32[2048]{0:T(1024)}, f32[2048]{0:T(1024)}) all-reduce(f32[2048]{0:T(1024)S(1)} %get-tuple-element.18, f32[2048]{0:T(1024)S(1)} %get-tuple-element.19), channel_id=1, replica_groups=mesh['rep'=32,'bn'=16] {'rep'}, use_global_device_ids=true, to_apply=%region_8.9 | all-reduce | flops 4096 | bytes 32768 | tf_op jit(solution)/shard_map/psum | solution.py:30
  513.1 56.5 %all-reduce.1 = (f32[]{:T(128)}, f32[]{:T(128)}) all-reduce(f32[]{:T(128)} %fusion.1, f32[]{:T(128)} %fusion.2), channel_id=1, replica_groups=mesh['rep'=32,'bn'=16] {'bn'}, use_global_device_ids=true, to_apply=%region_11.12 | all-reduce | flops 2 | bytes 16 | tf_op jit(solution)/shard_map/psum | solution.py:45
  571.1 1.6 fusion.4
  572.7 1.0 copy.16
  (11 shorter events, 0.0 us)
Async XLA Ops:
  7.2 50.8 %copy-start = (bf16[392,512]{1,0:T(8,128)(2,1)S(1)}, bf16[392,512]{1,0:T(8,128)(2,1)}, u32[]{:S(2)}) copy-start(bf16[392,512]{1,0:T(8,128)(2,1)} %param.8) | copy-start | bytes 1204228
  7.2 50.8 %all-gather.2.cloned.1.call-start = ((), (), s32[]{:S(2)}) async-start(), calls=%async_computation.1 | async-start | bytes 2228224 | tf_op jit(solution)/shard_map/all_gather | solution.py:14
  7.9 231.3 %reduce-scatter.4.cloned.1.call-start = ((), (), s32[]{:S(2)}) async-start(), calls=%async_computation.3 | async-start | bytes 4456448
  62.2 51.8 %copy-start.4 = (f32[2048]{0:T(1024)S(1)}, f32[2048]{0:T(1024)}, u32[]{:S(2)}) copy-start(f32[2048]{0:T(1024)} %param.10) | copy-start | bytes 24580
  62.2 51.8 %copy-start.1 = (bf16[392,2048]{1,0:T(8,128)(2,1)S(1)}, bf16[392,2048]{1,0:T(8,128)(2,1)}, u32[]{:S(2)}) copy-start(bf16[392,2048]{1,0:T(8,128)(2,1)} %param.12) | copy-start | bytes 4816900
  62.2 51.8 %copy-start.5 = (f32[2048]{0:T(1024)S(1)}, f32[2048]{0:T(1024)}, u32[]{:S(2)}) copy-start(f32[2048]{0:T(1024)} %param.11) | copy-start | bytes 24580
  173.3 0.9 copy-start.2
  173.3 1.2 copy-start.3
  173.3 225.1 %all-reduce.5.cloned.1.call-start = ((), (), s32[]{:S(2)}) async-start(), calls=%async_computation.2 | async-start | bytes 1048576 | tf_op jit(solution)/shard_map/psum | solution.py:43
Sparse Core Ops, SparseCore 0:
  10.1 47.7 all-gather.1
  173.4 65.7 reduce-scatter.3
  242.6 155.7 all-reduce.4
where the time goes:
time: 581 us; the launch traced here: 580 us
  waiting for transfers between devices  267 us (46%)
  blocking collectives  262 us (45%)
  between operations  15.3 us (3%)
  other arithmetic  14.4 us (2%)
  matrix products  11 us (2%)
  local copies, waits for them, and re-layouts  10.8 us (2%)
    psum x1, waiting for transfers between devices, local(): lax.psum(group_grad.astype(jnp.bfloat16), 'rep').astype(jnp.float32)  154 us
    psum x1, blocking collectives, local(): gain_grad, shift_grad = lax.psum((sum_cross, sum_grad), 'rep')  113 us
    unnamed x4, waiting for transfers between devices  63.2 us
    psum x1, blocking collectives, local(): lax.psum((jnp.sum(weight_f * weight_f), jnp.sum(weight_grad * weight_grad...  56.5 us
    all_gather x1, waiting for transfers between devices, local(): full_weight = lax.all_gather(conv_weight, 'bn', axis=0, tiled=True)  50 us
    psum x1, blocking collectives, local(): lax.psum((jnp.sum(grad_pre, axis=0), jnp.sum(grad_pre * normed, axis=0)),...  42.9 us
    psum x1, blocking collectives, local(): variance = lax.psum(jnp.sum(centered * centered, axis=0), 'bn') / group_rows  25.8 us
    psum x1, blocking collectives, local(): chan_total = lax.psum(jnp.sum(conv_out, axis=0), 'bn')  23.7 us
  transfers between devices with their start and end apart: 3, of which 3 were waited for; matrix products, arithmetic and copies ran while one was open for 1% of the time, Pallas kernels for 0%

commit v1 on v0

v1 whole, which is shorter than its diff:
```python
import jax
import jax.numpy as jnp
from jax import lax
from jax.sharding import Mesh, PartitionSpec as P

epsilon = 1e-05
weight_decay = 5e-05
momentum = 0.9
f32, bf16 = jnp.float32, jnp.bfloat16
rep = ("z", "x")
bn = ("y", "c")


def swap(value):
    return lax.ppermute(value, "c", [(0, 1), (1, 0)])


def exchange(pieces, axis):
    return lax.all_to_all(pieces, axis, 0, 0, tiled=True)


def copies(value, axis):
    n = lax.axis_size(axis)
    return exchange(jnp.broadcast_to(value[None], (n, *value.shape)), axis)


def split(value):
    high = value.astype(bf16)
    return high, (value - high.astype(f32)).astype(bf16)


def local(block_input, activations, conv_weight, bn_gain, bn_shift, out_grad, velocity):
    rows, cin = activations.shape
    part, cout = conv_weight.shape
    nz, nx, ny = lax.axis_size("z"), lax.axis_size("x"), lax.axis_size("y")
    core = lax.axis_index("c")
    group_rows = rows * lax.axis_size(bn)
    lanes = 128

    own = copies(conv_weight, "y")
    other = swap(own)
    first = jnp.where(core == 0, own, other)
    second = jnp.where(core == 0, other, own)
    full_weight = jnp.stack([first, second], axis=1).reshape(cin, cout)

    conv_out = jnp.dot(activations, full_weight, preferred_element_type=f32)
    local_mean = jnp.sum(conv_out, axis=0) / rows
    spread = conv_out - local_mean
    local_square = jnp.sum(spread * spread, axis=0)
    moments = jnp.stack([local_mean, local_square]).reshape(-1, lanes)
    moments = copies(moments, bn).reshape(-1, 2, cout)
    chan_mean = jnp.mean(moments[:, 0], axis=0)
    offset = moments[:, 0] - chan_mean
    variance = (jnp.sum(moments[:, 1], axis=0) + rows * jnp.sum(offset * offset, axis=0)) / group_rows
    inv_std = lax.rsqrt(variance + epsilon)

    normed = (conv_out - chan_mean) * inv_std
    summed = bn_gain * normed + bn_shift + block_input.astype(f32)
    grad_pre = jnp.where(summed > 0.0, out_grad.astype(f32), jnp.zeros_like(summed))
    stats = jnp.stack([jnp.sum(grad_pre, axis=0), jnp.sum(grad_pre * normed, axis=0)])
    stats = jnp.sum(copies(stats.reshape(-1, lanes), bn), axis=0).reshape(2, cout)
    sum_grad, sum_cross = stats[0], stats[1]
    grad_conv = (
        bn_gain * inv_std * (grad_pre - sum_grad / group_rows - normed * (sum_cross / group_rows))
    ).astype(bf16)

    partial = lax.dot_general(
        activations, grad_conv, (((0,), (0,)), ((), ())), preferred_element_type=f32
    ).astype(bf16)
    partial = partial.reshape(ny, 2, part, cout)
    mine = jnp.where(core == 0, partial[:, 0], partial[:, 1])
    theirs = jnp.where(core == 0, partial[:, 1], partial[:, 0])
    pair = (mine.astype(f32) + swap(theirs).astype(f32)).astype(bf16)
    pair = pair.reshape(ny, nx, part // nx, nz, cout // nz).transpose(3, 1, 0, 2, 4)
    pair = pair.reshape(nz * nx, cin // 2 // nx, cout // nz)
    grad_high, grad_low = split(sum_grad)
    cross_high, cross_low = split(sum_cross)
    tail = jnp.stack([grad_high, grad_low, cross_high, cross_low])
    tail = tail.reshape(nx, nz, 1, cout // nz).transpose(1, 0, 2, 3).reshape(nz * nx, 1, cout // nz)
    tail = jnp.pad(tail, ((0, 0), (0, 7), (0, 0)))
    summed_rep = jnp.sum(exchange(jnp.concatenate([pair, tail], axis=1), rep).astype(f32), axis=0)
    act_grad = lax.dot_general(
        grad_conv, full_weight, (((1,), (1,)), ((), ())), preferred_element_type=f32
    ).astype(bf16)
    block = summed_rep[: cin // 2 // nx].reshape(ny, part // nx, cout // nz)
    piece = jnp.sum(exchange(block, "y"), axis=0)
    tail_high, tail_low = split(summed_rep[cin // 2 // nx])
    low_rows = jnp.pad(jnp.stack([tail_high, tail_low]), ((0, 6), (0, 0)))
    whole = copies(jnp.concatenate([piece.astype(bf16), low_rows]), rep).astype(f32)
    whole = whole.reshape(nz, nx, -1, cout // nz)
    weight_grad = whole[:, :, : part // nx].transpose(1, 2, 0, 3).reshape(part, cout)
    totals = jnp.sum(whole[:, :, part // nx : part // nx + 2], axis=2)
    totals = totals.transpose(1, 0, 2).reshape(nx, cout)
    shift_grad = totals[0] + totals[1]
    gain_grad = totals[2] + totals[3]

    weight_f = conv_weight.astype(f32)
    full_f = full_weight.astype(f32)
    weight_norm = jnp.sqrt(jnp.sum(full_f * full_f))
    square = jnp.sum(weight_grad * weight_grad)
    squares = copies(jnp.broadcast_to(square, (8, lanes)), bn).reshape(-1, 8, lanes)
    grad_norm = jnp.sqrt(jnp.sum(squares[:, 0, 0]))
    ratio = weight_norm / (grad_norm + weight_decay * weight_norm)
    new_velocity = momentum * velocity + ratio * (weight_grad + weight_decay * weight_f)
    return (act_grad, gain_grad, shift_grad, new_velocity)


def solution(mesh, shape=(8, 4, 8, 2)):
    fine = Mesh(mesh.devices.reshape(shape), ("z", "x", "y", "c"))
    every = P(("z", "x", "y", "c"), None)
    return jax.shard_map(
        local,
        mesh=fine,
        in_specs=(every, every, P(bn, None), P(), P(), every, P(bn, None)),
        out_specs=(every, P(), P(), P(bn, None)),
        check_vma=False,
    )
```

time: 581 us -> 206 us (0.35)
  waiting for transfers between devices: 267 us -> 19.7 us
  blocking collectives: 262 us -> 108 us
  starting transfers between devices: 0.12 us -> 23.4 us
  other arithmetic: 14.4 us -> 28.7 us
  between operations: 15.3 us -> 2.34 us
    psum x5 -> x0, blocking collectives: 262 us -> none  [the longest x1 113 us: local(): gain_grad, shift_grad = lax.psum((sum_cross, sum_grad), 'rep')]
    psum x1 -> x0, waiting for transfers between devices: 154 us -> none  [local(): lax.psum(group_grad.astype(jnp.bfloat16), 'rep').astype(jnp.float32)]
    all_to_all x0 -> x4, blocking collectives: none -> 108 us  [exchange(): return lax.all_to_all(pieces, axis, 0, 0, tiled=True)]
    unnamed x4 -> x0, waiting for transfers between devices: 63.2 us -> none
    all_gather x1 -> x0, waiting for transfers between devices: 50 us -> none  [local(): full_weight = lax.all_gather(conv_weight, 'bn', axis=0, tiled=True)]
    all_to_all x0 -> x3, waiting for transfers between devices: none -> 16.5 us  [exchange(): return lax.all_to_all(pieces, axis, 0, 0, tiled=True)]
    all_to_all x0 -> x3, starting transfers between devices: none -> 15.9 us  [exchange(): return lax.all_to_all(pieces, axis, 0, 0, tiled=True)]
    ppermute x0 -> x2, starting transfers between devices: none -> 7.53 us  [swap(): return lax.ppermute(value, 'c', [(0, 1), (1, 0)])]
  transfers between devices with their start and end apart: 3 -> 5, of which waited for: 3 -> 5; matrix products, arithmetic and copies ran while one was open for 1% -> 5% of each run, Pallas kernels for 0% -> 0%
where the time goes in v1:
time: 206 us; the launch traced here: 204 us
  blocking collectives  108 us (52%)
  other arithmetic  28.7 us (14%)
  starting transfers between devices  23.4 us (11%)
  waiting for transfers between devices  19.7 us (10%)
  local copies, waits for them, and re-layouts  16.5 us (8%)
  matrix products  5.6 us (3%)
  between operations  2.34 us (1%)
    all_to_all x4, blocking collectives, exchange(): return lax.all_to_all(pieces, axis, 0, 0, tiled=True)  108 us
    all_to_all x3, waiting for transfers between devices, exchange(): return lax.all_to_all(pieces, axis, 0, 0, tiled=True)  16.5 us
    all_to_all x3, starting transfers between devices, exchange(): return lax.all_to_all(pieces, axis, 0, 0, tiled=True)  15.9 us
    ppermute x2, starting transfers between devices, swap(): return lax.ppermute(value, 'c', [(0, 1), (1, 0)])  7.53 us
    broadcast_in_dim x6, local copies, waits for them, and re-layouts, copies(): return exchange(jnp.broadcast_to(value[None], (n, *value.shape)), axis)  5.93 us
    reduce_sum x1, other arithmetic, local(): jnp.sum(grad_pre, axis=0)  5.35 us
    unnamed x21, local copies, waits for them, and re-layouts  4.49 us
  transfers between devices with their start and end apart: 5, of which 5 were waited for; matrix products, arithmetic and copies ran while one was open for 5% of the time, Pallas kernels for 0%

profile of v1, /device:TPU:1, one launch (start us, length us, event | category | flops | bytes accessed | tf_op | source)
XLA Modules:
  0.0 204.4 jit_solution(17557888060483088742)
XLA Ops:
  0.6 1.1 broadcast_in_dim.12
  1.7 33.4 %all_to_all.35 = bf16[8,32,2048]{2,1,0:T(8,128)(2,1)S(1)} all-to-all(bf16[8,32,2048]{2,1,0:T(8,128)(2,1)S(1)} %broadcast_in_dim.12), channel_id=1, replica_groups=mesh['z'=8,'x'=4,'y'=8,'c'=2] {'y'}, dimensions={0} | all-to-all | bytes 2097152 | tf_op jit(solution)/shard_map/all_to_all | solution.py:19
  35.1 5.6 %collective-permute-start = (bf16[8,32,2048]{2,1,0:T(8,128)(2,1)S(1)}, bf16[8,32,2048]{2,1,0:T(8,128)(2,1)S(1)}, u32[]{:S(2)}, u32[]{:S(2)}) collective-permute-start(bf16[8,32,2048]{2,1,0:T(8,128)(2,1)S(1)} %all_to_all.35), channel_id=1, source_target_pairs={{0,1},{1,0},{2,3},{3,2},{4,5},{5,4},{6,7},{7,6},{8,9},{9,8},{10,11... | collective-permute-start | bytes 3145736 | tf_op jit(solution)/shard_map/ppermute | solution.py:15
  40.8 2.3 %collective-permute-done = bf16[8,32,2048]{2,1,0:T(8,128)(2,1)S(1)} collective-permute-done((bf16[8,32,2048]{2,1,0:T(8,128)(2,1)S(1)}, bf16[8,32,2048]{2,1,0:T(8,128)(2,1)S(1)}, u32[]{:S(2)}, u32[]{:S(2)}) %collective-permute-start) | collective-permute-done | bytes 1048608 | tf_op jit(solution)/shard_map/ppermute | solution.py:15
  44.1 1.0 fusion.19
  45.2 1.6 copy-done.1
  47.8 1.3 broadcast_in_dim.13
  49.9 15.3 %all_to_all.36 = f32[16,32,128]{2,1,0:T(8,128)} all-to-all(f32[16,32,128]{2,1,0:T(8,128)S(1)} %broadcast_in_dim.14), channel_id=1, replica_groups=mesh['z'=8,'x'=4,'y'=8,'c'=2] {'y','c'}, dimensions={0} | all-to-all | bytes 524288 | tf_op jit(solution)/shard_map/all_to_all | solution.py:19
  65.2 1.8 reshape.170
  67.0 1.3 slice_reduce_fusion.3
  68.4 1.3 fusion.16
  69.7 5.3 %fusion.7 = (f32[2048]{0:T(1024)S(1)}, f32[2048]{0:T(1024)S(1)}, pred[392,2048]{1,0:T(8,128)(4,1)}) fusion(bf16[392,2048]{1,0:T(8,128)(2,1)} %param.12, f32[2048]{0:T(1024)S(1)} %get-tuple-element.9, f32[2048,392]{0,1:T(8,128)} %copy-done.1, f32[2048]{0:T(1024)S(1)} %broadcast_multiply_fusion, bf16[392,2048]{1,0:T(8,128)(2,1)} %param.7, f32[2048]{0:T(1024)} %param.11, ...), kind=kLoop, calls=%fused_computation.12 | loop fusion | flops 9629696 | bytes 7274496 | tf_op jit(solution)/shard_map/reduce_sum | solution.py:60
  75.7 1.3 broadcast_in_dim.15
  77.8 14.3 %all_to_all.37 = f32[16,32,128]{2,1,0:T(8,128)} all-to-all(f32[16,32,128]{2,1,0:T(8,128)S(1)} %broadcast_in_dim.16), channel_id=1, replica_groups=mesh['z'=8,'x'=4,'y'=8,'c'=2] {'y','c'}, dimensions={0} | all-to-all | bytes 524288 | tf_op jit(solution)/shard_map/all_to_all | solution.py:19
  92.1 1.6 reduce_sum.133
  94.4 3.8 %fusion.6 = bf16[392,2048]{1,0:T(8,128)(2,1)S(1)} fusion(pred[392,2048]{1,0:T(8,128)(4,1)} %get-tuple-element.10, bf16[392,2048]{1,0:T(8,128)(2,1)} %param.12, f32[2048,392]{0,1:T(8,128)} %copy-done.1, f32[2048]{0:T(1024)S(1)} %get-tuple-element.18, f32[2048]{0:T(1024)S(1)} %get-tuple-element.17, f32[2048]{0:T(1024)} %copy-done.9, ...), kind=kLoop, calls=%fused_computation.10 | loop fusion | flops 7225344 | bytes 7266304 | tf_op jit(solution)/shard_map/convert_element_type | solution.py:65
  98.2 1.3 convolution_convert_fusion
  99.5 1.3 copy-done.3
  100.9 1.1 select_bitcast_fusion
  102.0 1.9 collective-permute-start.1
  104.6 1.3 reshape.182
  106.8 2.4 %fusion.9 = bf16[8,32,2048]{2,1,0:T(8,128)(2,1)S(1)} fusion(bf16[8,32,2048]{2,1,0:T(8,128)(2,1)} %collective-permute-done.1, pred[]{:T(512)S(6)} %eq.2, bf16[8,2,32,2048]{3,2,1,0:T(8,128)(2,1)} %bitcast.103), kind=kLoop, calls=%fused_computation.21 | loop fusion | flops 2621440 | bytes 4194305 | tf_op jit(solution)/shard_map/convert_element_type | solution.py:73
  109.5 45.1 %all_to_all.38 = bf16[32,72,256]{2,1,0:T(8,128)(2,1)S(1)} all-to-all(bf16[32,72,256]{2,1,0:T(8,128)(2,1)S(1)} %fusion.10), channel_id=1, replica_groups=mesh['z'=8,'x'=4,'y'=8,'c'=2] {'z','x'}, dimensions={0} | all-to-all | bytes 2359296 | tf_op jit(solution)/shard_map/all_to_all | solution.py:19
  156.0 4.0 %all-to-all-start.4 = ((f32[8,8,256]{2,1,0:T(8,128)}), f32[8,8,256]{2,1,0:T(8,128)}, u32[]{:S(2)}, u32[]{:S(2)}) async-start(f32[8,8,256]{2,1,0:T(8,128)} %slice_bitcast_fusion.3), calls=%async_computation.4 | async-start | bytes 131072 | tf_op jit(solution)/shard_map/all_to_all | solution.py:19
  161.4 5.8 %all-to-all-done.4 = f32[8,8,256]{2,1,0:T(8,128)} async-done(((f32[8,8,256]{2,1,0:T(8,128)}), f32[8,8,256]{2,1,0:T(8,128)}, u32[]{:S(2)}, u32[]{:S(2)}) %all-to-all-start.4) | async-done | bytes 65568 | tf_op jit(solution)/shard_map/all_to_all | solution.py:19
  168.8 4.8 %all-to-all-start.5 = ((bf16[32,16,256]{2,1,0:T(8,128)(2,1)}), bf16[32,16,256]{2,1,0:T(8,128)(2,1)}, u32[]{:S(2)}, u32[]{:S(2)}) async-start(bf16[32,16,256]{2,1,0:T(8,128)(2,1)} %broadcast_in_dim.17), calls=%async_computation.5 | async-start | bytes 524288 | tf_op jit(solution)/shard_map/all_to_all | solution.py:19
  173.6 2.9 %multiply_reduce_fusion = f32[]{:T(128)} fusion(bf16[8,1,32,2048]{3,2,1,0:T(8,128)(2,1)} %copy-done.2, bf16[8,1,32,2048]{3,2,1,0:T(8,128)(2,1)S(1)} %get-tuple-element.11), kind=kLoop, calls=%fused_computation | loop fusion | flops 4194303 | bytes 2097156 | tf_op jit(solution)/shard_map/reduce_sum | solution.py:99
  177.2 3.3 %convolution_convert_fusion.1 = bf16[392,512]{1,0:T(8,128)(2,1)} fusion(bf16[392,2048]{1,0:T(8,128)(2,1)} %copy-done.4, bf16[512,2048]{1,0:T(8,128)(2,1)S(1)} %bitcast.101), kind=kOutput, calls=%fused_computation.22 | convolution fusion | flops 822284288 | bytes 4104192 | tf_op jit(solution)/shard_map/dot_general | solution.py:82
  180.5 3.5 %all-to-all-done.5 = bf16[32,16,256]{2,1,0:T(8,128)(2,1)} async-done(((bf16[32,16,256]{2,1,0:T(8,128)(2,1)}), bf16[32,16,256]{2,1,0:T(8,128)(2,1)}, u32[]{:S(2)}, u32[]{:S(2)}) %all-to-all-start.5) | async-done | bytes 262176 | tf_op jit(solution)/shard_map/all_to_all | solution.py:19
  186.0 1.3 broadcast_in_dim_broadcast_in_dim_broadcast_in_dim.3
  187.3 7.1 %all-to-all-start.6 = ((f32[16,8,128]{2,1,0:T(8,128)}), f32[16,8,128]{2,1,0:T(8,128)S(1)}, u32[]{:S(2)}, u32[]{:S(2)}) async-start(f32[16,8,128]{2,1,0:T(8,128)} %broadcast_in_dim_broadcast_in_dim_broadcast_in_dim.3), calls=%async_computation.6 | async-start | bytes 131072 | tf_op jit(solution)/shard_map/all_to_all | solution.py:19
  195.0 7.2 %all-to-all-done.6 = f32[16,8,128]{2,1,0:T(8,128)S(1)} async-done(((f32[16,8,128]{2,1,0:T(8,128)}), f32[16,8,128]{2,1,0:T(8,128)S(1)}, u32[]{:S(2)}, u32[]{:S(2)}) %all-to-all-start.6) | async-done | bytes 65568 | tf_op jit(solution)/shard_map/all_to_all | solution.py:19
  (53 shorter events, 15.3 us)
Async XLA Ops:
  0.6 43.5 %copy-start = (bf16[392,512]{1,0:T(8,128)(2,1)S(1)}, bf16[392,512]{1,0:T(8,128)(2,1)}, u32[]{:S(2)}) copy-start(bf16[392,512]{1,0:T(8,128)(2,1)} %param.8) | copy-start | bytes 1204228
  35.1 7.9 %collective-permute-start = (bf16[8,32,2048]{2,1,0:T(8,128)(2,1)S(1)}, bf16[8,32,2048]{2,1,0:T(8,128)(2,1)S(1)}, u32[]{:S(2)}, u32[]{:S(2)}) collective-permute-start(bf16[8,32,2048]{2,1,0:T(8,128)(2,1)S(1)} %all_to_all.35), channel_id=1, source_target_pairs={{0,1},{1,0},{2,3},{3,2},{4,5},{5,4},{6,7},{7,6},{8,9},{9,8},{10,11... | collective-permute-start | bytes 3145736 | tf_op jit(solution)/shard_map/ppermute | solution.py:15
  43.2 1.0 copy-start.2
  45.2 1.7 copy-start.1
  69.7 5.3 %copy-start.9 = (f32[2048]{0:T(1024)}, f32[2048]{0:T(1024)S(1)}, u32[]{:S(2)}) copy-start(f32[2048]{0:T(1024)S(1)} %get-tuple-element.9) | copy-start | bytes 24580
  98.2 1.3 copy-start.4
  99.5 1.4 copy-start.3
  102.0 4.9 %collective-permute-start.1 = (bf16[8,32,2048]{2,1,0:T(8,128)(2,1)}, bf16[8,32,2048]{2,1,0:T(8,128)(2,1)}, u32[]{:S(2)}, u32[]{:S(2)}) collective-permute-start(bf16[8,32,2048]{2,1,0:T(8,128)(2,1)} %select_bitcast_fusion), channel_id=1, source_target_pairs={{0,1},{1,0},{2,3},{3,2},{4,5},{5,4},{6,7},{7,6},{8,9},{9,8},{10,11... | collective-permute-start | bytes 3145736 | tf_op jit(solution)/shard_map/ppermute | solution.py:15
  105.9 3.4 %copy-start.8 = (bf16[32,1,256]{2,1,0:T(2,128)(2,1)S(1)}, bf16[32,1,256]{2,1,0:T(2,128)(2,1)}, u32[]{:S(2)}) copy-start(bf16[32,1,256]{2,1,0:T(2,128)(2,1)} %reshape.182) | copy-start | bytes 49156
  154.7 0.6 copy-start.6
  156.0 11.2 %all-to-all-start.4 = ((f32[8,8,256]{2,1,0:T(8,128)}), f32[8,8,256]{2,1,0:T(8,128)}, u32[]{:S(2)}, u32[]{:S(2)}) async-start(f32[8,8,256]{2,1,0:T(8,128)} %slice_bitcast_fusion.3), calls=%async_computation.4 | async-start | bytes 131072 | tf_op jit(solution)/shard_map/all_to_all | solution.py:19
  168.8 15.2 %all-to-all-start.5 = ((bf16[32,16,256]{2,1,0:T(8,128)(2,1)}), bf16[32,16,256]{2,1,0:T(8,128)(2,1)}, u32[]{:S(2)}, u32[]{:S(2)}) async-start(bf16[32,16,256]{2,1,0:T(8,128)(2,1)} %broadcast_in_dim.17), calls=%async_computation.5 | async-start | bytes 524288 | tf_op jit(solution)/shard_map/all_to_all | solution.py:19
  180.5 23.1 %copy-start.5 = (bf16[32,2048]{1,0:T(8,128)(2,1)S(1)}, bf16[32,2048]{1,0:T(8,128)(2,1)}, u32[]{:S(2)}) copy-start(bf16[32,2048]{1,0:T(8,128)(2,1)} %param.9) | copy-start | bytes 393220
  180.5 23.1 %copy-start.7 = (f32[32,2048]{1,0:T(8,128)S(1)}, f32[32,2048]{1,0:T(8,128)}, u32[]{:S(2)}) copy-start(f32[32,2048]{1,0:T(8,128)} %param.13) | copy-start | bytes 786436
  187.3 15.0 %all-to-all-start.6 = ((f32[16,8,128]{2,1,0:T(8,128)}), f32[16,8,128]{2,1,0:T(8,128)S(1)}, u32[]{:S(2)}, u32[]{:S(2)}) async-start(f32[16,8,128]{2,1,0:T(8,128)} %broadcast_in_dim_broadcast_in_dim_broadcast_in_dim.3), calls=%async_computation.6 | async-start | bytes 131072 | tf_op jit(solution)/shard_map/all_to_all | solution.py:19

commit v2 on v1

v2 whole, which is shorter than its diff:
```python
import jax
import jax.numpy as jnp
from jax import lax
from jax.experimental import pallas as pl
from jax.experimental.pallas import tpu as pltpu
from jax.sharding import Mesh, PartitionSpec as P

epsilon = 1e-05
weight_decay = 5e-05
momentum = 0.9
f32, bf16 = jnp.float32, jnp.bfloat16
rep = ("z", "x")
bn = ("y", "c")
lanes = 128
chunk = 512
groups = chunk // lanes


def swap(value):
    return lax.ppermute(value, "c", [(0, 1), (1, 0)])


def exchange(pieces, axis):
    return lax.all_to_all(pieces, axis, 0, 0, tiled=True)


def copies(value, axis):
    n = lax.axis_size(axis)
    return exchange(jnp.broadcast_to(value[None], (n, *value.shape)), axis)


def fold(row):
    return [row[:, q * lanes : (q + 1) * lanes] for q in range(groups)]


def unfold(tile):
    return jnp.concatenate([tile[q : q + 1] for q in range(groups)], axis=1)


def high_low(value):
    high = value.astype(bf16).astype(f32)
    return high, value - high


def moments_kernel(acts, own, other, weight, conv, moments):
    core = lax.axis_index("c")
    count, part, _ = own.shape
    for y in range(count):
        at = pl.multiple_of((2 * y + core) * part, part)
        weight[pl.ds(at, part), :] = own[y]
        at = pl.multiple_of((2 * y + 1 - core) * part, part)
        weight[pl.ds(at, part), :] = other[y]
    out = jnp.dot(acts[...], weight[...], preferred_element_type=f32)
    conv[...] = out
    mean = jnp.sum(out, axis=0, keepdims=True) / out.shape[0]
    spread = out - mean
    square = jnp.sum(spread * spread, axis=0, keepdims=True)
    tile = jnp.concatenate(fold(mean) + fold(square), axis=0)
    moments[...] = jnp.broadcast_to(tile[None], moments.shape)


def pooled(moments, rows):
    members = moments.shape[0]
    means, squares = moments[:, :groups], moments[:, groups:]
    mean = jnp.sum(means, axis=0) / members
    offset = means - mean[None]
    square = jnp.sum(squares, axis=0) + rows * jnp.sum(offset * offset, axis=0)
    inv_std = lax.rsqrt(square / (rows * members) + epsilon)
    return unfold(mean), unfold(inv_std)


def stats_kernel(conv, moments, gain, shift, block_input, out_grad, grad, stats):
    mean, inv_std = pooled(moments[...], conv.shape[0])
    centered = conv[...] - mean
    summed = centered * (gain[...] * inv_std) + shift[...] + block_input[...].astype(f32)
    value = jnp.where(summed > 0.0, out_grad[...].astype(f32), 0.0)
    grad[...] = value.astype(bf16)
    sum_grad = jnp.sum(value, axis=0, keepdims=True)
    sum_cross = jnp.sum(value * centered, axis=0, keepdims=True) * inv_std
    tile = jnp.concatenate(fold(sum_grad) + fold(sum_cross), axis=0)
    stats[...] = jnp.broadcast_to(tile[None], stats.shape)


def weight_kernel(conv, moments, stats, gain, grad, acts_t, grad_conv, mine, theirs, tail, wide):
    core = lax.axis_index("c")
    rows = conv.shape[0]
    group_rows = rows * moments.shape[0]
    mean, inv_std = pooled(moments[...], rows)
    sums = jnp.sum(stats[...], axis=0)
    sum_grad, sum_cross = sums[:groups], sums[groups:]
    shift = unfold(sum_grad) / group_rows
    slope = inv_std * unfold(sum_cross) / group_rows
    value = grad[...].astype(f32) - shift - (conv[...] - mean) * slope
    narrow = (gain[...] * inv_std * value).astype(bf16)
    grad_conv[...] = narrow
    wide[...] = jnp.dot(acts_t[...], narrow, preferred_element_type=f32)
    nz, nx, length, _ = mine.shape
    part = 8 * nx
    ny = wide.shape[0] // (2 * part)
    halves = chunk // nz // lanes
    for z in range(nz):
        for x in range(nx):
            for out, owner in ((mine, core), (theirs, 1 - core)):
                rows_of = [
                    wide[
                        pl.ds(pl.multiple_of((2 * y + owner) * part + 8 * x, 8), 8),
                        pl.ds((z * halves + h) * lanes, lanes),
                    ]
                    for h in range(halves)
                    for y in range(ny)
                ]
                out[z, x] = jnp.concatenate(rows_of, axis=0).astype(bf16)
    planes = (*high_low(sum_grad), *high_low(sum_cross))
    for z in range(nz):
        for x in range(nx):
            rows_of = planes[x][z * halves : (z + 1) * halves]
            tail[z, x] = jnp.concatenate([rows_of, jnp.zeros((8 - halves, lanes), f32)], axis=0)


def act_kernel(grad_conv, weight, act_grad, squares, total):
    step = pl.program_id(0)
    term = lax.dot_general(
        grad_conv[...], weight[...], (((1,), (1,)), ((), ())), preferred_element_type=f32
    )
    wide = weight[...].astype(f32)
    square = jnp.sum((wide * wide).reshape(-1, 8, wide.shape[1]), axis=0)
    square = sum(fold(square))

    @pl.when(step == 0)
    def _():
        total[...] = term
        squares[...] = square

    @pl.when(step > 0)
    def _():
        total[...] += term
        squares[...] += square

    act_grad[...] = total[...].astype(bf16)


def total_kernel(partial, tail, out, total):
    ny = partial.shape[0]
    halves = tail.shape[0]
    total[...] = jnp.sum(partial[...].astype(f32), axis=0)
    value = total[...]
    square = jnp.sum(jnp.sum(value * value, axis=0, keepdims=True), axis=1, keepdims=True)
    square = jnp.broadcast_to(square, (1, lanes))
    y = lax.axis_index("y")
    own = [total[pl.ds(pl.multiple_of((h * ny + y) * 8, 8), 8), :] for h in range(halves)]
    extra = [*high_low(tail[...]), *high_low(square)]
    used = sum(e.shape[0] for e in extra)
    extra.append(jnp.zeros((8 - used, lanes), f32))
    tile = jnp.concatenate(own + extra, axis=0).astype(bf16)
    out[...] = jnp.broadcast_to(tile[None], out.shape)


def shape(dims, dtype):
    return jax.ShapeDtypeStruct(dims, dtype)


def whole(dims):
    return pl.BlockSpec(dims, lambda j: (0,) * len(dims))


def across(dims, axis):
    return pl.BlockSpec(dims, lambda j: tuple(j if a == axis else 0 for a in range(len(dims))))


def params(mib=24):
    return pltpu.CompilerParams(vmem_limit_bytes=mib << 20)


def local(block_input, activations, conv_weight, bn_gain, bn_shift, out_grad, velocity):
    rows, cin = activations.shape
    part, cout = conv_weight.shape
    nz, nx, ny = lax.axis_size("z"), lax.axis_size("x"), lax.axis_size("y")
    members = lax.axis_size(bn)
    steps = cout // chunk
    gain, shift = bn_gain.reshape(1, cout), bn_shift.reshape(1, cout)
    acts_t = activations.T
    per = nz // steps
    halves = cout // nz // lanes
    length = halves * ny * 8

    own = copies(conv_weight, "y").reshape(ny, part, cout)
    other = swap(own)
    tile = shape((members, steps * 8, lanes), f32)
    wide_block = across((rows, chunk), 1)
    tile_block = across((members, 8, lanes), 1)
    row_block = across((1, chunk), 1)
    weight, conv, moments = pl.pallas_call(
        moments_kernel,
        grid=(steps,),
        in_specs=[whole((rows, cin)), across((ny, part, chunk), 2), across((ny, part, chunk), 2)],
        out_specs=[across((cin, chunk), 1), wide_block, tile_block],
        out_shape=[shape((cin, cout), bf16), shape((rows, cout), f32), tile],
        compiler_params=params(),
        name="moments",
    )(activations, own, other)
    moments = exchange(moments, bn)

    grad, stats = pl.pallas_call(
        stats_kernel,
        grid=(steps,),
        in_specs=[wide_block, tile_block, row_block, row_block, wide_block, wide_block],
        out_specs=[wide_block, tile_block],
        out_shape=[shape((rows, cout), bf16), tile],
        compiler_params=params(),
        name="stats",
    )(conv, moments, gain, shift, block_input, out_grad)
    stats = exchange(stats, bn)

    piece = shape((nz, nx, length, lanes), bf16)
    piece_block = across((per, nx, length, lanes), 0)
    grad_conv, mine, theirs, tail = pl.pallas_call(
        weight_kernel,
        grid=(steps,),
        in_specs=[wide_block, tile_block, tile_block, row_block, wide_block, whole((cin, rows))],
        out_specs=[wide_block, piece_block, piece_block, across((per, nx, 8, lanes), 0)],
        out_shape=[shape((rows, cout), bf16), piece, piece, shape((nz, nx, 8, lanes), f32)],
        scratch_shapes=[pltpu.VMEM((cin, chunk), f32)],
        compiler_params=params(),
        name="weight_partial",
    )(conv, moments, stats, gain, grad, acts_t)
    pair = (mine.astype(f32) + swap(theirs).astype(f32)).astype(bf16)
    pair = jnp.concatenate([pair, tail.astype(bf16)], axis=2).reshape(nz * nx, length + 8, lanes)
    received = exchange(pair, rep)
    act_grad, squares = pl.pallas_call(
        act_kernel,
        grid=(steps,),
        in_specs=[wide_block, across((cin, chunk), 1)],
        out_specs=[whole((rows, cin)), whole((8, lanes))],
        out_shape=[shape((rows, cin), bf16), shape((8, lanes), f32)],
        scratch_shapes=[pltpu.VMEM((rows, cin), f32)],
        compiler_params=params(),
        cost_estimate=pl.CostEstimate(
            flops=2 * rows * cin * cout, bytes_accessed=2 * (rows + cin) * cout, transcendentals=0
        ),
        name="act_grad",
    )(grad_conv, weight)
    summed = jnp.sum(received.astype(f32), axis=0)
    blocks = copies(summed[:length].astype(bf16), "y")
    blocks = blocks.reshape(ny, length, lanes)
    depth = halves * 8 + 8
    ready = pl.pallas_call(
        total_kernel,
        grid=(1,),
        in_specs=[whole((ny, length, lanes)), whole((halves, lanes))],
        out_specs=whole((nz * nx, depth, lanes)),
        out_shape=shape((nz * nx, depth, lanes), bf16),
        scratch_shapes=[pltpu.VMEM((length, lanes), f32)],
        compiler_params=params(),
        name="totals",
    )(blocks, summed[length : length + halves])
    everything = exchange(ready, rep).astype(f32)

    at = halves * 8
    square = jnp.sum(everything[:, at + 2 * halves : at + 2 * halves + 2, 0])
    square_other = swap(jnp.broadcast_to(square, (8, lanes)))[0, 0]
    grid = everything.reshape(nz, nx, depth, lanes)
    weight_grad = grid[:, :, :at].reshape(nz, nx, halves, 8, lanes)
    weight_grad = weight_grad.transpose(1, 3, 0, 2, 4).reshape(part, cout)
    totals = grid[:, :, at : at + halves] + grid[:, :, at + halves : at + 2 * halves]
    totals = totals.transpose(1, 0, 2, 3).reshape(nx, cout)
    shift_grad = totals[0] + totals[1]
    gain_grad = totals[2] + totals[3]

    weight_f = conv_weight.astype(f32)
    weight_norm = jnp.sqrt(jnp.sum(squares))
    grad_norm = jnp.sqrt(square + square_other)
    ratio = weight_norm / (grad_norm + weight_decay * weight_norm)
    new_velocity = momentum * velocity + ratio * (weight_grad + weight_decay * weight_f)
    return (act_grad, gain_grad, shift_grad, new_velocity)


def solution(mesh, dims=(8, 4, 8, 2)):
    fine = Mesh(mesh.devices.reshape(dims), ("z", "x", "y", "c"))
    every = P(("z", "x", "y", "c"), None)
    return jax.shard_map(
        local,
        mesh=fine,
        in_specs=(every, every, P(bn, None), P(), P(), every, P(bn, None)),
        out_specs=(every, P(), P(), P(bn, None)),
        check_vma=False,
    )
```

time: 206 us -> 177 us (0.86)
  other arithmetic: 28.7 us -> 3.28 us
  blocking collectives: 108 us -> 92.2 us
  Pallas kernels: 0 us -> 13.3 us
  waiting for transfers between devices: 19.7 us -> 27.9 us
  matrix products: 5.6 us -> 0 us
  local copies, waits for them, and re-layouts: 16.5 us -> 12.1 us
    all_to_all x4 -> x3, blocking collectives: 108 us -> 92.2 us  [exchange(): return lax.all_to_all(pieces, axis, 0, 0, tiled=True)]
    pallas_call x0 -> x5, Pallas kernels: none -> 13.3 us  [the longest x1 4.49 us: local(): pl.pallas_call(weight_kernel, grid=(steps,), in_specs=[wide_block, tile_b...]
    reduce_sum x11 -> x3, other arithmetic: 14 us -> 1.39 us  [the longest x1 0.63 us: local(): square = jnp.sum(everything[:, at + 2 * halves:at + 2 * halves + 2, 0])]
    all_to_all x3, waiting for transfers between devices: 16.5 us -> 22.9 us  [exchange(): return lax.all_to_all(pieces, axis, 0, 0, tiled=True)]
    ppermute x2 -> x3, starting transfers between devices: 7.53 us -> 13.6 us  [swap(): return lax.ppermute(value, 'c', [(0, 1), (1, 0)])]
    dot_general x3 -> x0, matrix products: 5.6 us -> none  [the longest x1 3.29 us: local(): lax.dot_general(grad_conv, full_weight, (((1,), (1,)), ((), ())), preferr...]
    unnamed x21 -> x31, local copies, waits for them, and re-layouts: 4.49 us -> 9.1 us
    all_to_all x3, starting transfers between devices: 15.9 us -> 11.4 us  [exchange(): return lax.all_to_all(pieces, axis, 0, 0, tiled=True)]
  transfers between devices with their start and end apart: 5 -> 6, of which waited for: 5 -> 6; matrix products, arithmetic and copies ran while one was open for 5% -> 2% of each run, Pallas kernels for 0% -> 2%
where the time goes in v2:
time: 177 us
  blocking collectives  92.2 us (52%)
  waiting for transfers between devices  27.9 us (16%)
  starting transfers between devices  25 us (14%)
  Pallas kernels  13.3 us (8%)
  local copies, waits for them, and re-layouts  12.1 us (7%)
  other arithmetic  3.28 us (2%)
  between operations  2.87 us (2%)
    all_to_all x3, blocking collectives, exchange(): return lax.all_to_all(pieces, axis, 0, 0, tiled=True)  92.2 us
    all_to_all x3, waiting for transfers between devices, exchange(): return lax.all_to_all(pieces, axis, 0, 0, tiled=True)  22.9 us
    ppermute x3, starting transfers between devices, swap(): return lax.ppermute(value, 'c', [(0, 1), (1, 0)])  13.6 us
    all_to_all x3, starting transfers between devices, exchange(): return lax.all_to_all(pieces, axis, 0, 0, tiled=True)  11.4 us
    unnamed x31, local copies, waits for them, and re-layouts  9.1 us
    ppermute x3, waiting for transfers between devices, swap(): return lax.ppermute(value, 'c', [(0, 1), (1, 0)])  5.04 us
    pallas_call x1, Pallas kernels, local(): pl.pallas_call(weight_kernel, grid=(steps,), in_specs=[wide_block, tile_b...  4.49 us
  transfers between devices with their start and end apart: 6, of which 6 were waited for; matrix products, arithmetic and copies ran while one was open for 2% of the time, Pallas kernels for 2%

profile of v2, /device:TPU:1, one launch (start us, length us, event | category | flops | bytes accessed | tf_op | source)
XLA Modules:
  0.0 176.7 jit_solution(132437414583371956)
XLA Ops:
  0.6 1.1 broadcast_in_dim.6
  1.7 33.5 %all_to_all.30.own = bf16[8,32,2048]{2,1,0:T(8,128)(2,1)S(1)} all-to-all(bf16[8,32,2048]{2,1,0:T(8,128)(2,1)S(1)} %broadcast_in_dim.6), channel_id=1, replica_groups=mesh['z'=8,'x'=4,'y'=8,'c'=2] {'y'}, dimensions={0} | all-to-all | bytes 2097152 | tf_op jit(solution)/shard_map/all_to_all | solution.py:24
  35.3 5.8 %collective-permute-start = (bf16[8,32,2048]{2,1,0:T(8,128)(2,1)S(1)}, bf16[8,32,2048]{2,1,0:T(8,128)(2,1)S(1)}, u32[]{:S(2)}, u32[]{:S(2)}) collective-permute-start(bf16[8,32,2048]{2,1,0:T(8,128)(2,1)S(1)} %all_to_all.30.own), channel_id=1, source_target_pairs={{0,1},{1,0},{2,3},{3,2},{4,5},{5,4},{6,7},{7,6},{8,9},{9,8},{10,11... | collective-permute-start | bytes 3145736 | tf_op jit(solution)/shard_map/ppermute | solution.py:20
  41.0 2.3 %collective-permute-done.other = bf16[8,32,2048]{2,1,0:T(8,128)(2,1)S(1)} collective-permute-done((bf16[8,32,2048]{2,1,0:T(8,128)(2,1)S(1)}, bf16[8,32,2048]{2,1,0:T(8,128)(2,1)S(1)}, u32[]{:S(2)}, u32[]{:S(2)}) %collective-permute-start) | collective-permute-done | bytes 1048608 | tf_op jit(solution)/shard_map/ppermute | solution.py:20
  43.3 2.7 %moments.1 = (bf16[512,2048]{1,0:T(8,128)(2,1)S(1)}, f32[392,2048]{1,0:T(8,128)S(1)}, f32[16,32,128]{2,1,0:T(8,128)S(1)}) custom-call(bf16[392,512]{1,0:T(8,128)(2,1)S(1)} %copy-done.3, bf16[8,32,2048]{2,1,0:T(8,128)(2,1)S(1)} %all_to_all.30.own, bf16[8,32,2048]{2,1,0:T(8,128)(2,1)S(1)} %collective-permute-done.other), custom_call_target="tpu_custom_call" | custom-call | tf_op jit(solution)/shard_map/moments/pallas_call | solution.py:192
  46.0 1.3 copy-done.1
  47.4 14.6 %all_to_all.31.moments = f32[16,32,128]{2,1,0:T(8,128)S(1)} all-to-all(f32[16,32,128]{2,1,0:T(8,128)S(1)} %get-tuple-element.16), channel_id=1, replica_groups=mesh['z'=8,'x'=4,'y'=8,'c'=2] {'y','c'}, dimensions={0} | all-to-all | bytes 524288 | tf_op jit(solution)/shard_map/all_to_all | solution.py:24
  62.0 2.1 %stats.1 = (bf16[392,2048]{1,0:T(8,128)(2,1)S(1)}, f32[16,32,128]{2,1,0:T(8,128)S(1)}) custom-call(f32[392,2048]{1,0:T(8,128)S(1)} %get-tuple-element.15.conv, f32[16,32,128]{2,1,0:T(8,128)S(1)} %all_to_all.31.moments, f32[1,2048]{1,0:T(1,128)S(1)} %bitcast.16, f32[1,2048]{1,0:T(1,128)S(1)} %bitcast.18, bf16[392,2048]{1,0:T(8,128)(2,1)S(1)} %copy-done.6, ...), custom_call_target="tpu_custom_call" | custom-call | tf_op jit(solution)/shard_map/stats/pallas_call | solution.py:203
  64.2 1.1 copy-done.8
  65.3 0.7 copy-done.10
  66.0 4.1 %all-to-all-start.2 = ((f32[16,32,128]{2,1,0:T(8,128)}), f32[16,32,128]{2,1,0:T(8,128)}, u32[]{:S(2)}, u32[]{:S(2)}) async-start(f32[16,32,128]{2,1,0:T(8,128)} %copy-done.10), calls=%async_computation.2 | async-start | bytes 524288 | tf_op jit(solution)/shard_map/all_to_all | solution.py:24
  70.1 2.0 %copy.11 = bf16[392,512]{0,1:T(8,128)(2,1)} copy(bf16[392,512]{1,0:T(8,128)(2,1)} %acts.1) | data formatting | bytes 802816 | tf_op args[1]
  72.1 8.9 %all-to-all-done.2.stats = f32[16,32,128]{2,1,0:T(8,128)} async-done(((f32[16,32,128]{2,1,0:T(8,128)}), f32[16,32,128]{2,1,0:T(8,128)}, u32[]{:S(2)}, u32[]{:S(2)}) %all-to-all-start.2) | async-done | bytes 262176 | tf_op jit(solution)/shard_map/all_to_all | solution.py:24
  81.0 1.0 copy-done
  82.0 1.4 copy-done.9
  83.5 4.5 %weight_partial.1 = (bf16[392,2048]{1,0:T(8,128)(2,1)S(1)}, bf16[8,4,128,128]{3,2,1,0:T(8,128)(2,1)S(1)}, bf16[8,4,128,128]{3,2,1,0:T(8,128)(2,1)S(1)}, f32[8,4,8,128]{3,2,1,0:T(8,128)S(1)}) custom-call(f32[392,2048]{1,0:T(8,128)S(1)} %get-tuple-element.15.conv, f32[16,32,128]{2,1,0:T(8,128)S(1)} %all_to_all.31.moments, ...), custom_call_target="tpu_custom_call" | custom-call | tf_op jit(solution)/shard_map/weight_partial/pallas_call | solution.py:216
  88.0 1.9 %collective-permute-start.1 = (bf16[8,4,128,128]{3,2,1,0:T(8,128)(2,1)S(1)}, bf16[8,4,128,128]{3,2,1,0:T(8,128)(2,1)S(1)}, u32[]{:S(2)}, u32[]{:S(2)}) collective-permute-start(bf16[8,4,128,128]{3,2,1,0:T(8,128)(2,1)S(1)} %get-tuple-element.23), channel_id=1, source_target_pairs={{0,1},{1,0},{2,3},{3,2},{4,5},{5,4},{6,7},{7,6},{8,9},{9,8},{10,11... | collective-permute-start | bytes 3145736 | tf_op jit(solution)/shard_map/ppermute | solution.py:20
  89.9 2.6 %collective-permute-done.1 = bf16[8,4,128,128]{3,2,1,0:T(8,128)(2,1)S(1)} collective-permute-done((bf16[8,4,128,128]{3,2,1,0:T(8,128)(2,1)S(1)}, bf16[8,4,128,128]{3,2,1,0:T(8,128)(2,1)S(1)}, u32[]{:S(2)}, u32[]{:S(2)}) %collective-permute-start.1) | collective-permute-done | bytes 1048608 | tf_op jit(solution)/shard_map/ppermute | solution.py:20
  93.0 44.0 %all_to_all.32 = bf16[32,136,128]{2,1,0:T(8,128)(2,1)S(1)} all-to-all(bf16[32,136,128]{2,1,0:T(8,128)(2,1)S(1)} %bitcast.19), channel_id=1, replica_groups=mesh['z'=8,'x'=4,'y'=8,'c'=2] {'z','x'}, dimensions={0} | all-to-all | bytes 2228224 | tf_op jit(solution)/shard_map/all_to_all | solution.py:24
  137.2 0.7 broadcast_in_dim.7
  137.9 3.4 %all-to-all-start.4 = ((bf16[8,128,128]{2,1,0:T(8,128)(2,1)}), bf16[8,128,128]{2,1,0:T(8,128)(2,1)S(1)}, u32[]{:S(2)}, u32[]{:S(2)}) async-start(bf16[8,128,128]{2,1,0:T(8,128)(2,1)} %broadcast_in_dim.7), calls=%async_computation.4 | async-start | bytes 524288 | tf_op jit(solution)/shard_map/all_to_all | solution.py:24
  141.4 10.0 %all-to-all-done.4.partial = bf16[8,128,128]{2,1,0:T(8,128)(2,1)S(1)} async-done(((bf16[8,128,128]{2,1,0:T(8,128)(2,1)}), bf16[8,128,128]{2,1,0:T(8,128)(2,1)S(1)}, u32[]{:S(2)}, u32[]{:S(2)}) %all-to-all-start.4) | async-done | bytes 262176 | tf_op jit(solution)/shard_map/all_to_all | solution.py:24
  151.3 0.8 totals.1
  152.2 3.9 %all-to-all-start.5 = ((bf16[32,24,128]{2,1,0:T(8,128)(2,1)}), bf16[32,24,128]{2,1,0:T(8,128)(2,1)S(1)}, u32[]{:S(2)}, u32[]{:S(2)}) async-start(bf16[32,24,128]{2,1,0:T(8,128)(2,1)} %totals.1), calls=%async_computation.5 | async-start | bytes 393216 | tf_op jit(solution)/shard_map/all_to_all | solution.py:24
  156.1 1.4 copy-done.5
  157.5 3.1 %act_grad.1 = (bf16[392,512]{1,0:T(8,128)(2,1)}, f32[8,128]{1,0:T(8,128)S(1)}) custom-call(bf16[392,2048]{1,0:T(8,128)(2,1)S(1)} %copy-done.5, bf16[512,2048]{1,0:T(8,128)(2,1)S(1)} %copy-done.2), custom_call_target="tpu_custom_call" | custom-call | flops 822083584 | bytes 3702784 | tf_op jit(solution)/shard_map/act_grad/pallas_call | solution.py:229
  162.0 4.0 %all-to-all-done.5 = bf16[32,24,128]{2,1,0:T(8,128)(2,1)S(1)} async-done(((bf16[32,24,128]{2,1,0:T(8,128)(2,1)}), bf16[32,24,128]{2,1,0:T(8,128)(2,1)S(1)}, u32[]{:S(2)}, u32[]{:S(2)}) %all-to-all-start.5) | async-done | bytes 196640 | tf_op jit(solution)/shard_map/all_to_all | solution.py:24
  166.0 0.6 slice_reduce_fusion
  166.7 0.6 broadcast_in_dim.8
  167.4 5.9 %collective-permute-start.2 = (f32[8,128]{1,0:T(8,128)S(1)}, f32[8,128]{1,0:T(8,128)S(1)}, u32[]{:S(2)}, u32[]{:S(2)}) collective-permute-start(f32[8,128]{1,0:T(8,128)S(1)} %broadcast_in_dim.8), channel_id=1, source_target_pairs={{0,1},{1,0},{2,3},{3,2},{4,5},{5,4},{6,7},{7,6},{8,9},{9,8},{10,11... | collective-permute-start | bytes 12296 | tf_op jit(solution)/shard_map/ppermute | solution.py:20
  173.3 0.6 slice_add_fusion.1
  175.9 0.8 multiply_add_fusion
  (37 shorter events, 2.1 us)
Async XLA Ops:
  0.6 42.7 %copy-start.3 = (bf16[392,512]{1,0:T(8,128)(2,1)S(1)}, bf16[392,512]{1,0:T(8,128)(2,1)}, u32[]{:S(2)}) copy-start(bf16[392,512]{1,0:T(8,128)(2,1)} %acts.1) | copy-start | bytes 1204228
  1.7 60.3 %copy-start.7 = (bf16[392,2048]{1,0:T(8,128)(2,1)S(1)}, bf16[392,2048]{1,0:T(8,128)(2,1)}, u32[]{:S(2)}) copy-start(bf16[392,2048]{1,0:T(8,128)(2,1)} %out_grad.1) | copy-start | bytes 4816900
  35.3 26.7 %copy-start.6 = (bf16[392,2048]{1,0:T(8,128)(2,1)S(1)}, bf16[392,2048]{1,0:T(8,128)(2,1)}, u32[]{:S(2)}) copy-start(bf16[392,2048]{1,0:T(8,128)(2,1)} %block_input.1) | copy-start | bytes 4816900
  35.3 26.7 %copy-start.11 = (f32[2048]{0:T(1024)S(1)}, f32[2048]{0:T(1024)}, u32[]{:S(2)}) copy-start(f32[2048]{0:T(1024)} %param.10) | copy-start | bytes 24580
  35.3 26.7 %copy-start.12 = (f32[2048]{0:T(1024)S(1)}, f32[2048]{0:T(1024)}, u32[]{:S(2)}) copy-start(f32[2048]{0:T(1024)} %param.11) | copy-start | bytes 24580
  35.3 8.0 %collective-permute-start = (bf16[8,32,2048]{2,1,0:T(8,128)(2,1)S(1)}, bf16[8,32,2048]{2,1,0:T(8,128)(2,1)S(1)}, u32[]{:S(2)}, u32[]{:S(2)}) collective-permute-start(bf16[8,32,2048]{2,1,0:T(8,128)(2,1)S(1)} %all_to_all.30.own), channel_id=1, source_target_pairs={{0,1},{1,0},{2,3},{3,2},{4,5},{5,4},{6,7},{7,6},{8,9},{9,8},{10,11... | collective-permute-start | bytes 3145736 | tf_op jit(solution)/shard_map/ppermute | solution.py:20
  46.0 1.3 copy-start.1
  64.1 1.2 copy-start.8
  65.3 0.7 copy-start.10
  66.0 15.0 %all-to-all-start.2 = ((f32[16,32,128]{2,1,0:T(8,128)}), f32[16,32,128]{2,1,0:T(8,128)}, u32[]{:S(2)}, u32[]{:S(2)}) async-start(f32[16,32,128]{2,1,0:T(8,128)} %copy-done.10), calls=%async_computation.2 | async-start | bytes 524288 | tf_op jit(solution)/shard_map/all_to_all | solution.py:24
  81.0 1.0 copy-start
  82.0 1.4 copy-start.9
  88.0 4.9 %copy-start.4 = (bf16[392,2048]{1,0:T(8,128)(2,1)}, bf16[392,2048]{1,0:T(8,128)(2,1)S(1)}, u32[]{:S(2)}) copy-start(bf16[392,2048]{1,0:T(8,128)(2,1)S(1)} %get-tuple-element.19.grad_conv) | copy-start | bytes 4816900
  88.0 4.6 %collective-permute-start.1 = (bf16[8,4,128,128]{3,2,1,0:T(8,128)(2,1)S(1)}, bf16[8,4,128,128]{3,2,1,0:T(8,128)(2,1)S(1)}, u32[]{:S(2)}, u32[]{:S(2)}) collective-permute-start(bf16[8,4,128,128]{3,2,1,0:T(8,128)(2,1)S(1)} %get-tuple-element.23), channel_id=1, source_target_pairs={{0,1},{1,0},{2,3},{3,2},{4,5},{5,4},{6,7},{7,6},{8,9},{9,8},{10,11... | collective-permute-start | bytes 3145736 | tf_op jit(solution)/shard_map/ppermute | solution.py:20
  137.0 19.1 %copy-start.2 = (bf16[512,2048]{1,0:T(8,128)(2,1)S(1)}, bf16[512,2048]{1,0:T(8,128)(2,1)}, u32[]{:S(2)}) copy-start(bf16[512,2048]{1,0:T(8,128)(2,1)} %copy-done.1) | copy-start | bytes 6291460
  137.9 13.4 %all-to-all-start.4 = ((bf16[8,128,128]{2,1,0:T(8,128)(2,1)}), bf16[8,128,128]{2,1,0:T(8,128)(2,1)S(1)}, u32[]{:S(2)}, u32[]{:S(2)}) async-start(bf16[8,128,128]{2,1,0:T(8,128)(2,1)} %broadcast_in_dim.7), calls=%async_computation.4 | async-start | bytes 524288 | tf_op jit(solution)/shard_map/all_to_all | solution.py:24
  152.2 13.8 %all-to-all-start.5 = ((bf16[32,24,128]{2,1,0:T(8,128)(2,1)}), bf16[32,24,128]{2,1,0:T(8,128)(2,1)S(1)}, u32[]{:S(2)}, u32[]{:S(2)}) async-start(bf16[32,24,128]{2,1,0:T(8,128)(2,1)} %totals.1), calls=%async_computation.5 | async-start | bytes 393216 | tf_op jit(solution)/shard_map/all_to_all | solution.py:24
  156.1 1.4 copy-start.5
  160.7 15.2 %copy-start.13 = (bf16[32,2048]{1,0:T(8,128)(2,1)S(1)}, bf16[32,2048]{1,0:T(8,128)(2,1)}, u32[]{:S(2)}) copy-start(bf16[32,2048]{1,0:T(8,128)(2,1)} %param.9) | copy-start | bytes 393220
  160.7 15.2 %copy-start.14 = (f32[32,2048]{1,0:T(8,128)S(1)}, f32[32,2048]{1,0:T(8,128)}, u32[]{:S(2)}) copy-start(f32[32,2048]{1,0:T(8,128)} %param.13) | copy-start | bytes 786436
  167.4 6.7 %collective-permute-start.2 = (f32[8,128]{1,0:T(8,128)S(1)}, f32[8,128]{1,0:T(8,128)S(1)}, u32[]{:S(2)}, u32[]{:S(2)}) collective-permute-start(f32[8,128]{1,0:T(8,128)S(1)} %broadcast_in_dim.8), channel_id=1, source_target_pairs={{0,1},{1,0},{2,3},{3,2},{4,5},{5,4},{6,7},{7,6},{8,9},{9,8},{10,11... | collective-permute-start | bytes 12296 | tf_op jit(solution)/shard_map/ppermute | solution.py:20

commit v3 on v2

--- a/solution.py
+++ b/solution.py
@@ -1,3 +1,5 @@
+import functools
+
 import jax
 import jax.numpy as jnp
 from jax import lax
@@ -81,7 +83,9 @@
     stats[...] = jnp.broadcast_to(tile[None], stats.shape)
 
 
-def weight_kernel(conv, moments, stats, gain, grad, acts_t, grad_conv, mine, theirs, tail, wide):
+def weight_kernel(
+    conv, moments, stats, gain, grad, acts, grad_conv, mine, theirs, tail, wide, acts_t
+):
     core = lax.axis_index("c")
     rows = conv.shape[0]
     group_rows = rows * moments.shape[0]
@@ -93,6 +97,11 @@
     value = grad[...].astype(f32) - shift - (conv[...] - mean) * slope
     narrow = (gain[...] * inv_std * value).astype(bf16)
     grad_conv[...] = narrow
+
+    @pl.when(pl.program_id(0) == 0)
+    def _():
+        acts_t[...] = acts[...].T
+
     wide[...] = jnp.dot(acts_t[...], narrow, preferred_element_type=f32)
     nz, nx, length, _ = mine.shape
     part = 8 * nx
@@ -139,20 +148,41 @@
     act_grad[...] = total[...].astype(bf16)
 
 
-def total_kernel(partial, tail, out, total):
-    ny = partial.shape[0]
-    halves = tail.shape[0]
+def total_kernel(partial, summed, out, total):
+    ny, length, _ = partial.shape
+    halves = length // (8 * ny)
     total[...] = jnp.sum(partial[...].astype(f32), axis=0)
     value = total[...]
     square = jnp.sum(jnp.sum(value * value, axis=0, keepdims=True), axis=1, keepdims=True)
     square = jnp.broadcast_to(square, (1, lanes))
     y = lax.axis_index("y")
     own = [total[pl.ds(pl.multiple_of((h * ny + y) * 8, 8), 8), :] for h in range(halves)]
-    extra = [*high_low(tail[...]), *high_low(square)]
+    extra = [*high_low(summed[length : length + halves, :]), *high_low(square)]
     used = sum(e.shape[0] for e in extra)
     extra.append(jnp.zeros((8 - used, lanes), f32))
     tile = jnp.concatenate(own + extra, axis=0).astype(bf16)
     out[...] = jnp.broadcast_to(tile[None], out.shape)
+
+
+def step_kernel(nx, parts, squares, weight_squares, weight, velocity, out, gain, shift):
+    nz = parts.shape[0] // nx
+    halves = out.shape[1] // nz // lanes
+    grad_square = jnp.sum(squares[...], axis=0, keepdims=True)[:, :1]
+    weight_square = jnp.sum(weight_squares[...], axis=0, keepdims=True)
+    weight_square = jnp.sum(weight_square, axis=1, keepdims=True)
+    weight_norm = jnp.sqrt(weight_square)
+    ratio = weight_norm / (jnp.sqrt(grad_square) + weight_decay * weight_norm)
+    at = 8 * halves
+    for z in range(nz):
+        values = [parts[z * nx + x].astype(f32) for x in range(nx)]
+        for h in range(halves):
+            cols = pl.ds((z * halves + h) * lanes, lanes)
+            weight_grad = jnp.concatenate([v[8 * h : 8 * h + 8] for v in values], axis=0)
+            decayed = weight_grad + weight_decay * weight[:, cols].astype(f32)
+            out[:, cols] = momentum * velocity[:, cols] + ratio * decayed
+            sums = [v[at + h : at + h + 1] + v[at + halves + h : at + halves + h + 1] for v in values]
+            shift[:, cols] = sums[0] + sums[1]
+            gain[:, cols] = sums[2] + sums[3]
 
 
 def shape(dims, dtype):
@@ -178,7 +208,6 @@
     members = lax.axis_size(bn)
     steps = cout // chunk
     gain, shift = bn_gain.reshape(1, cout), bn_shift.reshape(1, cout)
-    acts_t = activations.T
     per = nz // steps
     halves = cout // nz // lanes
     length = halves * ny * 8
@@ -194,7 +223,7 @@
         grid=(steps,),
         in_specs=[whole((rows, cin)), across((ny, part, chunk), 2), across((ny, part, chunk), 2)],
         out_specs=[across((cin, chunk), 1), wide_block, tile_block],
-        out_shape=[shape((cin, cout), bf16), shape((rows, cout), f32), tile],
+        out_shape=[pltpu.HBM((cin, cout), bf16), shape((rows, cout), f32), tile],
         compiler_params=params(),
         name="moments",
     )(activations, own, other)
@@ -216,13 +245,13 @@
     grad_conv, mine, theirs, tail = pl.pallas_call(
         weight_kernel,
         grid=(steps,),
-        in_specs=[wide_block, tile_block, tile_block, row_block, wide_block, whole((cin, rows))],
+        in_specs=[wide_block, tile_block, tile_block, row_block, wide_block, whole((rows, cin))],
         out_specs=[wide_block, piece_block, piece_block, across((per, nx, 8, lanes), 0)],
-        out_shape=[shape((rows, cout), bf16), piece, piece, shape((nz, nx, 8, lanes), f32)],
-        scratch_shapes=[pltpu.VMEM((cin, chunk), f32)],
+        out_shape=[pltpu.HBM((rows, cout), bf16), piece, piece, shape((nz, nx, 8, lanes), f32)],
+        scratch_shapes=[pltpu.VMEM((cin, chunk), f32), pltpu.VMEM((cin, rows), bf16)],
         compiler_params=params(),
         name="weight_partial",
-    )(conv, moments, stats, gain, grad, acts_t)
+    )(conv, moments, stats, gain, grad, activations)
     pair = (mine.astype(f32) + swap(theirs).astype(f32)).astype(bf16)
     pair = jnp.concatenate([pair, tail.astype(bf16)], axis=2).reshape(nz * nx, length + 8, lanes)
     received = exchange(pair, rep)
@@ -246,32 +275,33 @@
     ready = pl.pallas_call(
         total_kernel,
         grid=(1,),
-        in_specs=[whole((ny, length, lanes)), whole((halves, lanes))],
+        in_specs=[whole((ny, length, lanes)), whole((length + 8, lanes))],
         out_specs=whole((nz * nx, depth, lanes)),
         out_shape=shape((nz * nx, depth, lanes), bf16),
         scratch_shapes=[pltpu.VMEM((length, lanes), f32)],
         compiler_params=params(),
         name="totals",
-    )(blocks, summed[length : length + halves])
-    everything = exchange(ready, rep).astype(f32)
-
-    at = halves * 8
-    square = jnp.sum(everything[:, at + 2 * halves : at + 2 * halves + 2, 0])
-    square_other = swap(jnp.broadcast_to(square, (8, lanes)))[0, 0]
-    grid = everything.reshape(nz, nx, depth, lanes)
-    weight_grad = grid[:, :, :at].reshape(nz, nx, halves, 8, lanes)
-    weight_grad = weight_grad.transpose(1, 3, 0, 2, 4).reshape(part, cout)
-    totals = grid[:, :, at : at + halves] + grid[:, :, at + halves : at + 2 * halves]
-    totals = totals.transpose(1, 0, 2, 3).reshape(nx, cout)
-    shift_grad = totals[0] + totals[1]
-    gain_grad = totals[2] + totals[3]
-
-    weight_f = conv_weight.astype(f32)
-    weight_norm = jnp.sqrt(jnp.sum(squares))
-    grad_norm = jnp.sqrt(square + square_other)
-    ratio = weight_norm / (grad_norm + weight_decay * weight_norm)
-    new_velocity = momentum * velocity + ratio * (weight_grad + weight_decay * weight_f)
-    return (act_grad, gain_grad, shift_grad, new_velocity)
+    )(blocks, summed)
+    ready = exchange(ready, rep)
+    at = halves * 8 + 2 * halves
+    square = jnp.sum(ready[:, at : at + 2].astype(f32), axis=(0, 1))
+    square = lax.all_gather(square, "c")
+    new_velocity, gain_grad, shift_grad = pl.pallas_call(
+        functools.partial(step_kernel, nx),
+        grid=(1,),
+        in_specs=[
+            whole((nz * nx, depth, lanes)),
+            whole((2, lanes)),
+            whole((8, lanes)),
+            whole((part, cout)),
+            whole((part, cout)),
+        ],
+        out_specs=[whole((part, cout)), whole((1, cout)), whole((1, cout))],
+        out_shape=[shape((part, cout), f32), shape((1, cout), f32), shape((1, cout), f32)],
+        compiler_params=params(),
+        name="step",
+    )(ready, square, squares, conv_weight, velocity)
+    return (act_grad, gain_grad.reshape(cout), shift_grad.reshape(cout), new_velocity)
 
 
 def solution(mesh, dims=(8, 4, 8, 2)):

time: 177 us -> 165 us (0.932)
  blocking collectives: 92.2 us -> 125 us
  waiting for transfers between devices: 27.9 us -> 10.2 us
  starting transfers between devices: 25 us -> 11.6 us
  local copies, waits for them, and re-layouts: 12.1 us -> 2.55 us
  other arithmetic: 3.28 us -> 0.69 us
  between operations: 2.87 us -> 0.76 us
    all_to_all x3 -> x5, blocking collectives: 92.2 us -> 119 us  [exchange(): return lax.all_to_all(pieces, axis, 0, 0, tiled=True)]
    all_to_all x3 -> x1, waiting for transfers between devices: 22.9 us -> 5.3 us  [exchange(): return lax.all_to_all(pieces, axis, 0, 0, tiled=True)]
    unnamed x31 -> x18, local copies, waits for them, and re-layouts: 9.1 us -> 1.44 us
    all_to_all x3 -> x1, starting transfers between devices: 11.4 us -> 3.92 us  [exchange(): return lax.all_to_all(pieces, axis, 0, 0, tiled=True)]
    ppermute x3 -> x2, starting transfers between devices: 13.6 us -> 7.66 us  [swap(): return lax.ppermute(value, 'c', [(0, 1), (1, 0)])]
    all_gather x0 -> x1, blocking collectives: none -> 5.46 us  [local(): square = lax.all_gather(square, 'c')]
    ppermute x3 -> x2, waiting for transfers between devices: 5.04 us -> 4.87 us  [swap(): return lax.ppermute(value, 'c', [(0, 1), (1, 0)])]
  transfers between devices with their start and end apart: 6 -> 3, of which waited for: 6 -> 3; matrix products, arithmetic and copies ran while one was open for 2% -> 0% of each run, Pallas kernels for 2% -> 2%
where the time goes in v3:
time: 165 us; the launch traced here: 164 us
  blocking collectives  125 us (76%)
  Pallas kernels  14.2 us (9%)
  starting transfers between devices  11.6 us (7%)
  waiting for transfers between devices  10.2 us (6%)
  local copies, waits for them, and re-layouts  2.55 us (2%)
    all_to_all x5, blocking collectives, exchange(): return lax.all_to_all(pieces, axis, 0, 0, tiled=True)  119 us
    ppermute x2, starting transfers between devices, swap(): return lax.ppermute(value, 'c', [(0, 1), (1, 0)])  7.66 us
    all_gather x1, blocking collectives, local(): square = lax.all_gather(square, 'c')  5.46 us
    all_to_all x1, waiting for transfers between devices, exchange(): return lax.all_to_all(pieces, axis, 0, 0, tiled=True)  5.3 us
    ppermute x2, waiting for transfers between devices, swap(): return lax.ppermute(value, 'c', [(0, 1), (1, 0)])  4.87 us
    pallas_call x1, Pallas kernels, local(): pl.pallas_call(weight_kernel, grid=(steps,), in_specs=[wide_block, tile_b...  4.32 us
    all_to_all x1, starting transfers between devices, exchange(): return lax.all_to_all(pieces, axis, 0, 0, tiled=True)  3.92 us
  transfers between devices with their start and end apart: 3, of which 3 were waited for; matrix products, arithmetic and copies ran while one was open for 0% of the time, Pallas kernels for 2%

profile of v3, /device:TPU:1, one launch (start us, length us, event | category | flops | bytes accessed | tf_op | source)
XLA Modules:
  0.0 164.5 jit_solution(3832367082252835199)
XLA Ops:
  0.6 0.0 copy-start.1
  0.6 1.1 broadcast_in_dim.4
  1.7 0.0 copy-start.4
  1.7 33.5 %all_to_all.30.own = bf16[8,32,2048]{2,1,0:T(8,128)(2,1)S(1)} all-to-all(bf16[8,32,2048]{2,1,0:T(8,128)(2,1)S(1)} %broadcast_in_dim.4), channel_id=1, replica_groups=mesh['z'=8,'x'=4,'y'=8,'c'=2] {'y'}, dimensions={0} | all-to-all | bytes 2097152 | tf_op jit(solution)/shard_map/all_to_all | solution.py:26
  35.3 5.8 %collective-permute-start = (bf16[8,32,2048]{2,1,0:T(8,128)(2,1)S(1)}, bf16[8,32,2048]{2,1,0:T(8,128)(2,1)S(1)}, u32[]{:S(2)}, u32[]{:S(2)}) collective-permute-start(bf16[8,32,2048]{2,1,0:T(8,128)(2,1)S(1)} %all_to_all.30.own), channel_id=1, source_target_pairs={{0,1},{1,0},{2,3},{3,2},{4,5},{5,4},{6,7},{7,6},{8,9},{9,8},{10,11... | collective-permute-start | bytes 3145736 | tf_op jit(solution)/shard_map/ppermute | solution.py:22
  41.0 2.3 %collective-permute-done.other = bf16[8,32,2048]{2,1,0:T(8,128)(2,1)S(1)} collective-permute-done((bf16[8,32,2048]{2,1,0:T(8,128)(2,1)S(1)}, bf16[8,32,2048]{2,1,0:T(8,128)(2,1)S(1)}, u32[]{:S(2)}, u32[]{:S(2)}) %collective-permute-start) | collective-permute-done | bytes 1048608 | tf_op jit(solution)/shard_map/ppermute | solution.py:22
  43.3 0.0 copy-done.1
  43.3 2.9 %moments.1 = (bf16[512,2048]{1,0:T(8,128)(2,1)}, f32[392,2048]{1,0:T(8,128)S(1)}, f32[16,32,128]{2,1,0:T(8,128)S(1)}) custom-call(bf16[392,512]{1,0:T(8,128)(2,1)S(1)} %copy-done.1, bf16[8,32,2048]{2,1,0:T(8,128)(2,1)S(1)} %all_to_all.30.own, bf16[8,32,2048]{2,1,0:T(8,128)(2,1)S(1)} %collective-permute-done.other), custom_call_target="tpu_custom_call" | custom-call | tf_op jit(solution)/shard_map/moments/pallas_call | solution.py:221
  46.2 14.6 %all_to_all.31.moments = f32[16,32,128]{2,1,0:T(8,128)S(1)} all-to-all(f32[16,32,128]{2,1,0:T(8,128)S(1)} %get-tuple-element.19), channel_id=1, replica_groups=mesh['z'=8,'x'=4,'y'=8,'c'=2] {'y','c'}, dimensions={0} | all-to-all | bytes 524288 | tf_op jit(solution)/shard_map/all_to_all | solution.py:26
  60.8 0.0 copy-done.4
  60.8 0.0 copy-done.3
  60.8 0.0 copy-done.7
  60.8 0.0 copy-done.8
  60.8 2.1 %stats.1 = (bf16[392,2048]{1,0:T(8,128)(2,1)S(1)}, f32[16,32,128]{2,1,0:T(8,128)S(1)}) custom-call(f32[392,2048]{1,0:T(8,128)S(1)} %get-tuple-element.18.conv, f32[16,32,128]{2,1,0:T(8,128)S(1)} %all_to_all.31.moments, f32[1,2048]{1,0:T(1,128)S(1)} %bitcast.7, f32[1,2048]{1,0:T(1,128)S(1)} %bitcast.9, bf16[392,2048]{1,0:T(8,128)(2,1)S(1)} %copy-done.3, ...), custom_call_target="tpu_custom_call" | custom-call | tf_op jit(solution)/shard_map/stats/pallas_call | solution.py:232
  63.0 14.3 %all_to_all.32.stats = f32[16,32,128]{2,1,0:T(8,128)S(1)} all-to-all(f32[16,32,128]{2,1,0:T(8,128)S(1)} %get-tuple-element.20), channel_id=1, replica_groups=mesh['z'=8,'x'=4,'y'=8,'c'=2] {'y','c'}, dimensions={0} | all-to-all | bytes 524288 | tf_op jit(solution)/shard_map/all_to_all | solution.py:26
  77.2 4.3 %weight_partial.1 = (bf16[392,2048]{1,0:T(8,128)(2,1)}, bf16[8,4,128,128]{3,2,1,0:T(8,128)(2,1)S(1)}, bf16[8,4,128,128]{3,2,1,0:T(8,128)(2,1)S(1)}, f32[8,4,8,128]{3,2,1,0:T(8,128)S(1)}) custom-call(f32[392,2048]{1,0:T(8,128)S(1)} %get-tuple-element.18.conv, f32[16,32,128]{2,1,0:T(8,128)S(1)} %all_to_all.31.moments, f32[16,32,128]{2,1,0:T(8,128)S(1)} %all_to_all.32.stats, ...), custom_call_target="tpu_custom_call" | custom-call | tf_op jit(solution)/shard_map/weight_partial/pallas_call | solution.py:245
  81.6 1.9 %collective-permute-start.1 = (bf16[8,4,128,128]{3,2,1,0:T(8,128)(2,1)S(1)}, bf16[8,4,128,128]{3,2,1,0:T(8,128)(2,1)S(1)}, u32[]{:S(2)}, u32[]{:S(2)}) collective-permute-start(bf16[8,4,128,128]{3,2,1,0:T(8,128)(2,1)S(1)} %get-tuple-element.26), channel_id=1, source_target_pairs={{0,1},{1,0},{2,3},{3,2},{4,5},{5,4},{6,7},{7,6},{8,9},{9,8},{10,11... | collective-permute-start | bytes 3145736 | tf_op jit(solution)/shard_map/ppermute | solution.py:22
  83.5 2.6 %collective-permute-done.1 = bf16[8,4,128,128]{3,2,1,0:T(8,128)(2,1)S(1)} collective-permute-done((bf16[8,4,128,128]{3,2,1,0:T(8,128)(2,1)S(1)}, bf16[8,4,128,128]{3,2,1,0:T(8,128)(2,1)S(1)}, u32[]{:S(2)}, u32[]{:S(2)}) %collective-permute-start.1) | collective-permute-done | bytes 1048608 | tf_op jit(solution)/shard_map/ppermute | solution.py:22
  86.1 0.4 add_convert_fusion
  86.5 0.1 pad_maximum_fusion
  86.6 44.0 %all_to_all.33 = bf16[32,136,128]{2,1,0:T(8,128)(2,1)S(1)} all-to-all(bf16[32,136,128]{2,1,0:T(8,128)(2,1)S(1)} %bitcast.11), channel_id=1, replica_groups=mesh['z'=8,'x'=4,'y'=8,'c'=2] {'z','x'}, dimensions={0} | all-to-all | bytes 2228224 | tf_op jit(solution)/shard_map/all_to_all | solution.py:26
  130.6 0.2 convert_reduce_fusion.summed
  130.8 12.6 %all_to_all.34.partial = bf16[8,128,128]{2,1,0:T(8,128)(2,1)S(1)} all-to-all(bf16[8,128,128]{2,1,0:T(8,128)(2,1)S(1)} %broadcast_in_dim.5), channel_id=1, replica_groups=mesh['z'=8,'x'=4,'y'=8,'c'=2] {'y'}, dimensions={0} | all-to-all | bytes 524288 | tf_op jit(solution)/shard_map/all_to_all | solution.py:26
  143.4 0.8 totals.1
  144.3 3.9 %all-to-all-start.5 = ((bf16[32,24,128]{2,1,0:T(8,128)(2,1)}), bf16[32,24,128]{2,1,0:T(8,128)(2,1)S(1)}, u32[]{:S(2)}, u32[]{:S(2)}) async-start(bf16[32,24,128]{2,1,0:T(8,128)(2,1)} %totals.1), calls=%async_computation.5 | async-start | bytes 393216 | tf_op jit(solution)/shard_map/all_to_all | solution.py:26
  148.2 1.4 copy-done.2
  149.6 3.1 %act_grad.1 = (bf16[392,512]{1,0:T(8,128)(2,1)}, f32[8,128]{1,0:T(8,128)S(1)}) custom-call(bf16[392,2048]{1,0:T(8,128)(2,1)S(1)} %copy-done.2, bf16[512,2048]{1,0:T(8,128)(2,1)S(1)} %copy-done), custom_call_target="tpu_custom_call" | custom-call | flops 822083584 | bytes 3702784 | tf_op jit(solution)/shard_map/act_grad/pallas_call | solution.py:258
  152.8 5.3 %all-to-all-done.5.parts = bf16[32,24,128]{2,1,0:T(8,128)(2,1)S(1)} async-done(((bf16[32,24,128]{2,1,0:T(8,128)(2,1)}), bf16[32,24,128]{2,1,0:T(8,128)(2,1)S(1)}, u32[]{:S(2)}, u32[]{:S(2)}) %all-to-all-start.5) | async-done | bytes 196640 | tf_op jit(solution)/shard_map/all_to_all | solution.py:26
  158.1 0.1 convert_reduce_fusion.1
  158.1 5.5 %all-gather.1 = f32[2,1,128]{2,1,0:T(1,128)S(1)} all-gather(f32[1,1,128]{2,1,0:T(1,128)S(1)} %bitcast.12), channel_id=2, replica_groups=mesh['z'=8,'x'=4,'y'=8,'c'=2] {'c'}, dimensions={0}, use_global_device_ids=true | all-gather | bytes 1536 | tf_op jit(solution)/shard_map/all_gather | solution.py:288
  163.6 0.0 copy-done.5
  163.6 0.9 step.1
  (12 shorter events, 0.1 us)
Async XLA Ops:
  0.6 42.7 %copy-start.1 = (bf16[392,512]{1,0:T(8,128)(2,1)S(1)}, bf16[392,512]{1,0:T(8,128)(2,1)}, u32[]{:S(2)}) copy-start(bf16[392,512]{1,0:T(8,128)(2,1)} %acts.3) | copy-start | bytes 1204228
  1.7 59.1 %copy-start.4 = (bf16[392,2048]{1,0:T(8,128)(2,1)S(1)}, bf16[392,2048]{1,0:T(8,128)(2,1)}, u32[]{:S(2)}) copy-start(bf16[392,2048]{1,0:T(8,128)(2,1)} %out_grad.1) | copy-start | bytes 4816900
  35.3 25.6 %copy-start.3 = (bf16[392,2048]{1,0:T(8,128)(2,1)S(1)}, bf16[392,2048]{1,0:T(8,128)(2,1)}, u32[]{:S(2)}) copy-start(bf16[392,2048]{1,0:T(8,128)(2,1)} %block_input.1) | copy-start | bytes 4816900
  35.3 25.6 %copy-start.7 = (f32[2048]{0:T(1024)S(1)}, f32[2048]{0:T(1024)}, u32[]{:S(2)}) copy-start(f32[2048]{0:T(1024)} %param.10) | copy-start | bytes 24580
  35.3 25.6 %copy-start.8 = (f32[2048]{0:T(1024)S(1)}, f32[2048]{0:T(1024)}, u32[]{:S(2)}) copy-start(f32[2048]{0:T(1024)} %param.11) | copy-start | bytes 24580
  35.3 8.0 %collective-permute-start = (bf16[8,32,2048]{2,1,0:T(8,128)(2,1)S(1)}, bf16[8,32,2048]{2,1,0:T(8,128)(2,1)S(1)}, u32[]{:S(2)}, u32[]{:S(2)}) collective-permute-start(bf16[8,32,2048]{2,1,0:T(8,128)(2,1)S(1)} %all_to_all.30.own), channel_id=1, source_target_pairs={{0,1},{1,0},{2,3},{3,2},{4,5},{5,4},{6,7},{7,6},{8,9},{9,8},{10,11... | collective-permute-start | bytes 3145736 | tf_op jit(solution)/shard_map/ppermute | solution.py:22
  81.6 4.5 %collective-permute-start.1 = (bf16[8,4,128,128]{3,2,1,0:T(8,128)(2,1)S(1)}, bf16[8,4,128,128]{3,2,1,0:T(8,128)(2,1)S(1)}, u32[]{:S(2)}, u32[]{:S(2)}) collective-permute-start(bf16[8,4,128,128]{3,2,1,0:T(8,128)(2,1)S(1)} %get-tuple-element.26), channel_id=1, source_target_pairs={{0,1},{1,0},{2,3},{3,2},{4,5},{5,4},{6,7},{7,6},{8,9},{9,8},{10,11... | collective-permute-start | bytes 3145736 | tf_op jit(solution)/shard_map/ppermute | solution.py:22
  130.6 17.6 %copy-start = (bf16[512,2048]{1,0:T(8,128)(2,1)S(1)}, bf16[512,2048]{1,0:T(8,128)(2,1)}, u32[]{:S(2)}) copy-start(bf16[512,2048]{1,0:T(8,128)(2,1)} %get-tuple-element.23.weight) | copy-start | bytes 6291460
  144.3 13.8 %all-to-all-start.5 = ((bf16[32,24,128]{2,1,0:T(8,128)(2,1)}), bf16[32,24,128]{2,1,0:T(8,128)(2,1)S(1)}, u32[]{:S(2)}, u32[]{:S(2)}) async-start(bf16[32,24,128]{2,1,0:T(8,128)(2,1)} %totals.1), calls=%async_computation.5 | async-start | bytes 393216 | tf_op jit(solution)/shard_map/all_to_all | solution.py:26
  148.2 1.4 copy-start.2
  149.6 14.0 %copy-start.5 = (bf16[32,2048]{1,0:T(8,128)(2,1)S(1)}, bf16[32,2048]{1,0:T(8,128)(2,1)}, u32[]{:S(2)}) copy-start(bf16[32,2048]{1,0:T(8,128)(2,1)} %weight.1) | copy-start | bytes 393220
  149.6 14.0 %copy-start.6 = (f32[32,2048]{1,0:T(8,128)S(1)}, f32[32,2048]{1,0:T(8,128)}, u32[]{:S(2)}) copy-start(f32[32,2048]{1,0:T(8,128)} %velocity.1) | copy-start | bytes 786436

commit v4 on v3

v4 whole, which is shorter than its diff:
```python
import functools

import jax
import jax.numpy as jnp
from jax import lax
from jax.experimental import pallas as pl
from jax.experimental.pallas import tpu as pltpu
from jax.sharding import Mesh, PartitionSpec as P

epsilon = 1e-05
weight_decay = 5e-05
momentum = 0.9
f32, bf16 = jnp.float32, jnp.bfloat16
rep = ("z", "x")
bn = ("y", "c")
lanes = 128
chunk = 512
groups = chunk // lanes


def swap(value):
    return lax.ppermute(value, "c", [(0, 1), (1, 0)])


def exchange(pieces, axis):
    return lax.all_to_all(pieces, axis, 0, 0, tiled=True)


def copies(value, axis):
    n = lax.axis_size(axis)
    return exchange(jnp.broadcast_to(value[None], (n, *value.shape)), axis)


def fold(row):
    return [row[:, q * lanes : (q + 1) * lanes] for q in range(groups)]


def unfold(tile):
    return jnp.concatenate([tile[q : q + 1] for q in range(groups)], axis=1)


def high_low(value):
    high = value.astype(bf16).astype(f32)
    return high, value - high


def columns(width):
    return [pl.ds(start, chunk) for start in range(0, width, chunk)]


def moments_kernel(acts, own, other, weight, conv, moments):
    core = lax.axis_index("c")
    count, part, cout = own.shape
    for y in range(count):
        at = pl.multiple_of((2 * y + core) * part, part)
        weight[pl.ds(at, part), :] = own[y]
        at = pl.multiple_of((2 * y + 1 - core) * part, part)
        weight[pl.ds(at, part), :] = other[y]
    for j, cols in enumerate(columns(cout)):
        out = jnp.dot(acts[...], weight[:, cols], preferred_element_type=f32)
        conv[:, cols] = out
        mean = jnp.sum(out, axis=0, keepdims=True) / out.shape[0]
        spread = out - mean
        square = jnp.sum(spread * spread, axis=0, keepdims=True)
        tile = jnp.concatenate(fold(mean) + fold(square), axis=0)
        moments[:, 8 * j : 8 * j + 8] = jnp.broadcast_to(tile[None], (moments.shape[0], 8, lanes))


def pooled(moments, rows):
    members = moments.shape[0]
    means, squares = moments[:, :groups], moments[:, groups:]
    mean = jnp.sum(means, axis=0) / members
    offset = means - mean[None]
    square = jnp.sum(squares, axis=0) + rows * jnp.sum(offset * offset, axis=0)
    inv_std = lax.rsqrt(square / (rows * members) + epsilon)
    return unfold(mean), unfold(inv_std)


def stats_kernel(conv, moments, gain, shift, block_input, out_grad, grad, stats):
    rows, cout = conv.shape
    for j, cols in enumerate(columns(cout)):
        mean, inv_std = pooled(moments[:, 8 * j : 8 * j + 8], rows)
        centered = conv[:, cols] - mean
        scale = gain[:, cols] * inv_std
        summed = centered * scale + shift[:, cols] + block_input[:, cols].astype(f32)
        value = jnp.where(summed > 0.0, out_grad[:, cols].astype(f32), 0.0)
        grad[:, cols] = value.astype(bf16)
        sum_grad = jnp.sum(value, axis=0, keepdims=True)
        sum_cross = jnp.sum(value * centered, axis=0, keepdims=True) * inv_std
        tile = jnp.concatenate(fold(sum_grad) + fold(sum_cross), axis=0)
        stats[:, 8 * j : 8 * j + 8] = jnp.broadcast_to(tile[None], (stats.shape[0], 8, lanes))


def weight_kernel(
    conv, moments, stats, gain, grad, acts, grad_conv, mine, theirs, tail, wide, acts_t
):
    core = lax.axis_index("c")
    rows, cout = conv.shape
    group_rows = rows * moments.shape[0]
    nz, nx, length, _ = mine.shape
    part = 8 * nx
    ny = wide.shape[0] // (2 * part)
    halves = cout // nz // lanes
    per = chunk // lanes // halves
    acts_t[...] = acts[...].T
    for j, cols in enumerate(columns(cout)):
        mean, inv_std = pooled(moments[:, 8 * j : 8 * j + 8], rows)
        sums = jnp.sum(stats[:, 8 * j : 8 * j + 8], axis=0)
        sum_grad, sum_cross = sums[:groups], sums[groups:]
        shift = unfold(sum_grad) / group_rows
        slope = inv_std * unfold(sum_cross) / group_rows
        value = grad[:, cols].astype(f32) - shift - (conv[:, cols] - mean) * slope
        narrow = (gain[:, cols] * inv_std * value).astype(bf16)
        grad_conv[:, cols] = narrow
        wide[...] = jnp.dot(acts_t[...], narrow, preferred_element_type=f32)
        planes = (*high_low(sum_grad), *high_low(sum_cross))
        for k in range(per):
            for x in range(nx):
                for out, owner in ((mine, core), (theirs, 1 - core)):
                    rows_of = [
                        wide[
                            pl.ds(pl.multiple_of((2 * y + owner) * part + 8 * x, 8), 8),
                            pl.ds((k * halves + h) * lanes, lanes),
                        ]
                        for h in range(halves)
                        for y in range(ny)
                    ]
                    out[j * per + k, x] = jnp.concatenate(rows_of, axis=0).astype(bf16)
                rows_of = planes[x][k * halves : (k + 1) * halves]
                rows_of = [rows_of, jnp.zeros((16 - halves, lanes), f32)]
                tail[j * per + k, x] = jnp.concatenate(rows_of, axis=0).astype(bf16)


def act_kernel(grad_conv, weight, act_grad, squares):
    act_grad[...] = lax.dot_general(
        grad_conv[...], weight[...], (((1,), (1,)), ((), ())), preferred_element_type=f32
    ).astype(bf16)
    total = jnp.zeros((8, lanes), f32)
    for cols in columns(weight.shape[1]):
        wide = weight[:, cols].astype(f32)
        total += sum(fold(jnp.sum((wide * wide).reshape(-1, 8, chunk), axis=0)))
    squares[...] = total


def total_kernel(partial, summed, out, total):
    ny, length, _ = partial.shape
    halves = length // (8 * ny)
    total[...] = jnp.sum(partial[...].astype(f32), axis=0)
    value = total[...]
    square = jnp.sum(jnp.sum(value * value, axis=0, keepdims=True), axis=1, keepdims=True)
    square = jnp.broadcast_to(square, (1, lanes))
    y = lax.axis_index("y")
    own = [total[pl.ds(pl.multiple_of((h * ny + y) * 8, 8), 8), :] for h in range(halves)]
    extra = [*high_low(summed[length : length + halves, :]), *high_low(square)]
    used = sum(e.shape[0] for e in extra)
    extra.append(jnp.zeros((8 - used, lanes), f32))
    tile = jnp.concatenate(own + extra, axis=0).astype(bf16)
    out[...] = jnp.broadcast_to(tile[None], out.shape)


def step_kernel(nx, parts, squares, weight_squares, weight, velocity, out, gain, shift):
    nz = parts.shape[0] // nx
    halves = out.shape[1] // nz // lanes
    grad_square = jnp.sum(squares[...], axis=0, keepdims=True)[:, :1]
    weight_square = jnp.sum(weight_squares[...], axis=0, keepdims=True)
    weight_square = jnp.sum(weight_square, axis=1, keepdims=True)
    weight_norm = jnp.sqrt(weight_square)
    ratio = weight_norm / (jnp.sqrt(grad_square) + weight_decay * weight_norm)
    at = 8 * halves
    for z in range(nz):
        values = [parts[z * nx + x].astype(f32) for x in range(nx)]
        for h in range(halves):
            cols = pl.ds((z * halves + h) * lanes, lanes)
            weight_grad = jnp.concatenate([v[8 * h : 8 * h + 8] for v in values], axis=0)
            decayed = weight_grad + weight_decay * weight[:, cols].astype(f32)
            out[:, cols] = momentum * velocity[:, cols] + ratio * decayed
            sums = [v[at + h : at + h + 1] + v[at + halves + h : at + halves + h + 1] for v in values]
            shift[:, cols] = sums[0] + sums[1]
            gain[:, cols] = sums[2] + sums[3]


def shape(dims, dtype):
    return jax.ShapeDtypeStruct(dims, dtype)


def whole(dims):
    return pl.BlockSpec(dims, lambda j: (0,) * len(dims))


def params(mib=24):
    return pltpu.CompilerParams(vmem_limit_bytes=mib << 20)


def local(block_input, activations, conv_weight, bn_gain, bn_shift, out_grad, velocity):
    rows, cin = activations.shape
    part, cout = conv_weight.shape
    nz, nx, ny = lax.axis_size("z"), lax.axis_size("x"), lax.axis_size("y")
    members = lax.axis_size(bn)
    gain, shift = bn_gain.reshape(1, cout), bn_shift.reshape(1, cout)
    halves = cout // nz // lanes
    length = halves * ny * 8

    own = copies(conv_weight, "y").reshape(ny, part, cout)
    other = swap(own)
    sums = (members, 2 * cout // lanes, lanes)
    weight, conv, moments = pl.pallas_call(
        moments_kernel,
        grid=(1,),
        in_specs=[whole((rows, cin)), whole((ny, part, cout)), whole((ny, part, cout))],
        out_specs=[whole((cin, cout)), whole((rows, cout)), whole(sums)],
        out_shape=[shape((cin, cout), bf16), shape((rows, cout), f32), shape(sums, f32)],
        compiler_params=params(),
        name="moments",
    )(activations, own, other)
    moments = exchange(moments, bn)

    grad, stats = pl.pallas_call(
        stats_kernel,
        grid=(1,),
        in_specs=[whole((rows, cout)), whole(sums)]
        + [whole((1, cout))] * 2
        + [whole((rows, cout))] * 2,
        out_specs=[whole((rows, cout)), whole(sums)],
        out_shape=[shape((rows, cout), bf16), shape(sums, f32)],
        compiler_params=params(),
        name="stats",
    )(conv, moments, gain, shift, block_input, out_grad)
    stats = exchange(stats, bn)

    piece, extra = (nz, nx, length, lanes), (nz, nx, 16, lanes)
    grad_conv, mine, theirs, tail = pl.pallas_call(
        weight_kernel,
        grid=(1,),
        in_specs=[
            whole((rows, cout)),
            whole(sums),
            whole(sums),
            whole((1, cout)),
            whole((rows, cout)),
            whole((rows, cin)),
        ],
        out_specs=[whole((rows, cout)), whole(piece), whole(piece), whole(extra)],
        out_shape=[
            shape((rows, cout), bf16),
            shape(piece, bf16),
            shape(piece, bf16),
            shape(extra, bf16),
        ],
        scratch_shapes=[
            pltpu.VMEM((cin, chunk), f32),
            pltpu.VMEM((cin, rows), bf16),
        ],
        compiler_params=params(),
        name="weight_partial",
    )(conv, moments, stats, gain, grad, activations)
    arrived = swap(theirs)
    act_grad, squares = pl.pallas_call(
        act_kernel,
        grid=(1,),
        in_specs=[whole((rows, cout)), whole((cin, cout))],
        out_specs=[whole((rows, cin)), whole((8, lanes))],
        out_shape=[shape((rows, cin), bf16), shape((8, lanes), f32)],
        compiler_params=params(),
        cost_estimate=pl.CostEstimate(
            flops=2 * rows * cin * cout, bytes_accessed=2 * (rows + cin) * cout, transcendentals=0
        ),
        name="act_grad",
    )(grad_conv, weight)
    arrived, act_grad = lax.optimization_barrier((arrived, act_grad))
    pair = (mine.astype(f32) + arrived.astype(f32)).astype(bf16)
    pair = jnp.concatenate([pair, tail], axis=2).reshape(nz * nx, length + 16, lanes)
    received = exchange(pair, rep)
    summed = jnp.sum(received.astype(f32), axis=0)
    blocks = copies(summed[:length].astype(bf16), "y")
    blocks = blocks.reshape(ny, length, lanes)
    depth = halves * 8 + 8
    ready = pl.pallas_call(
        total_kernel,
        grid=(1,),
        in_specs=[whole((ny, length, lanes)), whole((length + 16, lanes))],
        out_specs=whole((nz * nx, depth, lanes)),
        out_shape=shape((nz * nx, depth, lanes), bf16),
        scratch_shapes=[pltpu.VMEM((length, lanes), f32)],
        compiler_params=params(),
        name="totals",
    )(blocks, summed)
    ready = exchange(ready, rep)
    at = halves * 8 + 2 * halves
    square = jnp.sum(ready[:, at : at + 2].astype(f32), axis=(0, 1))
    square = lax.all_gather(square, "c")
    new_velocity, gain_grad, shift_grad = pl.pallas_call(
        functools.partial(step_kernel, nx),
        grid=(1,),
        in_specs=[
            whole((nz * nx, depth, lanes)),
            whole((2, lanes)),
            whole((8, lanes)),
            whole((part, cout)),
            whole((part, cout)),
        ],
        out_specs=[whole((part, cout)), whole((1, cout)), whole((1, cout))],
        out_shape=[shape((part, cout), f32), shape((1, cout), f32), shape((1, cout), f32)],
        compiler_params=params(),
        name="step",
    )(ready, square, squares, conv_weight, velocity)
    return (act_grad, gain_grad.reshape(cout), shift_grad.reshape(cout), new_velocity)


def solution(mesh, dims=(8, 4, 8, 2)):
    fine = Mesh(mesh.devices.reshape(dims), ("z", "x", "y", "c"))
    every = P(("z", "x", "y", "c"), None)
    return jax.shard_map(
        local,
        mesh=fine,
        in_specs=(every, every, P(bn, None), P(), P(), every, P(bn, None)),
        out_specs=(every, P(), P(), P(bn, None)),
        check_vma=False,
    )
```

time: 165 us -> 160 us (0.970)
  blocking collectives: 125 us -> 139 us
  waiting for transfers between devices: 10.2 us -> 3.1 us
  Pallas kernels: 14.2 us -> 7.62 us
  starting transfers between devices: 11.6 us -> 7.67 us
    all_to_all x5 -> x6, blocking collectives: 119 us -> 134 us  [exchange(): return lax.all_to_all(pieces, axis, 0, 0, tiled=True)]
    pallas_call x4, Pallas kernels: 12.5 us -> 6.56 us  [the longest x1 1.84 us: local(): pl.pallas_call(weight_kernel, grid=(1,), in_specs=[whole((rows, cout)), w...]
    all_to_all x1 -> x0, waiting for transfers between devices: 5.3 us -> none  [exchange(): return lax.all_to_all(pieces, axis, 0, 0, tiled=True)]
    all_to_all x1 -> x0, starting transfers between devices: 3.92 us -> none  [exchange(): return lax.all_to_all(pieces, axis, 0, 0, tiled=True)]
    ppermute x2, waiting for transfers between devices: 4.87 us -> 3.1 us  [swap(): return lax.ppermute(value, 'c', [(0, 1), (1, 0)])]
  transfers between devices with their start and end apart: 3 -> 2, of which waited for: 3 -> 2; matrix products, arithmetic and copies ran while one was open for 0% -> 0% of each run, Pallas kernels for 2% -> 1%
where the time goes in v4:
time: 160 us
  blocking collectives  139 us (87%)
  starting transfers between devices  7.67 us (5%)
  Pallas kernels  7.62 us (5%)
  waiting for transfers between devices  3.1 us (2%)
    all_to_all x6, blocking collectives, exchange(): return lax.all_to_all(pieces, axis, 0, 0, tiled=True)  134 us
    ppermute x2, starting transfers between devices, swap(): return lax.ppermute(value, 'c', [(0, 1), (1, 0)])  7.67 us
    all_gather x1, blocking collectives, local(): square = lax.all_gather(square, 'c')  5.21 us
  transfers between devices with their start and end apart: 2, of which 2 were waited for; matrix products, arithmetic and copies ran while one was open for 0% of the time, Pallas kernels for 1%

profile of v4, /device:TPU:1, one launch (start us, length us, event | category | flops | bytes accessed | tf_op | source)
XLA Modules:
  0.0 160.0 jit_solution(5445643212057122778)
XLA Ops:
  0.6 0.0 copy-start
  0.6 1.1 broadcast_in_dim.4
  1.7 0.0 copy-start.2
  1.7 33.5 %all_to_all.30.own = bf16[8,32,2048]{2,1,0:T(8,128)(2,1)S(1)} all-to-all(bf16[8,32,2048]{2,1,0:T(8,128)(2,1)S(1)} %broadcast_in_dim.4), channel_id=1, replica_groups=mesh['z'=8,'x'=4,'y'=8,'c'=2] {'y'}, dimensions={0} | all-to-all | bytes 2097152 | tf_op jit(solution)/shard_map/all_to_all | solution.py:26
  35.3 0.0 copy-start.1
  35.3 5.8 %collective-permute-start = (bf16[8,32,2048]{2,1,0:T(8,128)(2,1)S(1)}, bf16[8,32,2048]{2,1,0:T(8,128)(2,1)S(1)}, u32[]{:S(2)}, u32[]{:S(2)}) collective-permute-start(bf16[8,32,2048]{2,1,0:T(8,128)(2,1)S(1)} %all_to_all.30.own), channel_id=1, source_target_pairs={{0,1},{1,0},{2,3},{3,2},{4,5},{5,4},{6,7},{7,6},{8,9},{9,8},{10,11... | collective-permute-start | bytes 3145736 | tf_op jit(solution)/shard_map/ppermute | solution.py:22
  41.0 2.3 %collective-permute-done.other = bf16[8,32,2048]{2,1,0:T(8,128)(2,1)S(1)} collective-permute-done((bf16[8,32,2048]{2,1,0:T(8,128)(2,1)S(1)}, bf16[8,32,2048]{2,1,0:T(8,128)(2,1)S(1)}, u32[]{:S(2)}, u32[]{:S(2)}) %collective-permute-start) | collective-permute-done | bytes 1048608 | tf_op jit(solution)/shard_map/ppermute | solution.py:22
  43.3 0.0 copy-done
  43.3 1.5 moments.1
  44.8 14.6 %all_to_all.31.moments = f32[16,32,128]{2,1,0:T(8,128)S(1)} all-to-all(f32[16,32,128]{2,1,0:T(8,128)S(1)} %get-tuple-element.21), channel_id=1, replica_groups=mesh['z'=8,'x'=4,'y'=8,'c'=2] {'y','c'}, dimensions={0} | all-to-all | bytes 524288 | tf_op jit(solution)/shard_map/all_to_all | solution.py:26
  59.5 0.0 copy-done.2
  59.5 0.0 copy-done.1
  59.5 0.0 copy-done.5
  59.5 0.0 copy-done.6
  59.5 1.4 stats.1
  60.9 14.3 %all_to_all.32.stats = f32[16,32,128]{2,1,0:T(8,128)S(1)} all-to-all(f32[16,32,128]{2,1,0:T(8,128)S(1)} %get-tuple-element.22), channel_id=1, replica_groups=mesh['z'=8,'x'=4,'y'=8,'c'=2] {'y','c'}, dimensions={0} | all-to-all | bytes 524288 | tf_op jit(solution)/shard_map/all_to_all | solution.py:26
  75.2 1.8 %weight_partial.1 = (bf16[392,2048]{1,0:T(8,128)(2,1)S(1)}, bf16[8,4,128,128]{3,2,1,0:T(8,128)(2,1)S(1)}, bf16[8,4,128,128]{3,2,1,0:T(8,128)(2,1)S(1)}, bf16[8,4,16,128]{3,2,1,0:T(8,128)(2,1)S(1)}) custom-call(f32[392,2048]{1,0:T(8,128)S(1)} %get-tuple-element.20.conv, f32[16,32,128]{2,1,0:T(8,128)S(1)} %all_to_all.31.moments, ...), custom_call_target="tpu_custom_call" | custom-call | tf_op jit(solution)/shard_map/weight_partial/pallas_call | solution.py:231
  77.0 1.9 %collective-permute-start.1 = (bf16[8,4,128,128]{3,2,1,0:T(8,128)(2,1)S(1)}, bf16[8,4,128,128]{3,2,1,0:T(8,128)(2,1)S(1)}, u32[]{:S(2)}, u32[]{:S(2)}) collective-permute-start(bf16[8,4,128,128]{3,2,1,0:T(8,128)(2,1)S(1)} %get-tuple-element.24), channel_id=1, source_target_pairs={{0,1},{1,0},{2,3},{3,2},{4,5},{5,4},{6,7},{7,6},{8,9},{9,8},{10,11... | collective-permute-start | bytes 3145736 | tf_op jit(solution)/shard_map/ppermute | solution.py:22
  79.0 1.8 %act_grad.1 = (bf16[392,512]{1,0:T(8,128)(2,1)}, f32[8,128]{1,0:T(8,128)S(1)}) custom-call(bf16[392,2048]{1,0:T(8,128)(2,1)S(1)} %get-tuple-element.25.grad_conv, bf16[512,2048]{1,0:T(8,128)(2,1)S(1)} %get-tuple-element.26.weight), custom_call_target="tpu_custom_call" | custom-call | flops 822083584 | bytes 3702784 | tf_op jit(solution)/shard_map/act_grad/pallas_call | solution.py:257
  80.8 0.8 collective-permute-done.1
  81.6 0.5 add_convert_fusion
  82.0 0.1 pad_maximum_fusion
  82.2 45.1 %all_to_all.33 = bf16[32,144,128]{2,1,0:T(8,128)(2,1)S(1)} all-to-all(bf16[32,144,128]{2,1,0:T(8,128)(2,1)S(1)} %bitcast.11), channel_id=1, replica_groups=mesh['z'=8,'x'=4,'y'=8,'c'=2] {'z','x'}, dimensions={0} | all-to-all | bytes 2359296 | tf_op jit(solution)/shard_map/all_to_all | solution.py:26
  127.3 0.2 convert_reduce_fusion.summed
  127.5 12.6 %all_to_all.34.partial = bf16[8,128,128]{2,1,0:T(8,128)(2,1)S(1)} all-to-all(bf16[8,128,128]{2,1,0:T(8,128)(2,1)S(1)} %broadcast_in_dim.5), channel_id=1, replica_groups=mesh['z'=8,'x'=4,'y'=8,'c'=2] {'y'}, dimensions={0} | all-to-all | bytes 524288 | tf_op jit(solution)/shard_map/all_to_all | solution.py:26
  140.1 0.2 totals.1
  140.2 13.6 %all_to_all.35.parts = bf16[32,24,128]{2,1,0:T(8,128)(2,1)S(1)} all-to-all(bf16[32,24,128]{2,1,0:T(8,128)(2,1)S(1)} %totals.1), channel_id=1, replica_groups=mesh['z'=8,'x'=4,'y'=8,'c'=2] {'z','x'}, dimensions={0} | all-to-all | bytes 393216 | tf_op jit(solution)/shard_map/all_to_all | solution.py:26
  153.9 0.1 convert_reduce_fusion.1
  153.9 5.2 %all-gather.1 = f32[2,1,128]{2,1,0:T(1,128)S(1)} all-gather(f32[1,1,128]{2,1,0:T(1,128)S(1)} %bitcast.12), channel_id=2, replica_groups=mesh['z'=8,'x'=4,'y'=8,'c'=2] {'c'}, dimensions={0}, use_global_device_ids=true | all-gather | bytes 1536 | tf_op jit(solution)/shard_map/all_gather | solution.py:290
  159.1 0.0 copy-done.3
  159.1 0.0 copy-done.4
  159.1 0.9 step.1
  (6 shorter events, 0.0 us)
Async XLA Ops:
  0.6 42.7 %copy-start = (bf16[392,512]{1,0:T(8,128)(2,1)S(1)}, bf16[392,512]{1,0:T(8,128)(2,1)}, u32[]{:S(2)}) copy-start(bf16[392,512]{1,0:T(8,128)(2,1)} %acts.3) | copy-start | bytes 1204228
  1.7 57.8 %copy-start.2 = (bf16[392,2048]{1,0:T(8,128)(2,1)S(1)}, bf16[392,2048]{1,0:T(8,128)(2,1)}, u32[]{:S(2)}) copy-start(bf16[392,2048]{1,0:T(8,128)(2,1)} %out_grad.1) | copy-start | bytes 4816900
  35.3 24.2 %copy-start.1 = (bf16[392,2048]{1,0:T(8,128)(2,1)S(1)}, bf16[392,2048]{1,0:T(8,128)(2,1)}, u32[]{:S(2)}) copy-start(bf16[392,2048]{1,0:T(8,128)(2,1)} %block_input.1) | copy-start | bytes 4816900
  35.3 24.2 %copy-start.5 = (f32[2048]{0:T(1024)S(1)}, f32[2048]{0:T(1024)}, u32[]{:S(2)}) copy-start(f32[2048]{0:T(1024)} %param.10) | copy-start | bytes 24580
  35.3 24.2 %copy-start.6 = (f32[2048]{0:T(1024)S(1)}, f32[2048]{0:T(1024)}, u32[]{:S(2)}) copy-start(f32[2048]{0:T(1024)} %param.11) | copy-start | bytes 24580
  35.3 8.0 %collective-permute-start = (bf16[8,32,2048]{2,1,0:T(8,128)(2,1)S(1)}, bf16[8,32,2048]{2,1,0:T(8,128)(2,1)S(1)}, u32[]{:S(2)}, u32[]{:S(2)}) collective-permute-start(bf16[8,32,2048]{2,1,0:T(8,128)(2,1)S(1)} %all_to_all.30.own), channel_id=1, source_target_pairs={{0,1},{1,0},{2,3},{3,2},{4,5},{5,4},{6,7},{7,6},{8,9},{9,8},{10,11... | collective-permute-start | bytes 3145736 | tf_op jit(solution)/shard_map/ppermute | solution.py:22
  77.0 4.6 %collective-permute-start.1 = (bf16[8,4,128,128]{3,2,1,0:T(8,128)(2,1)S(1)}, bf16[8,4,128,128]{3,2,1,0:T(8,128)(2,1)S(1)}, u32[]{:S(2)}, u32[]{:S(2)}) collective-permute-start(bf16[8,4,128,128]{3,2,1,0:T(8,128)(2,1)S(1)} %get-tuple-element.24), channel_id=1, source_target_pairs={{0,1},{1,0},{2,3},{3,2},{4,5},{5,4},{6,7},{7,6},{8,9},{9,8},{10,11... | collective-permute-start | bytes 3145736 | tf_op jit(solution)/shard_map/ppermute | solution.py:22
  127.3 31.9 %copy-start.3 = (bf16[32,2048]{1,0:T(8,128)(2,1)S(1)}, bf16[32,2048]{1,0:T(8,128)(2,1)}, u32[]{:S(2)}) copy-start(bf16[32,2048]{1,0:T(8,128)(2,1)} %weight.1) | copy-start | bytes 393220
  127.3 31.9 %copy-start.4 = (f32[32,2048]{1,0:T(8,128)S(1)}, f32[32,2048]{1,0:T(8,128)}, u32[]{:S(2)}) copy-start(f32[32,2048]{1,0:T(8,128)} %velocity.1) | copy-start | bytes 786436

commit v5 on v4

--- a/solution.py
+++ b/solution.py
@@ -78,6 +78,7 @@
 
 def stats_kernel(conv, moments, gain, shift, block_input, out_grad, grad, stats):
     rows, cout = conv.shape
+    tiles = []
     for j, cols in enumerate(columns(cout)):
         mean, inv_std = pooled(moments[:, 8 * j : 8 * j + 8], rows)
         centered = conv[:, cols] - mean
@@ -87,8 +88,9 @@
         grad[:, cols] = value.astype(bf16)
         sum_grad = jnp.sum(value, axis=0, keepdims=True)
         sum_cross = jnp.sum(value * centered, axis=0, keepdims=True) * inv_std
-        tile = jnp.concatenate(fold(sum_grad) + fold(sum_cross), axis=0)
-        stats[:, 8 * j : 8 * j + 8] = jnp.broadcast_to(tile[None], (stats.shape[0], 8, lanes))
+        tiles += fold(sum_grad) + fold(sum_cross)
+    tile = jnp.concatenate(tiles, axis=0).astype(bf16)
+    stats[...] = jnp.broadcast_to(tile[None], stats.shape)
 
 
 def weight_kernel(
@@ -103,9 +105,10 @@
     halves = cout // nz // lanes
     per = chunk // lanes // halves
     acts_t[...] = acts[...].T
+    totals = jnp.sum(stats[...].astype(f32), axis=0)
     for j, cols in enumerate(columns(cout)):
         mean, inv_std = pooled(moments[:, 8 * j : 8 * j + 8], rows)
-        sums = jnp.sum(stats[:, 8 * j : 8 * j + 8], axis=0)
+        sums = totals[8 * j : 8 * j + 8]
         sum_grad, sum_cross = sums[:groups], sums[groups:]
         shift = unfold(sum_grad) / group_rows
         slope = inv_std * unfold(sum_cross) / group_rows
@@ -127,8 +130,8 @@
                     ]
                     out[j * per + k, x] = jnp.concatenate(rows_of, axis=0).astype(bf16)
                 rows_of = planes[x][k * halves : (k + 1) * halves]
-                rows_of = [rows_of, jnp.zeros((16 - halves, lanes), f32)]
-                tail[j * per + k, x] = jnp.concatenate(rows_of, axis=0).astype(bf16)
+                rows_of = [rows_of, jnp.zeros((8 - halves, lanes), f32)]
+                tail[j * per + k, x] = jnp.concatenate(rows_of, axis=0)
 
 
 def act_kernel(grad_conv, weight, act_grad, squares):
@@ -221,13 +224,13 @@
         + [whole((1, cout))] * 2
         + [whole((rows, cout))] * 2,
         out_specs=[whole((rows, cout)), whole(sums)],
-        out_shape=[shape((rows, cout), bf16), shape(sums, f32)],
+        out_shape=[shape((rows, cout), bf16), shape(sums, bf16)],
         compiler_params=params(),
         name="stats",
     )(conv, moments, gain, shift, block_input, out_grad)
     stats = exchange(stats, bn)
 
-    piece, extra = (nz, nx, length, lanes), (nz, nx, 16, lanes)
+    piece, extra = (nz, nx, length, lanes), (nz, nx, 8, lanes)
     grad_conv, mine, theirs, tail = pl.pallas_call(
         weight_kernel,
         grid=(1,),
@@ -244,7 +247,7 @@
             shape((rows, cout), bf16),
             shape(piece, bf16),
             shape(piece, bf16),
-            shape(extra, bf16),
+            shape(extra, f32),
         ],
         scratch_shapes=[
             pltpu.VMEM((cin, chunk), f32),
@@ -268,7 +271,7 @@
     )(grad_conv, weight)
     arrived, act_grad = lax.optimization_barrier((arrived, act_grad))
     pair = (mine.astype(f32) + arrived.astype(f32)).astype(bf16)
-    pair = jnp.concatenate([pair, tail], axis=2).reshape(nz * nx, length + 16, lanes)
+    pair = jnp.concatenate([pair, tail.astype(bf16)], axis=2).reshape(nz * nx, length + 8, lanes)
     received = exchange(pair, rep)
     summed = jnp.sum(received.astype(f32), axis=0)
     blocks = copies(summed[:length].astype(bf16), "y")
@@ -277,7 +280,7 @@
     ready = pl.pallas_call(
         total_kernel,
         grid=(1,),
-        in_specs=[whole((ny, length, lanes)), whole((length + 16, lanes))],
+        in_specs=[whole((ny, length, lanes)), whole((length + 8, lanes))],
         out_specs=whole((nz * nx, depth, lanes)),
         out_shape=shape((nz * nx, depth, lanes), bf16),
         scratch_shapes=[pltpu.VMEM((length, lanes), f32)],

time: 160 us -> 157 us (0.981)
  blocking collectives: 139 us -> 135 us
    all_to_all x6, blocking collectives: 134 us -> 130 us  [exchange(): return lax.all_to_all(pieces, axis, 0, 0, tiled=True)]
where the time goes in v5:
time: 157 us; the launch traced here: 156 us
  blocking collectives  135 us (86%)
  starting transfers between devices  7.67 us (5%)
  Pallas kernels  7.64 us (5%)
  waiting for transfers between devices  3.07 us (2%)
    all_to_all x6, blocking collectives, exchange(): return lax.all_to_all(pieces, axis, 0, 0, tiled=True)  130 us
    ppermute x2, starting transfers between devices, swap(): return lax.ppermute(value, 'c', [(0, 1), (1, 0)])  7.67 us
    all_gather x1, blocking collectives, local(): square = lax.all_gather(square, 'c')  5.21 us
  transfers between devices with their start and end apart: 2, of which 2 were waited for; matrix products, arithmetic and copies ran while one was open for 0% of the time, Pallas kernels for 1%

profile of v5, /device:TPU:1, one launch (start us, length us, event | category | flops | bytes accessed | tf_op | source)
XLA Modules:
  0.0 156.2 jit_solution(18006297525830376989)
XLA Ops:
  0.6 0.0 copy-start.2
  0.6 1.1 broadcast_in_dim.4
  1.7 0.0 copy-start.1
  1.7 33.5 %all_to_all.30.own = bf16[8,32,2048]{2,1,0:T(8,128)(2,1)S(1)} all-to-all(bf16[8,32,2048]{2,1,0:T(8,128)(2,1)S(1)} %broadcast_in_dim.4), channel_id=1, replica_groups=mesh['z'=8,'x'=4,'y'=8,'c'=2] {'y'}, dimensions={0} | all-to-all | bytes 2097152 | tf_op jit(solution)/shard_map/all_to_all | solution.py:26
  35.3 0.0 copy-start
  35.3 5.8 %collective-permute-start = (bf16[8,32,2048]{2,1,0:T(8,128)(2,1)S(1)}, bf16[8,32,2048]{2,1,0:T(8,128)(2,1)S(1)}, u32[]{:S(2)}, u32[]{:S(2)}) collective-permute-start(bf16[8,32,2048]{2,1,0:T(8,128)(2,1)S(1)} %all_to_all.30.own), channel_id=1, source_target_pairs={{0,1},{1,0},{2,3},{3,2},{4,5},{5,4},{6,7},{7,6},{8,9},{9,8},{10,11... | collective-permute-start | bytes 3145736 | tf_op jit(solution)/shard_map/ppermute | solution.py:22
  41.0 2.3 %collective-permute-done.other = bf16[8,32,2048]{2,1,0:T(8,128)(2,1)S(1)} collective-permute-done((bf16[8,32,2048]{2,1,0:T(8,128)(2,1)S(1)}, bf16[8,32,2048]{2,1,0:T(8,128)(2,1)S(1)}, u32[]{:S(2)}, u32[]{:S(2)}) %collective-permute-start) | collective-permute-done | bytes 1048608 | tf_op jit(solution)/shard_map/ppermute | solution.py:22
  43.3 0.0 copy-done.2
  43.3 1.5 moments.1
  44.8 14.6 %all_to_all.31.moments = f32[16,32,128]{2,1,0:T(8,128)S(1)} all-to-all(f32[16,32,128]{2,1,0:T(8,128)S(1)} %get-tuple-element.21), channel_id=1, replica_groups=mesh['z'=8,'x'=4,'y'=8,'c'=2] {'y','c'}, dimensions={0} | all-to-all | bytes 524288 | tf_op jit(solution)/shard_map/all_to_all | solution.py:26
  59.5 0.0 copy-done.1
  59.5 0.0 copy-done
  59.5 0.0 copy-done.5
  59.5 0.0 copy-done.6
  59.5 1.4 stats.1
  60.9 11.7 %all_to_all.32.stats = bf16[16,32,128]{2,1,0:T(8,128)(2,1)S(1)} all-to-all(bf16[16,32,128]{2,1,0:T(8,128)(2,1)S(1)} %get-tuple-element.22), channel_id=1, replica_groups=mesh['z'=8,'x'=4,'y'=8,'c'=2] {'y','c'}, dimensions={0} | all-to-all | bytes 262144 | tf_op jit(solution)/shard_map/all_to_all | solution.py:26
  72.6 1.8 %weight_partial.1 = (bf16[392,2048]{1,0:T(8,128)(2,1)S(1)}, bf16[8,4,128,128]{3,2,1,0:T(8,128)(2,1)S(1)}, bf16[8,4,128,128]{3,2,1,0:T(8,128)(2,1)S(1)}, f32[8,4,8,128]{3,2,1,0:T(8,128)S(1)}) custom-call(f32[392,2048]{1,0:T(8,128)S(1)} %get-tuple-element.20.conv, f32[16,32,128]{2,1,0:T(8,128)S(1)} %all_to_all.31.moments, ...), custom_call_target="tpu_custom_call" | custom-call | tf_op jit(solution)/shard_map/weight_partial/pallas_call | solution.py:234
  74.5 1.9 %collective-permute-start.1 = (bf16[8,4,128,128]{3,2,1,0:T(8,128)(2,1)S(1)}, bf16[8,4,128,128]{3,2,1,0:T(8,128)(2,1)S(1)}, u32[]{:S(2)}, u32[]{:S(2)}) collective-permute-start(bf16[8,4,128,128]{3,2,1,0:T(8,128)(2,1)S(1)} %get-tuple-element.24), channel_id=1, source_target_pairs={{0,1},{1,0},{2,3},{3,2},{4,5},{5,4},{6,7},{7,6},{8,9},{9,8},{10,11... | collective-permute-start | bytes 3145736 | tf_op jit(solution)/shard_map/ppermute | solution.py:22
  76.4 1.8 %act_grad.1 = (bf16[392,512]{1,0:T(8,128)(2,1)}, f32[8,128]{1,0:T(8,128)S(1)}) custom-call(bf16[392,2048]{1,0:T(8,128)(2,1)S(1)} %get-tuple-element.25.grad_conv, bf16[512,2048]{1,0:T(8,128)(2,1)S(1)} %get-tuple-element.26.weight), custom_call_target="tpu_custom_call" | custom-call | flops 822083584 | bytes 3702784 | tf_op jit(solution)/shard_map/act_grad/pallas_call | solution.py:260
  78.2 0.8 collective-permute-done.1
  79.1 0.4 add_convert_fusion
  79.4 0.1 pad_maximum_fusion
  79.5 44.0 %all_to_all.33 = bf16[32,136,128]{2,1,0:T(8,128)(2,1)S(1)} all-to-all(bf16[32,136,128]{2,1,0:T(8,128)(2,1)S(1)} %bitcast.11), channel_id=1, replica_groups=mesh['z'=8,'x'=4,'y'=8,'c'=2] {'z','x'}, dimensions={0} | all-to-all | bytes 2228224 | tf_op jit(solution)/shard_map/all_to_all | solution.py:26
  123.5 0.2 convert_reduce_fusion.summed
  123.8 12.5 %all_to_all.34.partial = bf16[8,128,128]{2,1,0:T(8,128)(2,1)S(1)} all-to-all(bf16[8,128,128]{2,1,0:T(8,128)(2,1)S(1)} %broadcast_in_dim.5), channel_id=1, replica_groups=mesh['z'=8,'x'=4,'y'=8,'c'=2] {'y'}, dimensions={0} | all-to-all | bytes 524288 | tf_op jit(solution)/shard_map/all_to_all | solution.py:26
  136.2 0.2 totals.1
  136.4 13.6 %all_to_all.35.parts = bf16[32,24,128]{2,1,0:T(8,128)(2,1)S(1)} all-to-all(bf16[32,24,128]{2,1,0:T(8,128)(2,1)S(1)} %totals.1), channel_id=1, replica_groups=mesh['z'=8,'x'=4,'y'=8,'c'=2] {'z','x'}, dimensions={0} | all-to-all | bytes 393216 | tf_op jit(solution)/shard_map/all_to_all | solution.py:26
  150.0 0.1 convert_reduce_fusion.1
  150.0 5.2 %all-gather.1 = f32[2,1,128]{2,1,0:T(1,128)S(1)} all-gather(f32[1,1,128]{2,1,0:T(1,128)S(1)} %bitcast.12), channel_id=2, replica_groups=mesh['z'=8,'x'=4,'y'=8,'c'=2] {'c'}, dimensions={0}, use_global_device_ids=true | all-gather | bytes 1536 | tf_op jit(solution)/shard_map/all_gather | solution.py:293
  155.3 0.0 copy-done.3
  155.3 0.0 copy-done.4
  155.3 0.9 step.1
  (7 shorter events, 0.1 us)
Async XLA Ops:
  0.6 42.7 %copy-start.2 = (bf16[392,512]{1,0:T(8,128)(2,1)S(1)}, bf16[392,512]{1,0:T(8,128)(2,1)}, u32[]{:S(2)}) copy-start(bf16[392,512]{1,0:T(8,128)(2,1)} %acts.3) | copy-start | bytes 1204228
  1.7 57.8 %copy-start.1 = (bf16[392,2048]{1,0:T(8,128)(2,1)S(1)}, bf16[392,2048]{1,0:T(8,128)(2,1)}, u32[]{:S(2)}) copy-start(bf16[392,2048]{1,0:T(8,128)(2,1)} %out_grad.1) | copy-start | bytes 4816900
  35.3 24.2 %copy-start = (bf16[392,2048]{1,0:T(8,128)(2,1)S(1)}, bf16[392,2048]{1,0:T(8,128)(2,1)}, u32[]{:S(2)}) copy-start(bf16[392,2048]{1,0:T(8,128)(2,1)} %block_input.1) | copy-start | bytes 4816900
  35.3 24.2 %copy-start.5 = (f32[2048]{0:T(1024)S(1)}, f32[2048]{0:T(1024)}, u32[]{:S(2)}) copy-start(f32[2048]{0:T(1024)} %param.10) | copy-start | bytes 24580
  35.3 24.2 %copy-start.6 = (f32[2048]{0:T(1024)S(1)}, f32[2048]{0:T(1024)}, u32[]{:S(2)}) copy-start(f32[2048]{0:T(1024)} %param.11) | copy-start | bytes 24580
  35.3 8.0 %collective-permute-start = (bf16[8,32,2048]{2,1,0:T(8,128)(2,1)S(1)}, bf16[8,32,2048]{2,1,0:T(8,128)(2,1)S(1)}, u32[]{:S(2)}, u32[]{:S(2)}) collective-permute-start(bf16[8,32,2048]{2,1,0:T(8,128)(2,1)S(1)} %all_to_all.30.own), channel_id=1, source_target_pairs={{0,1},{1,0},{2,3},{3,2},{4,5},{5,4},{6,7},{7,6},{8,9},{9,8},{10,11... | collective-permute-start | bytes 3145736 | tf_op jit(solution)/shard_map/ppermute | solution.py:22
  74.5 4.6 %collective-permute-start.1 = (bf16[8,4,128,128]{3,2,1,0:T(8,128)(2,1)S(1)}, bf16[8,4,128,128]{3,2,1,0:T(8,128)(2,1)S(1)}, u32[]{:S(2)}, u32[]{:S(2)}) collective-permute-start(bf16[8,4,128,128]{3,2,1,0:T(8,128)(2,1)S(1)} %get-tuple-element.24), channel_id=1, source_target_pairs={{0,1},{1,0},{2,3},{3,2},{4,5},{5,4},{6,7},{7,6},{8,9},{9,8},{10,11... | collective-permute-start | bytes 3145736 | tf_op jit(solution)/shard_map/ppermute | solution.py:22
  123.5 31.7 %copy-start.3 = (bf16[32,2048]{1,0:T(8,128)(2,1)S(1)}, bf16[32,2048]{1,0:T(8,128)(2,1)}, u32[]{:S(2)}) copy-start(bf16[32,2048]{1,0:T(8,128)(2,1)} %weight.1) | copy-start | bytes 393220
  123.5 31.7 %copy-start.4 = (f32[32,2048]{1,0:T(8,128)S(1)}, f32[32,2048]{1,0:T(8,128)}, u32[]{:S(2)}) copy-start(f32[32,2048]{1,0:T(8,128)} %velocity.1) | copy-start | bytes 786436

commit v6 on v5

--- a/solution.py
+++ b/solution.py
@@ -11,8 +11,11 @@
 weight_decay = 5e-05
 momentum = 0.9
 f32, bf16 = jnp.float32, jnp.bfloat16
-rep = ("z", "x")
-bn = ("y", "c")
+rep = ("zh", "zl", "x")
+y_axes = ("yh", "yl")
+bn = ("yh", "yl", "c")
+near = ("zl", "x", "yl")
+far = ("zh", "yh")
 lanes = 128
 chunk = 512
 groups = chunk // lanes
@@ -94,18 +97,16 @@
 
 
 def weight_kernel(
-    conv, moments, stats, gain, grad, acts, grad_conv, mine, theirs, tail, wide, acts_t
+    sizes, conv, moments, stats, gain, grad, acts, grad_conv, mine, theirs, tail, wide, acts_t
 ):
+    nzl, nx, nyl, nyh = sizes
     core = lax.axis_index("c")
     rows, cout = conv.shape
     group_rows = rows * moments.shape[0]
-    nz, nx, length, _ = mine.shape
     part = 8 * nx
-    ny = wide.shape[0] // (2 * part)
-    halves = cout // nz // lanes
-    per = chunk // lanes // halves
     acts_t[...] = acts[...].T
     totals = jnp.sum(stats[...].astype(f32), axis=0)
+    per = cout // nzl // chunk
     for j, cols in enumerate(columns(cout)):
         mean, inv_std = pooled(moments[:, 8 * j : 8 * j + 8], rows)
         sums = totals[8 * j : 8 * j + 8]
@@ -117,21 +118,23 @@
         grad_conv[:, cols] = narrow
         wide[...] = jnp.dot(acts_t[...], narrow, preferred_element_type=f32)
         planes = (*high_low(sum_grad), *high_low(sum_cross))
-        for k in range(per):
-            for x in range(nx):
+        zl, k = j // per, j % per
+        length = groups * nyh * 8
+        for x in range(nx):
+            for yl in range(nyl):
+                piece = (zl * nx + x) * nyl + yl
                 for out, owner in ((mine, core), (theirs, 1 - core)):
                     rows_of = [
                         wide[
-                            pl.ds(pl.multiple_of((2 * y + owner) * part + 8 * x, 8), 8),
-                            pl.ds((k * halves + h) * lanes, lanes),
+                            pl.ds(pl.multiple_of((2 * (yh * nyl + yl) + owner) * part + 8 * x, 8), 8),
+                            pl.ds(q * lanes, lanes),
                         ]
-                        for h in range(halves)
-                        for y in range(ny)
+                        for q in range(groups)
+                        for yh in range(nyh)
                     ]
-                    out[j * per + k, x] = jnp.concatenate(rows_of, axis=0).astype(bf16)
-                rows_of = planes[x][k * halves : (k + 1) * halves]
-                rows_of = [rows_of, jnp.zeros((8 - halves, lanes), f32)]
-                tail[j * per + k, x] = jnp.concatenate(rows_of, axis=0)
+                    rows_of = jnp.concatenate(rows_of, axis=0).astype(bf16)
+                    out[piece, k * length : (k + 1) * length] = rows_of
+                tail[piece, k * groups : (k + 1) * groups] = planes[x] / (nyl * nyh)
 
 
 def act_kernel(grad_conv, weight, act_grad, squares):
@@ -145,26 +148,40 @@
     squares[...] = total
 
 
-def total_kernel(partial, summed, out, total):
-    ny, length, _ = partial.shape
-    halves = length // (8 * ny)
-    total[...] = jnp.sum(partial[...].astype(f32), axis=0)
-    value = total[...]
+def near_kernel(nyh, received, out, total):
+    count, depth, _ = out.shape
+    nzh = count // nyh
+    total[...] = jnp.sum(received[...].astype(f32), axis=0)
+    halves = (total.shape[0] - 8) // (nzh * nyh * 8)
+    base = nzh * halves * nyh * 8
+    for zh in range(nzh):
+        high, low = high_low(total[base + zh * halves : base + (zh + 1) * halves, :])
+        extra = jnp.concatenate([high, low, jnp.zeros((8 - 2 * halves, lanes), f32)], axis=0)
+        for yh in range(nyh):
+            starts = [((zh * halves + h) * nyh + yh) * 8 for h in range(halves)]
+            own = [total[at : at + 8, :] for at in starts]
+            out[zh * nyh + yh] = jnp.concatenate([*own, extra], axis=0).astype(bf16)
+
+
+def far_kernel(halves, received, out):
+    total = jnp.sum(received[...].astype(f32), axis=0)
+    at = 8 * halves
+    value = total[:at]
     square = jnp.sum(jnp.sum(value * value, axis=0, keepdims=True), axis=1, keepdims=True)
     square = jnp.broadcast_to(square, (1, lanes))
-    y = lax.axis_index("y")
-    own = [total[pl.ds(pl.multiple_of((h * ny + y) * 8, 8), 8), :] for h in range(halves)]
-    extra = [*high_low(summed[length : length + halves, :]), *high_low(square)]
+    tail = total[at : at + halves] + total[at + halves : at + 2 * halves]
+    extra = [*high_low(tail), *high_low(square)]
     used = sum(e.shape[0] for e in extra)
     extra.append(jnp.zeros((8 - used, lanes), f32))
-    tile = jnp.concatenate(own + extra, axis=0).astype(bf16)
+    tile = jnp.concatenate([value, *extra], axis=0).astype(bf16)
     out[...] = jnp.broadcast_to(tile[None], out.shape)
 
 
-def step_kernel(nx, parts, squares, weight_squares, weight, velocity, out, gain, shift):
+def step_kernel(nzl, nx, parts, squares, weight_squares, weight, velocity, out, gain, shift):
     nz = parts.shape[0] // nx
+    nzh = nz // nzl
     halves = out.shape[1] // nz // lanes
-    grad_square = jnp.sum(squares[...], axis=0, keepdims=True)[:, :1]
+    grad_square = jnp.sum(squares[...], axis=0)[:1, :1]
     weight_square = jnp.sum(weight_squares[...], axis=0, keepdims=True)
     weight_square = jnp.sum(weight_square, axis=1, keepdims=True)
     weight_norm = jnp.sqrt(weight_square)
@@ -173,7 +190,7 @@
     for z in range(nz):
         values = [parts[z * nx + x].astype(f32) for x in range(nx)]
         for h in range(halves):
-            cols = pl.ds((z * halves + h) * lanes, lanes)
+            cols = pl.ds(((z % nzl * nzh + z // nzl) * halves + h) * lanes, lanes)
             weight_grad = jnp.concatenate([v[8 * h : 8 * h + 8] for v in values], axis=0)
             decayed = weight_grad + weight_decay * weight[:, cols].astype(f32)
             out[:, cols] = momentum * velocity[:, cols] + ratio * decayed
@@ -197,13 +214,16 @@
 def local(block_input, activations, conv_weight, bn_gain, bn_shift, out_grad, velocity):
     rows, cin = activations.shape
     part, cout = conv_weight.shape
-    nz, nx, ny = lax.axis_size("z"), lax.axis_size("x"), lax.axis_size("y")
+    nzh, nzl, nx = (lax.axis_size(a) for a in rep)
+    nyh, nyl = (lax.axis_size(a) for a in y_axes)
+    nz, ny = nzh * nzl, nyh * nyl
     members = lax.axis_size(bn)
     gain, shift = bn_gain.reshape(1, cout), bn_shift.reshape(1, cout)
     halves = cout // nz // lanes
-    length = halves * ny * 8
-
-    own = copies(conv_weight, "y").reshape(ny, part, cout)
+    length = nzh * halves * nyh * 8
+    depth = halves * 8 + 8
+
+    own = copies(conv_weight, y_axes).reshape(ny, part, cout)
     other = swap(own)
     sums = (members, 2 * cout // lanes, lanes)
     weight, conv, moments = pl.pallas_call(
@@ -230,9 +250,10 @@
     )(conv, moments, gain, shift, block_input, out_grad)
     stats = exchange(stats, bn)
 
-    piece, extra = (nz, nx, length, lanes), (nz, nx, 8, lanes)
+    pieces = nzl * nx * nyl
+    piece, extra = (pieces, length, lanes), (pieces, 8, lanes)
     grad_conv, mine, theirs, tail = pl.pallas_call(
-        weight_kernel,
+        functools.partial(weight_kernel, (nzl, nx, nyl, nyh)),
         grid=(1,),
         in_specs=[
             whole((rows, cout)),
@@ -271,32 +292,38 @@
     )(grad_conv, weight)
     arrived, act_grad = lax.optimization_barrier((arrived, act_grad))
     pair = (mine.astype(f32) + arrived.astype(f32)).astype(bf16)
-    pair = jnp.concatenate([pair, tail.astype(bf16)], axis=2).reshape(nz * nx, length + 8, lanes)
-    received = exchange(pair, rep)
-    summed = jnp.sum(received.astype(f32), axis=0)
-    blocks = copies(summed[:length].astype(bf16), "y")
-    blocks = blocks.reshape(ny, length, lanes)
-    depth = halves * 8 + 8
+    pair = jnp.concatenate([pair, tail.astype(bf16)], axis=1)
+    received = exchange(pair, near)
+    partial = pl.pallas_call(
+        functools.partial(near_kernel, nyh),
+        grid=(1,),
+        in_specs=[whole((pieces, length + 8, lanes))],
+        out_specs=whole((nzh * nyh, depth, lanes)),
+        out_shape=shape((nzh * nyh, depth, lanes), bf16),
+        scratch_shapes=[pltpu.VMEM((length + 8, lanes), f32)],
+        compiler_params=params(),
+        name="near_sum",
+    )(received)
+    partial = exchange(partial, far)
     ready = pl.pallas_call(
-        total_kernel,
-        grid=(1,),
-        in_specs=[whole((ny, length, lanes)), whole((length + 8, lanes))],
+        functools.partial(far_kernel, halves),
+        grid=(1,),
+        in_specs=[whole((nzh * nyh, depth, lanes))],
         out_specs=whole((nz * nx, depth, lanes)),
         out_shape=shape((nz * nx, depth, lanes), bf16),
-        scratch_shapes=[pltpu.VMEM((length, lanes), f32)],
-        compiler_params=params(),
-        name="totals",
-    )(blocks, summed)
+        compiler_params=params(),
+        name="far_sum",
+    )(partial)
     ready = exchange(ready, rep)
     at = halves * 8 + 2 * halves
     square = jnp.sum(ready[:, at : at + 2].astype(f32), axis=(0, 1))
-    square = lax.all_gather(square, "c")
+    square = exchange(jnp.broadcast_to(square, (members, 8, lanes)), bn)
     new_velocity, gain_grad, shift_grad = pl.pallas_call(
-        functools.partial(step_kernel, nx),
+        functools.partial(step_kernel, nzl, nx),
         grid=(1,),
         in_specs=[
             whole((nz * nx, depth, lanes)),
-            whole((2, lanes)),
+            whole((members, 8, lanes)),
             whole((8, lanes)),
             whole((part, cout)),
             whole((part, cout)),
@@ -309,9 +336,9 @@
     return (act_grad, gain_grad.reshape(cout), shift_grad.reshape(cout), new_velocity)
 
 
-def solution(mesh, dims=(8, 4, 8, 2)):
-    fine = Mesh(mesh.devices.reshape(dims), ("z", "x", "y", "c"))
-    every = P(("z", "x", "y", "c"), None)
+def solution(mesh, dims=(4, 2, 4, 4, 2, 2)):
+    fine = Mesh(mesh.devices.reshape(dims), rep + bn)
+    every = P(rep + bn, None)
     return jax.shard_map(
         local,
         mesh=fine,

time: 157 us -> 153 us (0.975)
  blocking collectives: 135 us -> 132 us
    all_gather x1 -> x0, blocking collectives: 5.21 us -> none  [local(): square = lax.all_gather(square, 'c')]
    all_to_all x6 -> x7, blocking collectives: 130 us -> 132 us  [exchange(): return lax.all_to_all(pieces, axis, 0, 0, tiled=True)]
where the time goes in v6:
time: 153 us; the launch traced here: 152 us
  blocking collectives  132 us (86%)
  Pallas kernels  7.76 us (5%)
  starting transfers between devices  7.67 us (5%)
  waiting for transfers between devices  3.08 us (2%)
    all_to_all x7, blocking collectives, exchange(): return lax.all_to_all(pieces, axis, 0, 0, tiled=True)  132 us
    ppermute x2, starting transfers between devices, swap(): return lax.ppermute(value, 'c', [(0, 1), (1, 0)])  7.67 us
    ppermute x2, waiting for transfers between devices, swap(): return lax.ppermute(value, 'c', [(0, 1), (1, 0)])  3.08 us
  transfers between devices with their start and end apart: 2, of which 2 were waited for; matrix products, arithmetic and copies ran while one was open for 0% of the time, Pallas kernels for 1%

profile of v6, /device:TPU:1, one launch (start us, length us, event | category | flops | bytes accessed | tf_op | source)
XLA Modules:
  0.0 152.4 jit_solution(8292151791787427394)
XLA Ops:
  0.6 0.0 copy-start.2
  0.6 1.1 broadcast_in_dim.4
  1.7 0.0 copy-start.1
  1.7 33.5 %all_to_all.35.own = bf16[8,32,2048]{2,1,0:T(8,128)(2,1)S(1)} all-to-all(bf16[8,32,2048]{2,1,0:T(8,128)(2,1)S(1)} %broadcast_in_dim.4), channel_id=1, replica_groups=mesh['zh'=4,'zl'=2,'x'=4,'yh'=4,'yl'=2,'c'=2] {'yh','yl'}, dimensions={0} | all-to-all | bytes 2097152 | tf_op jit(solution)/shard_map/all_to_all | solution.py:29
  35.3 0.0 copy-start
  35.3 5.8 %collective-permute-start = (bf16[8,32,2048]{2,1,0:T(8,128)(2,1)S(1)}, bf16[8,32,2048]{2,1,0:T(8,128)(2,1)S(1)}, u32[]{:S(2)}, u32[]{:S(2)}) collective-permute-start(bf16[8,32,2048]{2,1,0:T(8,128)(2,1)S(1)} %all_to_all.35.own), channel_id=1, source_target_pairs={{0,1},{1,0},{2,3},{3,2},{4,5},{5,4},{6,7},{7,6},{8,9},{9,8},{10,11... | collective-permute-start | bytes 3145736 | tf_op jit(solution)/shard_map/ppermute | solution.py:25
  41.0 2.3 %collective-permute-done.other = bf16[8,32,2048]{2,1,0:T(8,128)(2,1)S(1)} collective-permute-done((bf16[8,32,2048]{2,1,0:T(8,128)(2,1)S(1)}, bf16[8,32,2048]{2,1,0:T(8,128)(2,1)S(1)}, u32[]{:S(2)}, u32[]{:S(2)}) %collective-permute-start) | collective-permute-done | bytes 1048608 | tf_op jit(solution)/shard_map/ppermute | solution.py:25
  43.3 0.0 copy-done.2
  43.3 1.5 moments.1
  44.8 14.6 %all_to_all.36.moments = f32[16,32,128]{2,1,0:T(8,128)S(1)} all-to-all(f32[16,32,128]{2,1,0:T(8,128)S(1)} %get-tuple-element.21), channel_id=1, replica_groups=mesh['zh'=4,'zl'=2,'x'=4,'yh'=4,'yl'=2,'c'=2] {'yh','yl','c'}, dimensions={0} | all-to-all | bytes 524288 | tf_op jit(solution)/shard_map/all_to_all | solution.py:29
  59.5 0.0 copy-done.1
  59.5 0.0 copy-done
  59.5 0.0 copy-done.5
  59.5 0.0 copy-done.6
  59.5 1.4 stats.1
  60.9 11.7 %all_to_all.37.stats = bf16[16,32,128]{2,1,0:T(8,128)(2,1)S(1)} all-to-all(bf16[16,32,128]{2,1,0:T(8,128)(2,1)S(1)} %get-tuple-element.22), channel_id=1, replica_groups=mesh['zh'=4,'zl'=2,'x'=4,'yh'=4,'yl'=2,'c'=2] {'yh','yl','c'}, dimensions={0} | all-to-all | bytes 262144 | tf_op jit(solution)/shard_map/all_to_all | solution.py:29
  72.6 1.8 %weight_partial.1 = (bf16[392,2048]{1,0:T(8,128)(2,1)S(1)}, bf16[16,256,128]{2,1,0:T(8,128)(2,1)S(1)}, bf16[16,256,128]{2,1,0:T(8,128)(2,1)S(1)}, f32[16,8,128]{2,1,0:T(8,128)S(1)}) custom-call(f32[392,2048]{1,0:T(8,128)S(1)} %get-tuple-element.20.conv, f32[16,32,128]{2,1,0:T(8,128)S(1)} %all_to_all.36.moments, bf16[16,32,128]{2,1,0:T(8,128)(2,1)S(1)} %all_to_all.37.stats, ...), custom_call_target="tpu_custom_call" | custom-call | tf_op jit(solution)/shard_map/weight_partial/pallas_call | solution.py:255
  74.5 1.9 %collective-permute-start.1 = (bf16[16,256,128]{2,1,0:T(8,128)(2,1)S(1)}, bf16[16,256,128]{2,1,0:T(8,128)(2,1)S(1)}, u32[]{:S(2)}, u32[]{:S(2)}) collective-permute-start(bf16[16,256,128]{2,1,0:T(8,128)(2,1)S(1)} %get-tuple-element.24), channel_id=1, source_target_pairs={{0,1},{1,0},{2,3},{3,2},{4,5},{5,4},{6,7},{7,6},{8,9},{9,8},{10,11... | collective-permute-start | bytes 3145736 | tf_op jit(solution)/shard_map/ppermute | solution.py:25
  76.4 1.8 %act_grad.1 = (bf16[392,512]{1,0:T(8,128)(2,1)}, f32[8,128]{1,0:T(8,128)S(1)}) custom-call(bf16[392,2048]{1,0:T(8,128)(2,1)S(1)} %get-tuple-element.25.grad_conv, bf16[512,2048]{1,0:T(8,128)(2,1)S(1)} %get-tuple-element.26.weight), custom_call_target="tpu_custom_call" | custom-call | flops 822083584 | bytes 3702784 | tf_op jit(solution)/shard_map/act_grad/pallas_call | solution.py:281
  78.2 0.8 collective-permute-done.1
  79.0 0.3 add_convert_fusion
  79.3 0.1 pad_maximum_fusion
  79.4 22.1 %all_to_all.38.received = bf16[16,264,128]{2,1,0:T(8,128)(2,1)S(1)} all-to-all(bf16[16,264,128]{2,1,0:T(8,128)(2,1)S(1)} %pad_maximum_fusion), channel_id=1, replica_groups=mesh['zh'=4,'zl'=2,'x'=4,'yh'=4,'yl'=2,'c'=2] {'zl','x','yl'}, dimensions={0} | all-to-all | bytes 2162688 | tf_op jit(solution)/shard_map/all_to_all | solution.py:29
  101.5 0.2 near_sum.1
  101.7 21.6 %all_to_all.39.received = bf16[16,24,128]{2,1,0:T(8,128)(2,1)S(1)} all-to-all(bf16[16,24,128]{2,1,0:T(8,128)(2,1)S(1)} %near_sum.1), channel_id=1, replica_groups=mesh['zh'=4,'zl'=2,'x'=4,'yh'=4,'yl'=2,'c'=2] {'zh','yh'}, dimensions={0} | all-to-all | bytes 196608 | tf_op jit(solution)/shard_map/all_to_all | solution.py:29
  123.3 0.1 far_sum.1
  123.4 13.4 %all_to_all.40.parts = bf16[32,24,128]{2,1,0:T(8,128)(2,1)S(1)} all-to-all(bf16[32,24,128]{2,1,0:T(8,128)(2,1)S(1)} %far_sum.1), channel_id=1, replica_groups=mesh['zh'=4,'zl'=2,'x'=4,'yh'=4,'yl'=2,'c'=2] {'zh','zl','x'}, dimensions={0} | all-to-all | bytes 393216 | tf_op jit(solution)/shard_map/all_to_all | solution.py:29
  136.8 0.1 convert_reduce_fusion
  136.9 14.6 %all_to_all.41.squares = f32[16,8,128]{2,1,0:T(8,128)S(1)} all-to-all(f32[16,8,128]{2,1,0:T(8,128)S(1)} %broadcast_in_dim.10), channel_id=1, replica_groups=mesh['zh'=4,'zl'=2,'x'=4,'yh'=4,'yl'=2,'c'=2] {'yh','yl','c'}, dimensions={0} | all-to-all | bytes 131072 | tf_op jit(solution)/shard_map/all_to_all | solution.py:29
  151.5 0.0 copy-done.3
  151.5 0.0 copy-done.4
  151.5 0.9 step.1
  (6 shorter events, 0.0 us)
Async XLA Ops:
  0.6 42.7 %copy-start.2 = (bf16[392,512]{1,0:T(8,128)(2,1)S(1)}, bf16[392,512]{1,0:T(8,128)(2,1)}, u32[]{:S(2)}) copy-start(bf16[392,512]{1,0:T(8,128)(2,1)} %acts.3) | copy-start | bytes 1204228
  1.7 57.8 %copy-start.1 = (bf16[392,2048]{1,0:T(8,128)(2,1)S(1)}, bf16[392,2048]{1,0:T(8,128)(2,1)}, u32[]{:S(2)}) copy-start(bf16[392,2048]{1,0:T(8,128)(2,1)} %out_grad.1) | copy-start | bytes 4816900
  35.3 24.2 %copy-start = (bf16[392,2048]{1,0:T(8,128)(2,1)S(1)}, bf16[392,2048]{1,0:T(8,128)(2,1)}, u32[]{:S(2)}) copy-start(bf16[392,2048]{1,0:T(8,128)(2,1)} %block_input.1) | copy-start | bytes 4816900
  35.3 24.2 %copy-start.5 = (f32[2048]{0:T(1024)S(1)}, f32[2048]{0:T(1024)}, u32[]{:S(2)}) copy-start(f32[2048]{0:T(1024)} %param.10) | copy-start | bytes 24580
  35.3 24.2 %copy-start.6 = (f32[2048]{0:T(1024)S(1)}, f32[2048]{0:T(1024)}, u32[]{:S(2)}) copy-start(f32[2048]{0:T(1024)} %param.11) | copy-start | bytes 24580
  35.3 8.0 %collective-permute-start = (bf16[8,32,2048]{2,1,0:T(8,128)(2,1)S(1)}, bf16[8,32,2048]{2,1,0:T(8,128)(2,1)S(1)}, u32[]{:S(2)}, u32[]{:S(2)}) collective-permute-start(bf16[8,32,2048]{2,1,0:T(8,128)(2,1)S(1)} %all_to_all.35.own), channel_id=1, source_target_pairs={{0,1},{1,0},{2,3},{3,2},{4,5},{5,4},{6,7},{7,6},{8,9},{9,8},{10,11... | collective-permute-start | bytes 3145736 | tf_op jit(solution)/shard_map/ppermute | solution.py:25
  74.5 4.6 %collective-permute-start.1 = (bf16[16,256,128]{2,1,0:T(8,128)(2,1)S(1)}, bf16[16,256,128]{2,1,0:T(8,128)(2,1)S(1)}, u32[]{:S(2)}, u32[]{:S(2)}) collective-permute-start(bf16[16,256,128]{2,1,0:T(8,128)(2,1)S(1)} %get-tuple-element.24), channel_id=1, source_target_pairs={{0,1},{1,0},{2,3},{3,2},{4,5},{5,4},{6,7},{7,6},{8,9},{9,8},{10,11... | collective-permute-start | bytes 3145736 | tf_op jit(solution)/shard_map/ppermute | solution.py:25
  101.5 50.0 %copy-start.3 = (bf16[32,2048]{1,0:T(8,128)(2,1)S(1)}, bf16[32,2048]{1,0:T(8,128)(2,1)}, u32[]{:S(2)}) copy-start(bf16[32,2048]{1,0:T(8,128)(2,1)} %weight.1) | copy-start | bytes 393220
  101.5 50.0 %copy-start.4 = (f32[32,2048]{1,0:T(8,128)S(1)}, f32[32,2048]{1,0:T(8,128)}, u32[]{:S(2)}) copy-start(f32[32,2048]{1,0:T(8,128)} %velocity.1) | copy-start | bytes 786436

commit v7 on v0

v7 whole, which is shorter than its diff:
```python
import functools

import jax
import jax.numpy as jnp
from jax import lax
from jax.experimental import pallas as pl
from jax.experimental.pallas import tpu as pltpu
from jax.sharding import Mesh, PartitionSpec as P

epsilon = 1e-05
weight_decay = 5e-05
momentum = 0.9
f32, bf16 = jnp.float32, jnp.bfloat16
rep = ("zh", "zl", "x")
y_axes = ("yh", "yl")
bn = ("yh", "yl", "c")
near = ("zl", "x", "yl")
far = ("zh", "yh")
lanes = 128
chunk = 512
groups = chunk // lanes


def swap(value):
    return lax.ppermute(value, "c", [(0, 1), (1, 0)])


def exchange(pieces, axis):
    return lax.all_to_all(pieces, axis, 0, 0, tiled=True)


def copies(value, axis):
    n = lax.axis_size(axis)
    return exchange(jnp.broadcast_to(value[None], (n, *value.shape)), axis)


def fold(row):
    return [row[:, q * lanes : (q + 1) * lanes] for q in range(groups)]


def unfold(tile):
    return jnp.concatenate([tile[q : q + 1] for q in range(groups)], axis=1)


def high_low(value):
    high = value.astype(bf16).astype(f32)
    return high, value - high


def columns(width):
    return [pl.ds(start, chunk) for start in range(0, width, chunk)]


def moments_kernel(acts, acts_other, weight, conv, conv_other, moments):
    count = 2 * conv.shape[0]
    for j, cols in enumerate(columns(conv.shape[1])):
        both = []
        for rows, out in ((acts, conv), (acts_other, conv_other)):
            value = jnp.dot(rows[...], weight[:, cols], preferred_element_type=f32)
            out[:, cols] = value
            both.append(value)
        mean = sum(jnp.sum(value, axis=0, keepdims=True) for value in both) / count
        square = sum(jnp.sum((v - mean) * (v - mean), axis=0, keepdims=True) for v in both)
        tile = jnp.concatenate(fold(mean) + fold(square), axis=0)
        moments[:, 8 * j : 8 * j + 8] = jnp.broadcast_to(tile[None], (moments.shape[0], 8, lanes))


def pooled(moments, rows):
    members = moments.shape[0]
    means, squares = moments[:, :groups], moments[:, groups:]
    mean = jnp.sum(means, axis=0) / members
    offset = means - mean[None]
    square = jnp.sum(squares, axis=0) + rows * jnp.sum(offset * offset, axis=0)
    inv_std = lax.rsqrt(square / (rows * members) + epsilon)
    return unfold(mean), unfold(inv_std)


def stats_kernel(
    conv, conv_other, moments, gain, shift, block, block_other, out, out_other, grad, grad_other, stats
):
    rows, half = conv.shape
    core = lax.axis_index("c")
    for j, cols in enumerate(columns(half)):
        place = pl.ds(pl.multiple_of(core * half + j * chunk, chunk), chunk)
        mean, inv_std = pooled(moments[:, 8 * j : 8 * j + 8], 2 * rows)
        scale, bias = gain[:, place] * inv_std, shift[:, place]
        sum_grad = sum_cross = 0.0
        for of, added, incoming, result in (
            (conv, block[:, place], out[:, place], grad),
            (conv_other, block_other[:, cols], out_other[:, cols], grad_other),
        ):
            centered = of[:, cols] - mean
            summed = centered * scale + bias + added.astype(f32)
            value = jnp.where(summed > 0.0, incoming.astype(f32), 0.0)
            result[:, cols] = value.astype(bf16)
            sum_grad += jnp.sum(value, axis=0, keepdims=True)
            sum_cross += jnp.sum(value * centered, axis=0, keepdims=True)
        tile = jnp.concatenate(fold(sum_grad) + fold(sum_cross * inv_std), axis=0)
        stats[:, 8 * j : 8 * j + 8] = jnp.broadcast_to(tile[None], (stats.shape[0], 8, lanes))


def weight_kernel(
    sizes,
    conv,
    conv_other,
    moments,
    stats,
    gain,
    grad,
    grad_other,
    acts,
    acts_other,
    grad_conv,
    grad_conv_other,
    out,
    wide,
    acts_t,
    acts_t_other,
):
    nx, nyl, nyh = sizes
    core = lax.axis_index("c")
    rows, half = conv.shape
    group_rows = 2 * rows * moments.shape[0]
    part = wide.shape[0] // (nyl * nyh)
    step = part // nx
    length = groups * nyh * step
    acts_t[...] = acts[...].T
    acts_t_other[...] = acts_other[...].T
    for j, cols in enumerate(columns(half)):
        place = pl.ds(pl.multiple_of(core * half + j * chunk, chunk), chunk)
        mean, inv_std = pooled(moments[:, 8 * j : 8 * j + 8], 2 * rows)
        sums = jnp.sum(stats[:, 8 * j : 8 * j + 8], axis=0)
        sum_grad, sum_cross = sums[:groups], sums[groups:]
        shift = unfold(sum_grad) / group_rows
        slope = inv_std * unfold(sum_cross) / group_rows
        scale = gain[:, place] * inv_std
        product = 0.0
        for of, pre, left, result in (
            (conv, grad, acts_t, grad_conv),
            (conv_other, grad_other, acts_t_other, grad_conv_other),
        ):
            value = pre[:, cols].astype(f32) - shift - (of[:, cols] - mean) * slope
            narrow = (scale * value).astype(bf16)
            result[:, cols] = narrow
            product += jnp.dot(left[...], narrow, preferred_element_type=f32)
        wide[...] = product
        planes = (*high_low(sum_grad), *high_low(sum_cross))
        for x in range(nx):
            last = jnp.concatenate(
                [planes[x] / (nyl * nyh), jnp.zeros((16 - groups, lanes), f32)], axis=0
            )
            for yl in range(nyl):
                piece = (j * nx + x) * nyl + yl
                rows_of = [
                    wide[
                        pl.ds((yh * nyl + yl) * part + step * x, step), pl.ds(q * lanes, lanes)
                    ]
                    for q in range(groups)
                    for yh in range(nyh)
                ]
                out[piece, :length] = jnp.concatenate(rows_of, axis=0).astype(bf16)
                out[piece, length:] = last.astype(bf16)


def act_kernel(grad_conv, grad_conv_other, weight, act, act_other, squares):
    dims = (((1,), (1,)), ((), ()))
    act[...] = lax.dot_general(grad_conv[...], weight[...], dims, preferred_element_type=f32)
    act_other[...] = lax.dot_general(
        grad_conv_other[...], weight[...], dims, preferred_element_type=f32
    ).astype(bf16)
    total = jnp.zeros((8, lanes), f32)
    for cols in columns(weight.shape[1]):
        wide = weight[:, cols].astype(f32)
        total += sum(fold(jnp.sum((wide * wide).reshape(-1, 8, chunk), axis=0)))
    squares[...] = total


def near_kernel(nyh, received, out, total):
    count, depth, _ = out.shape
    step = depth - 8
    total[...] = jnp.sum(received[...].astype(f32), axis=0)
    for zh in range(count // nyh):
        base = count * step + zh
        high, low = high_low(total[base : base + 1, :])
        extra = jnp.concatenate([high, low, jnp.zeros((6, lanes), f32)], axis=0)
        for yh in range(nyh):
            at = (zh * nyh + yh) * step
            tile = jnp.concatenate([total[at : at + step, :], extra], axis=0)
            out[zh * nyh + yh] = tile.astype(bf16)


def far_kernel(received, out):
    total = jnp.sum(received[...].astype(f32), axis=0)
    step = total.shape[0] - 8
    value = total[:step]
    square = jnp.sum(jnp.sum(value * value, axis=0, keepdims=True), axis=1, keepdims=True)
    square = jnp.broadcast_to(square, (1, lanes))
    tail = total[step : step + 1] + total[step + 1 : step + 2]
    tile = [value, *high_low(tail), *high_low(square), jnp.zeros((4, lanes), f32)]
    tile = jnp.concatenate(tile, axis=0).astype(bf16)
    out[...] = jnp.broadcast_to(tile[None], out.shape)


def places(sizes):
    nzh, nzl, nx = sizes
    return [
        ((zh * nzl + zl) * nx, pl.ds((zl * nzh + zh) * lanes, lanes))
        for zh in range(nzh)
        for zl in range(nzl)
    ]


def owned(parts, first, owner, count):
    values = [parts[first + owner * count + i].astype(f32) for i in range(count)]
    return jnp.concatenate([v[: v.shape[0] - 8] for v in values], axis=0)


def sums_of(parts, first, nx):
    planes = []
    for x in range(nx):
        value = parts[first + x].astype(f32)
        at = value.shape[0] - 8
        planes.append(value[at : at + 1] + value[at + 1 : at + 2])
    return planes[0] + planes[1], planes[2] + planes[3]


def split_kernel(sizes, parts, weight_squares, theirs, squares):
    nx = sizes[2]
    other = 1 - lax.axis_index("c")
    part = theirs.shape[0] - 8
    for first, cols in places(sizes):
        theirs[:part, cols] = owned(parts, first, other, nx // 2)
        shift, gain = sums_of(parts, first, nx)
        theirs[part:, cols] = jnp.concatenate([shift, gain, jnp.zeros((6, lanes), f32)], axis=0)
    total = jnp.sum(parts[...].astype(f32), axis=0)
    at = total.shape[0] - 6
    square = total[at : at + 1] + total[at + 1 : at + 2]
    weight_square = jnp.sum(weight_squares[...], axis=0, keepdims=True)
    weight_square = jnp.sum(weight_square, axis=1, keepdims=True)
    weight_square = jnp.broadcast_to(weight_square, (1, lanes))
    tile = jnp.concatenate([square, weight_square, jnp.zeros((6, lanes), f32)], axis=0)
    squares[...] = jnp.broadcast_to(tile[None], squares.shape)


def step_kernel(sizes, parts, arrived, squares, weight, velocity, out, gain, shift):
    nx = sizes[2]
    core = lax.axis_index("c")
    part, cout = out.shape
    half = cout // 2
    total = jnp.sum(squares[...], axis=0)
    grad_norm = jnp.sqrt(total[:1, :1])
    weight_norm = jnp.sqrt(total[1:2, :1] / (squares.shape[0] // 2))
    ratio = weight_norm / (grad_norm + weight_decay * weight_norm)

    def update(cols, weight_grad):
        decayed = weight_grad + weight_decay * weight[:, cols].astype(f32)
        out[:, cols] = momentum * velocity[:, cols] + ratio * decayed

    for first, cols in places(sizes):
        here = pl.ds(pl.multiple_of(core * half + cols.start, lanes), lanes)
        there = pl.ds(pl.multiple_of((1 - core) * half + cols.start, lanes), lanes)
        update(here, owned(parts, first, core, nx // 2))
        update(there, arrived[:part, cols])
        shift[:, here], gain[:, here] = sums_of(parts, first, nx)
        last = arrived[part:, cols]
        shift[:, there], gain[:, there] = last[:1], last[1:2]


def shape(dims, dtype):
    return jax.ShapeDtypeStruct(dims, dtype)


def whole(dims):
    return pl.BlockSpec(dims, lambda j: (0,) * len(dims))


def params(mib=24):
    return pltpu.CompilerParams(vmem_limit_bytes=mib << 20)


def call(kernel, name, operands, outs, scratch=()):
    return pl.pallas_call(
        kernel,
        grid=(1,),
        in_specs=[whole(value.shape) for value in operands],
        out_specs=[whole(out.shape) for out in outs],
        out_shape=outs,
        scratch_shapes=scratch,
        compiler_params=params(),
        name=name,
    )(*operands)


def local(block_input, activations, conv_weight, bn_gain, bn_shift, out_grad, velocity):
    rows, cin = activations.shape
    part, cout = conv_weight.shape
    half = cout // 2
    nzh, nzl, nx = sizes = tuple(lax.axis_size(a) for a in rep)
    nyh, nyl = (lax.axis_size(a) for a in y_axes)
    ny = nyh * nyl
    members = 2 * ny
    first_core = lax.axis_index("c") == 0
    gain, shift = bn_gain.reshape(1, cout), bn_shift.reshape(1, cout)

    def other_half(value):
        return jnp.where(first_core, value[:, half:], value[:, :half])

    pieces = conv_weight.reshape(part, 2, half).transpose(1, 0, 2)
    pieces = jnp.broadcast_to(pieces[None], (ny, 2, part, half)).reshape(members, part, half)
    weight = exchange(pieces, bn).reshape(cin, half)
    acts_other = swap(activations)
    block_other = swap(other_half(block_input))
    out_other = swap(other_half(out_grad))
    weight, acts_other, block_other, out_other = lax.optimization_barrier(
        (weight, acts_other, block_other, out_other)
    )

    wide = shape((rows, half), f32)
    narrow = shape((rows, half), bf16)
    sums = shape((ny, 2 * half // lanes, lanes), f32)
    conv, conv_other, moments = call(
        moments_kernel, "moments", (activations, acts_other, weight), [wide, wide, sums]
    )
    moments = exchange(moments, y_axes)
    grad, grad_other, stats = call(
        stats_kernel,
        "stats",
        (conv, conv_other, moments, gain, shift, block_input, block_other, out_grad, out_other),
        [narrow, narrow, sums],
    )
    stats = exchange(stats, y_axes)
    count = nzl * nx * nyl
    step = 2 * part // nx
    length = groups * nyh * step
    grad_conv, grad_conv_other, partial = call(
        functools.partial(weight_kernel, (nx, nyl, nyh)),
        "weight_partial",
        (conv, conv_other, moments, stats, gain, grad, grad_other, activations, acts_other),
        [narrow, narrow, shape((count, length + 16, lanes), bf16)],
        [pltpu.VMEM((cin, chunk), f32)] + [pltpu.VMEM((cin, rows), bf16)] * 2,
    )
    act, act_other, weight_squares = call(
        act_kernel,
        "act_grad",
        (grad_conv, grad_conv_other, weight),
        [shape((rows, cin), f32), shape((rows, cin), bf16), shape((8, lanes), f32)],
    )
    partial, act_other = lax.optimization_barrier((partial, act_other))
    act_grad = (act + swap(act_other).astype(f32)).astype(bf16)

    (partial,) = call(
        functools.partial(near_kernel, nyh),
        "near_sum",
        (exchange(partial, near),),
        [shape((nzh * nyh, step + 8, lanes), bf16)],
        [pltpu.VMEM((length + 16, lanes), f32)],
    )
    (ready,) = call(
        far_kernel,
        "far_sum",
        (exchange(partial, far),),
        [shape((nzh * nzl * nx, step + 8, lanes), bf16)],
    )
    ready = exchange(ready, rep)
    theirs, squares = call(
        functools.partial(split_kernel, sizes),
        "split",
        (ready, weight_squares),
        [shape((part + 8, half), f32), shape((members, 8, lanes), f32)],
    )
    arrived = swap(theirs)
    squares = exchange(squares, bn)
    new_velocity, gain_grad, shift_grad = call(
        functools.partial(step_kernel, sizes),
        "step",
        (ready, arrived, squares, conv_weight, velocity),
        [shape((part, cout), f32), shape((1, cout), f32), shape((1, cout), f32)],
    )
    return (act_grad, gain_grad.reshape(cout), shift_grad.reshape(cout), new_velocity)


def solution(mesh, dims=(4, 2, 4, 4, 2, 2)):
    fine = Mesh(mesh.devices.reshape(dims), rep + bn)
    every = P(rep + bn, None)
    return jax.shard_map(
        local,
        mesh=fine,
        in_specs=(every, every, P(bn, None), P(), P(), every, P(bn, None)),
        out_specs=(every, P(), P(), P(bn, None)),
        check_vma=False,
    )
```

time: 581 us -> 142 us (0.24)
  waiting for transfers between devices: 267 us -> 27.2 us
  blocking collectives: 262 us -> 51 us
  starting transfers between devices: 0.12 us -> 46 us
  between operations: 15.3 us -> 0.81 us
  other arithmetic: 14.4 us -> 2.55 us
  matrix products: 11 us -> 0 us
  Pallas kernels: 0 us -> 7.74 us
    psum x5 -> x0, blocking collectives: 262 us -> none  [the longest x1 113 us: local(): gain_grad, shift_grad = lax.psum((sum_cross, sum_grad), 'rep')]
    psum x1 -> x0, waiting for transfers between devices: 154 us -> none  [local(): lax.psum(group_grad.astype(jnp.bfloat16), 'rep').astype(jnp.float32)]
    unnamed x4 -> x0, waiting for transfers between devices: 63.2 us -> none
    all_to_all x0 -> x4, blocking collectives: none -> 51 us  [exchange(): return lax.all_to_all(pieces, axis, 0, 0, tiled=True)]
    all_gather x1 -> x0, waiting for transfers between devices: 50 us -> none  [local(): full_weight = lax.all_gather(conv_weight, 'bn', axis=0, tiled=True)]
    all_to_all x0 -> x3, starting transfers between devices: none -> 30.5 us  [exchange(): return lax.all_to_all(pieces, axis, 0, 0, tiled=True)]
    all_to_all x0 -> x3, waiting for transfers between devices: none -> 25.7 us  [exchange(): return lax.all_to_all(pieces, axis, 0, 0, tiled=True)]
    ppermute x0 -> x5, starting transfers between devices: none -> 15.5 us  [swap(): return lax.ppermute(value, 'c', [(0, 1), (1, 0)])]
  transfers between devices with their start and end apart: 3 -> 8, of which waited for: 3 -> 4; matrix products, arithmetic and copies ran while one was open for 1% -> 2% of each run, Pallas kernels for 0% -> 1%
where the time goes in v7:
time: 142 us
  blocking collectives  51 us (36%)
  starting transfers between devices  46 us (32%)
  waiting for transfers between devices  27.2 us (19%)
  Pallas kernels  7.74 us (5%)
  local copies, waits for them, and re-layouts  6.25 us (4%)
  other arithmetic  2.55 us (2%)
    all_to_all x4, blocking collectives, exchange(): return lax.all_to_all(pieces, axis, 0, 0, tiled=True)  51 us
    all_to_all x3, starting transfers between devices, exchange(): return lax.all_to_all(pieces, axis, 0, 0, tiled=True)  30.5 us
    all_to_all x3, waiting for transfers between devices, exchange(): return lax.all_to_all(pieces, axis, 0, 0, tiled=True)  25.7 us
    ppermute x5, starting transfers between devices, swap(): return lax.ppermute(value, 'c', [(0, 1), (1, 0)])  15.5 us
    pallas_call x8, Pallas kernels, call(): pl.pallas_call(kernel, grid=(1,), in_specs=[whole(value.shape) for value...  7.74 us
    unnamed x22, local copies, waits for them, and re-layouts  4.1 us
  transfers between devices with their start and end apart: 8, of which 4 were waited for; matrix products, arithmetic and copies ran while one was open for 2% of the time, Pallas kernels for 1%

profile of v7, /device:TPU:1, one launch (start us, length us, event | category | flops | bytes accessed | tf_op | source)
XLA Modules:
  0.0 141.6 jit_solution(10613482038984942238)
XLA Ops:
  0.6 1.0 reshape.30
  1.7 1.1 broadcast_in_dim.2
  2.8 10.3 %all-to-all-start = ((bf16[16,32,1024]{2,1,0:T(8,128)(2,1)}), bf16[16,32,1024]{2,1,0:T(8,128)(2,1)S(1)}, u32[]{:S(2)}, u32[]{:S(2)}) async-start(bf16[16,32,1024]{2,1,0:T(8,128)(2,1)} %bitcast.1), calls=%async_computation | async-start | bytes 2097152 | tf_op jit(solution)/shard_map/all_to_all | solution.py:29
  13.1 1.6 %slice_select_fusion = bf16[392,1024]{1,0:T(8,128)(2,1)S(1)} fusion(bf16[392,2048]{1,0:T(8,128)(2,1)} %out.1, pred[]{:T(512)S(6)} %eq.3), kind=kLoop, calls=%fused_computation.1 | loop fusion | flops 401408 | bytes 2408449 | tf_op jit(solution)/shard_map/jit(_where)/select_n | solution.py:306
  14.8 2.3 %collective-permute-start.2 = (bf16[392,1024]{1,0:T(8,128)(2,1)S(1)}, bf16[392,1024]{1,0:T(8,128)(2,1)S(1)}, u32[]{:S(2)}, u32[]{:S(2)}) collective-permute-start(bf16[392,1024]{1,0:T(8,128)(2,1)S(1)} %slice_select_fusion), channel_id=1, source_target_pairs={{0,1},{1,0},{2,3},{3,2},{4,5},{5,4},{6,7},{7,6},{8,9},{9,8},{10,11... | collective-permute-start | bytes 2408456 | tf_op jit(solution)/shard_map/ppermute | solution.py:25
  17.1 2.2 %collective-permute-start.1 = (bf16[392,1024]{1,0:T(8,128)(2,1)S(1)}, bf16[392,1024]{1,0:T(8,128)(2,1)S(1)}, u32[]{:S(2)}, u32[]{:S(2)}) collective-permute-start(bf16[392,1024]{1,0:T(8,128)(2,1)S(1)} %slice_select_fusion.1), channel_id=1, source_target_pairs={{0,1},{1,0},{2,3},{3,2},{4,5},{5,4},{6,7},{7,6},{8,9},{9,8},{10,11... | collective-permute-start | bytes 2408456 | tf_op jit(solution)/shard_map/ppermute | solution.py:25
  19.3 2.1 %collective-permute-start = (bf16[392,512]{1,0:T(8,128)(2,1)S(1)}, bf16[392,512]{1,0:T(8,128)(2,1)S(1)}, u32[]{:S(2)}, u32[]{:S(2)}) collective-permute-start(bf16[392,512]{1,0:T(8,128)(2,1)S(1)} %copy-done.2), channel_id=1, source_target_pairs={{0,1},{1,0},{2,3},{3,2},{4,5},{5,4},{6,7},{7,6},{8,9},{9,8},{10,11... | collective-permute-start | bytes 1204232 | tf_op jit(solution)/shard_map/ppermute | solution.py:25
  21.5 1.5 %collective-permute-done.acts_other = bf16[392,512]{1,0:T(8,128)(2,1)S(1)} collective-permute-done((bf16[392,512]{1,0:T(8,128)(2,1)S(1)}, bf16[392,512]{1,0:T(8,128)(2,1)S(1)}, u32[]{:S(2)}, u32[]{:S(2)}) %collective-permute-start) | collective-permute-done | bytes 401440 | tf_op jit(solution)/shard_map/ppermute | solution.py:25
  23.0 0.9 copy-done.3
  23.9 0.9 copy-done.5
  24.8 16.3 %all-to-all-done = bf16[16,32,1024]{2,1,0:T(8,128)(2,1)S(1)} async-done(((bf16[16,32,1024]{2,1,0:T(8,128)(2,1)}), bf16[16,32,1024]{2,1,0:T(8,128)(2,1)S(1)}, u32[]{:S(2)}, u32[]{:S(2)}) %all-to-all-start) | async-done | bytes 1048608 | tf_op jit(solution)/shard_map/all_to_all | solution.py:29
  41.1 1.4 %moments.1 = (f32[392,1024]{1,0:T(8,128)S(1)}, f32[392,1024]{1,0:T(8,128)S(1)}, f32[8,16,128]{2,1,0:T(8,128)S(1)}) custom-call(bf16[392,512]{1,0:T(8,128)(2,1)S(1)} %copy-done.2, bf16[392,512]{1,0:T(8,128)(2,1)S(1)} %collective-permute-done.acts_other, bf16[512,1024]{1,0:T(8,128)(2,1)S(1)} %bitcast.7), custom_call_target="tpu_custom_call" | custom-call | tf_op jit(solution)/shard_map/moments/pallas_call | solution.py:282
  42.5 9.9 %all_to_all.35.moments = f32[8,16,128]{2,1,0:T(8,128)S(1)} all-to-all(f32[8,16,128]{2,1,0:T(8,128)S(1)} %get-tuple-element.31), channel_id=1, replica_groups=mesh['zh'=4,'zl'=2,'x'=4,'yh'=4,'yl'=2,'c'=2] {'yh','yl'}, dimensions={0} | all-to-all | bytes 131072 | tf_op jit(solution)/shard_map/all_to_all | solution.py:29
  52.4 1.1 copy-done.4
  53.5 1.1 copy-done.6
  54.7 1.3 stats.1
  56.0 9.7 %all_to_all.36.stats = f32[8,16,128]{2,1,0:T(8,128)S(1)} all-to-all(f32[8,16,128]{2,1,0:T(8,128)S(1)} %get-tuple-element.34), channel_id=1, replica_groups=mesh['zh'=4,'zl'=2,'x'=4,'yh'=4,'yl'=2,'c'=2] {'yh','yl'}, dimensions={0} | all-to-all | bytes 131072 | tf_op jit(solution)/shard_map/all_to_all | solution.py:29
  65.7 1.4 weight_partial.1
  67.1 1.0 act_grad.1
  68.1 17.7 %all_to_all.37.received = bf16[16,272,128]{2,1,0:T(8,128)(2,1)S(1)} all-to-all(bf16[16,272,128]{2,1,0:T(8,128)(2,1)S(1)} %get-tuple-element.43), channel_id=1, replica_groups=mesh['zh'=4,'zl'=2,'x'=4,'yh'=4,'yl'=2,'c'=2] {'zl','x','yl'}, dimensions={0} | all-to-all | bytes 2228224 | tf_op jit(solution)/shard_map/all_to_all | solution.py:29
  85.8 0.9 near_sum.1
  86.7 10.3 %all-to-all-start.4 = ((bf16[16,24,128]{2,1,0:T(8,128)(2,1)}), bf16[16,24,128]{2,1,0:T(8,128)(2,1)S(1)}, u32[]{:S(2)}, u32[]{:S(2)}) async-start(bf16[16,24,128]{2,1,0:T(8,128)(2,1)} %near_sum.1), calls=%async_computation.4 | async-start | bytes 196608 | tf_op jit(solution)/shard_map/all_to_all | solution.py:29
  97.0 6.7 %collective-permute-start.3 = (bf16[392,512]{1,0:T(8,128)(2,1)S(1)}, bf16[392,512]{1,0:T(8,128)(2,1)S(1)}, u32[]{:S(2)}, u32[]{:S(2)}) collective-permute-start(bf16[392,512]{1,0:T(8,128)(2,1)S(1)} %get-tuple-element.42), channel_id=1, source_target_pairs={{0,1},{1,0},{2,3},{3,2},{4,5},{5,4},{6,7},{7,6},{8,9},{9,8},{10,11... | collective-permute-start | bytes 1204232 | tf_op jit(solution)/shard_map/ppermute | solution.py:25
  103.7 4.6 %all-to-all-done.4.received = bf16[16,24,128]{2,1,0:T(8,128)(2,1)S(1)} async-done(((bf16[16,24,128]{2,1,0:T(8,128)(2,1)}), bf16[16,24,128]{2,1,0:T(8,128)(2,1)S(1)}, u32[]{:S(2)}, u32[]{:S(2)}) %all-to-all-start.4) | async-done | bytes 98336 | tf_op jit(solution)/shard_map/all_to_all | solution.py:29
  108.3 0.1 far_sum.1
  108.5 13.8 %all_to_all.38.parts = bf16[32,24,128]{2,1,0:T(8,128)(2,1)S(1)} all-to-all(bf16[32,24,128]{2,1,0:T(8,128)(2,1)S(1)} %far_sum.1), channel_id=1, replica_groups=mesh['zh'=4,'zl'=2,'x'=4,'yh'=4,'yl'=2,'c'=2] {'zh','zl','x'}, dimensions={0} | all-to-all | bytes 393216 | tf_op jit(solution)/shard_map/all_to_all | solution.py:29
  122.2 0.7 split.1
  123.0 9.9 %all-to-all-start.6 = ((f32[16,8,128]{2,1,0:T(8,128)}), f32[16,8,128]{2,1,0:T(8,128)S(1)}, u32[]{:S(2)}, u32[]{:S(2)}) async-start(f32[16,8,128]{2,1,0:T(8,128)} %get-tuple-element.46), calls=%async_computation.6 | async-start | bytes 131072 | tf_op jit(solution)/shard_map/all_to_all | solution.py:29
  132.9 2.1 %collective-permute-start.4 = (f32[40,1024]{1,0:T(8,128)S(1)}, f32[40,1024]{1,0:T(8,128)S(1)}, u32[]{:S(2)}, u32[]{:S(2)}) collective-permute-start(f32[40,1024]{1,0:T(8,128)S(1)} %get-tuple-element.45), channel_id=1, source_target_pairs={{0,1},{1,0},{2,3},{3,2},{4,5},{5,4},{6,7},{7,6},{8,9},{9,8},{10,11... | collective-permute-start | bytes 491528 | tf_op jit(solution)/shard_map/ppermute | solution.py:25
  135.0 0.9 add_convert_fusion
  135.9 4.8 %all-to-all-done.6.squares = f32[16,8,128]{2,1,0:T(8,128)S(1)} async-done(((f32[16,8,128]{2,1,0:T(8,128)}), f32[16,8,128]{2,1,0:T(8,128)S(1)}, u32[]{:S(2)}, u32[]{:S(2)}) %all-to-all-start.6) | async-done | bytes 65568 | tf_op jit(solution)/shard_map/all_to_all | solution.py:29
  140.7 0.8 step.1
  (24 shorter events, 0.2 us)
Async XLA Ops:
  2.8 38.3 %all-to-all-start = ((bf16[16,32,1024]{2,1,0:T(8,128)(2,1)}), bf16[16,32,1024]{2,1,0:T(8,128)(2,1)S(1)}, u32[]{:S(2)}, u32[]{:S(2)}) async-start(bf16[16,32,1024]{2,1,0:T(8,128)(2,1)} %bitcast.1), calls=%async_computation | async-start | bytes 2097152 | tf_op jit(solution)/shard_map/all_to_all | solution.py:29
  13.1 3.9 %copy-start = (bf16[392,2048]{1,0:T(8,128)(2,1)S(1)}, bf16[392,2048]{1,0:T(8,128)(2,1)}, u32[]{:S(2)}) copy-start(bf16[392,2048]{1,0:T(8,128)(2,1)} %block.1) | copy-start | bytes 4816900
  14.7 4.6 %copy-start.2 = (bf16[392,512]{1,0:T(8,128)(2,1)S(1)}, bf16[392,512]{1,0:T(8,128)(2,1)}, u32[]{:S(2)}) copy-start(bf16[392,512]{1,0:T(8,128)(2,1)} %acts.3) | copy-start | bytes 1204228
  14.7 37.7 %copy-start.9 = (f32[2048]{0:T(1024)S(1)}, f32[2048]{0:T(1024)}, u32[]{:S(2)}) copy-start(f32[2048]{0:T(1024)} %param.10) | copy-start | bytes 24580
  14.7 37.6 %copy-start.10 = (f32[2048]{0:T(1024)S(1)}, f32[2048]{0:T(1024)}, u32[]{:S(2)}) copy-start(f32[2048]{0:T(1024)} %param.11) | copy-start | bytes 24580
  14.8 8.2 %collective-permute-start.2 = (bf16[392,1024]{1,0:T(8,128)(2,1)S(1)}, bf16[392,1024]{1,0:T(8,128)(2,1)S(1)}, u32[]{:S(2)}, u32[]{:S(2)}) collective-permute-start(bf16[392,1024]{1,0:T(8,128)(2,1)S(1)} %slice_select_fusion), channel_id=1, source_target_pairs={{0,1},{1,0},{2,3},{3,2},{4,5},{5,4},{6,7},{7,6},{8,9},{9,8},{10,11... | collective-permute-start | bytes 2408456 | tf_op jit(solution)/shard_map/ppermute | solution.py:25
  17.1 6.8 %collective-permute-start.1 = (bf16[392,1024]{1,0:T(8,128)(2,1)S(1)}, bf16[392,1024]{1,0:T(8,128)(2,1)S(1)}, u32[]{:S(2)}, u32[]{:S(2)}) collective-permute-start(bf16[392,1024]{1,0:T(8,128)(2,1)S(1)} %slice_select_fusion.1), channel_id=1, source_target_pairs={{0,1},{1,0},{2,3},{3,2},{4,5},{5,4},{6,7},{7,6},{8,9},{9,8},{10,11... | collective-permute-start | bytes 2408456 | tf_op jit(solution)/shard_map/ppermute | solution.py:25
  19.3 3.6 %collective-permute-start = (bf16[392,512]{1,0:T(8,128)(2,1)S(1)}, bf16[392,512]{1,0:T(8,128)(2,1)S(1)}, u32[]{:S(2)}, u32[]{:S(2)}) collective-permute-start(bf16[392,512]{1,0:T(8,128)(2,1)S(1)} %copy-done.2), channel_id=1, source_target_pairs={{0,1},{1,0},{2,3},{3,2},{4,5},{5,4},{6,7},{7,6},{8,9},{9,8},{10,11... | collective-permute-start | bytes 1204232 | tf_op jit(solution)/shard_map/ppermute | solution.py:25
  23.0 0.9 copy-start.3
  23.9 0.9 copy-start.5
  41.1 11.3 %copy-start.1 = (bf16[392,2048]{1,0:T(8,128)(2,1)S(1)}, bf16[392,2048]{1,0:T(8,128)(2,1)}, u32[]{:S(2)}) copy-start(bf16[392,2048]{1,0:T(8,128)(2,1)} %out.1) | copy-start | bytes 4816900
  52.4 1.1 copy-start.4
  53.5 1.1 copy-start.6
  86.7 54.0 %copy-start.7 = (bf16[32,2048]{1,0:T(8,128)(2,1)S(1)}, bf16[32,2048]{1,0:T(8,128)(2,1)}, u32[]{:S(2)}) copy-start(bf16[32,2048]{1,0:T(8,128)(2,1)} %weight.1) | copy-start | bytes 393220
  86.7 54.0 %copy-start.8 = (f32[32,2048]{1,0:T(8,128)S(1)}, f32[32,2048]{1,0:T(8,128)}, u32[]{:S(2)}) copy-start(f32[32,2048]{1,0:T(8,128)} %velocity.1) | copy-start | bytes 786436
  86.7 21.7 %all-to-all-start.4 = ((bf16[16,24,128]{2,1,0:T(8,128)(2,1)}), bf16[16,24,128]{2,1,0:T(8,128)(2,1)S(1)}, u32[]{:S(2)}, u32[]{:S(2)}) async-start(bf16[16,24,128]{2,1,0:T(8,128)(2,1)} %near_sum.1), calls=%async_computation.4 | async-start | bytes 196608 | tf_op jit(solution)/shard_map/all_to_all | solution.py:29
  97.0 38.0 %collective-permute-start.3 = (bf16[392,512]{1,0:T(8,128)(2,1)S(1)}, bf16[392,512]{1,0:T(8,128)(2,1)S(1)}, u32[]{:S(2)}, u32[]{:S(2)}) collective-permute-start(bf16[392,512]{1,0:T(8,128)(2,1)S(1)} %get-tuple-element.42), channel_id=1, source_target_pairs={{0,1},{1,0},{2,3},{3,2},{4,5},{5,4},{6,7},{7,6},{8,9},{9,8},{10,11... | collective-permute-start | bytes 1204232 | tf_op jit(solution)/shard_map/ppermute | solution.py:25
  123.0 17.7 %all-to-all-start.6 = ((f32[16,8,128]{2,1,0:T(8,128)}), f32[16,8,128]{2,1,0:T(8,128)S(1)}, u32[]{:S(2)}, u32[]{:S(2)}) async-start(f32[16,8,128]{2,1,0:T(8,128)} %get-tuple-element.46), calls=%async_computation.6 | async-start | bytes 131072 | tf_op jit(solution)/shard_map/all_to_all | solution.py:29
  132.9 7.8 %collective-permute-start.4 = (f32[40,1024]{1,0:T(8,128)S(1)}, f32[40,1024]{1,0:T(8,128)S(1)}, u32[]{:S(2)}, u32[]{:S(2)}) collective-permute-start(f32[40,1024]{1,0:T(8,128)S(1)} %get-tuple-element.45), channel_id=1, source_target_pairs={{0,1},{1,0},{2,3},{3,2},{4,5},{5,4},{6,7},{7,6},{8,9},{9,8},{10,11... | collective-permute-start | bytes 491528 | tf_op jit(solution)/shard_map/ppermute | solution.py:25

commit v8 on v7

--- a/solution.py
+++ b/solution.py
@@ -305,15 +305,13 @@
     def other_half(value):
         return jnp.where(first_core, value[:, half:], value[:, :half])
 
-    pieces = conv_weight.reshape(part, 2, half).transpose(1, 0, 2)
+    pieces = jnp.stack([conv_weight[:, :half], conv_weight[:, half:]])
     pieces = jnp.broadcast_to(pieces[None], (ny, 2, part, half)).reshape(members, part, half)
     weight = exchange(pieces, bn).reshape(cin, half)
     acts_other = swap(activations)
     block_other = swap(other_half(block_input))
     out_other = swap(other_half(out_grad))
-    weight, acts_other, block_other, out_other = lax.optimization_barrier(
-        (weight, acts_other, block_other, out_other)
-    )
+    weight, acts_other = lax.optimization_barrier((weight, acts_other))
 
     wide = shape((rows, half), f32)
     narrow = shape((rows, half), bf16)
@@ -321,6 +319,7 @@
     conv, conv_other, moments = call(
         moments_kernel, "moments", (activations, acts_other, weight), [wide, wide, sums]
     )
+    moments, block_other, out_other = lax.optimization_barrier((moments, block_other, out_other))
     moments = exchange(moments, y_axes)
     grad, grad_other, stats = call(
         stats_kernel,
@@ -347,11 +346,12 @@
     )
     partial, act_other = lax.optimization_barrier((partial, act_other))
     act_grad = (act + swap(act_other).astype(f32)).astype(bf16)
+    partial, act_grad = lax.optimization_barrier((exchange(partial, near), act_grad))
 
     (partial,) = call(
         functools.partial(near_kernel, nyh),
         "near_sum",
-        (exchange(partial, near),),
+        (partial,),
         [shape((nzh * nyh, step + 8, lanes), bf16)],
         [pltpu.VMEM((length + 16, lanes), f32)],
     )

time: 142 us -> 143 us (level)
  blocking collectives: 51 us -> 64.6 us
  starting transfers between devices: 46 us -> 33.7 us
  local copies, waits for them, and re-layouts: 6.25 us -> 2.04 us
  other arithmetic: 2.55 us -> 4.33 us
    all_to_all x3 -> x2, starting transfers between devices: 30.5 us -> 14.5 us  [exchange(): return lax.all_to_all(pieces, axis, 0, 0, tiled=True)]
    all_to_all x4 -> x5, blocking collectives: 51 us -> 64.6 us  [exchange(): return lax.all_to_all(pieces, axis, 0, 0, tiled=True)]
    unnamed x22 -> x14, local copies, waits for them, and re-layouts: 4.1 us -> 0.03 us
    ppermute x5, starting transfers between devices: 15.5 us -> 19.2 us  [swap(): return lax.ppermute(value, 'c', [(0, 1), (1, 0)])]
    select_n x2, other arithmetic: 1.67 us -> 3.44 us  [other_half(): return jnp.where(first_core, value[:, half:], value[:, :half])]
    all_to_all x3 -> x2, waiting for transfers between devices: 25.7 us -> 25 us  [exchange(): return lax.all_to_all(pieces, axis, 0, 0, tiled=True)]
  transfers between devices with their start and end apart: 8 -> 7, of which waited for: 4 -> 4; matrix products, arithmetic and copies ran while one was open for 2% -> 3% of each run, Pallas kernels for 1% -> 1%
where the time goes in v8:
time: 143 us; the launch traced here: 142 us
  blocking collectives  64.6 us (45%)
  starting transfers between devices  33.7 us (24%)
  waiting for transfers between devices  27.8 us (19%)
  Pallas kernels  8.9 us (6%)
  other arithmetic  4.33 us (3%)
  local copies, waits for them, and re-layouts  2.04 us (1%)
    all_to_all x5, blocking collectives, exchange(): return lax.all_to_all(pieces, axis, 0, 0, tiled=True)  64.6 us
    all_to_all x2, waiting for transfers between devices, exchange(): return lax.all_to_all(pieces, axis, 0, 0, tiled=True)  25 us
    ppermute x5, starting transfers between devices, swap(): return lax.ppermute(value, 'c', [(0, 1), (1, 0)])  19.2 us
    all_to_all x2, starting transfers between devices, exchange(): return lax.all_to_all(pieces, axis, 0, 0, tiled=True)  14.5 us
    pallas_call x8, Pallas kernels, call(): pl.pallas_call(kernel, grid=(1,), in_specs=[whole(value.shape) for value...  8.9 us
    select_n x2, other arithmetic, other_half(): return jnp.where(first_core, value[:, half:], value[:, :half])  3.44 us
  transfers between devices with their start and end apart: 7, of which 4 were waited for; matrix products, arithmetic and copies ran while one was open for 3% of the time, Pallas kernels for 1%

profile of v8, /device:TPU:1, one launch (start us, length us, event | category | flops | bytes accessed | tf_op | source)
XLA Modules:
  0.0 142.2 jit_solution(1660310123106512860)
XLA Ops:
  0.6 0.9 slice_bitcast_fusion.1
  1.5 1.1 broadcast_in_dim.2
  2.7 10.3 %all-to-all-start = ((bf16[16,32,1024]{2,1,0:T(8,128)(2,1)}), bf16[16,32,1024]{2,1,0:T(8,128)(2,1)S(1)}, u32[]{:S(2)}, u32[]{:S(2)}) async-start(bf16[16,32,1024]{2,1,0:T(8,128)(2,1)} %bitcast.2), calls=%async_computation | async-start | bytes 2097152 | tf_op jit(solution)/shard_map/all_to_all | solution.py:29
  13.0 2.5 %slice_select_fusion = bf16[392,1024]{1,0:T(8,128)(2,1)} fusion(bf16[392,2048]{1,0:T(8,128)(2,1)} %out.1, pred[]{:T(512)S(6)} %eq.3), kind=kLoop, calls=%fused_computation.1 | loop fusion | flops 401408 | bytes 2408449 | tf_op jit(solution)/shard_map/jit(_where)/select_n | solution.py:306
  15.5 2.3 %collective-permute-start.2 = (bf16[392,1024]{1,0:T(8,128)(2,1)}, bf16[392,1024]{1,0:T(8,128)(2,1)}, u32[]{:S(2)}, u32[]{:S(2)}) collective-permute-start(bf16[392,1024]{1,0:T(8,128)(2,1)} %slice_select_fusion), channel_id=1, source_target_pairs={{0,1},{1,0},{2,3},{3,2},{4,5},{5,4},{6,7},{7,6},{8,9},{9,8},{10,11... | collective-permute-start | bytes 2408456 | tf_op jit(solution)/shard_map/ppermute | solution.py:25
  17.8 1.0 slice_select_fusion.1
  18.7 2.2 %collective-permute-start.1 = (bf16[392,1024]{1,0:T(8,128)(2,1)}, bf16[392,1024]{1,0:T(8,128)(2,1)}, u32[]{:S(2)}, u32[]{:S(2)}) collective-permute-start(bf16[392,1024]{1,0:T(8,128)(2,1)} %slice_select_fusion.1), channel_id=1, source_target_pairs={{0,1},{1,0},{2,3},{3,2},{4,5},{5,4},{6,7},{7,6},{8,9},{9,8},{10,11... | collective-permute-start | bytes 2408456 | tf_op jit(solution)/shard_map/ppermute | solution.py:25
  20.9 2.1 %collective-permute-start = (bf16[392,512]{1,0:T(8,128)(2,1)S(1)}, bf16[392,512]{1,0:T(8,128)(2,1)S(1)}, u32[]{:S(2)}, u32[]{:S(2)}) collective-permute-start(bf16[392,512]{1,0:T(8,128)(2,1)S(1)} %copy-done.2), channel_id=1, source_target_pairs={{0,1},{1,0},{2,3},{3,2},{4,5},{5,4},{6,7},{7,6},{8,9},{9,8},{10,11... | collective-permute-start | bytes 1204232 | tf_op jit(solution)/shard_map/ppermute | solution.py:25
  23.1 1.5 %collective-permute-done.acts_other = bf16[392,512]{1,0:T(8,128)(2,1)S(1)} collective-permute-done((bf16[392,512]{1,0:T(8,128)(2,1)S(1)}, bf16[392,512]{1,0:T(8,128)(2,1)S(1)}, u32[]{:S(2)}, u32[]{:S(2)}) %collective-permute-start) | collective-permute-done | bytes 401440 | tf_op jit(solution)/shard_map/ppermute | solution.py:25
  24.6 16.4 %all-to-all-done = bf16[16,32,1024]{2,1,0:T(8,128)(2,1)S(1)} async-done(((bf16[16,32,1024]{2,1,0:T(8,128)(2,1)}), bf16[16,32,1024]{2,1,0:T(8,128)(2,1)S(1)}, u32[]{:S(2)}, u32[]{:S(2)}) %all-to-all-start) | async-done | bytes 1048608 | tf_op jit(solution)/shard_map/all_to_all | solution.py:29
  41.0 1.4 %moments.1 = (f32[392,1024]{1,0:T(8,128)S(1)}, f32[392,1024]{1,0:T(8,128)S(1)}, f32[8,16,128]{2,1,0:T(8,128)S(1)}) custom-call(bf16[392,512]{1,0:T(8,128)(2,1)S(1)} %copy-done.2, bf16[392,512]{1,0:T(8,128)(2,1)S(1)} %collective-permute-done.acts_other, bf16[512,1024]{1,0:T(8,128)(2,1)S(1)} %bitcast.10), custom_call_target="tpu_custom_call" | custom-call | tf_op jit(solution)/shard_map/moments/pallas_call | solution.py:282
  42.4 0.0 collective-permute-done.2.out_other
  42.4 0.0 collective-permute-done.1.block_other
  42.4 9.9 %all_to_all.35.moments = f32[8,16,128]{2,1,0:T(8,128)S(1)} all-to-all(f32[8,16,128]{2,1,0:T(8,128)S(1)} %get-tuple-element.35), channel_id=1, replica_groups=mesh['zh'=4,'zl'=2,'x'=4,'yh'=4,'yl'=2,'c'=2] {'yh','yl'}, dimensions={0} | all-to-all | bytes 131072 | tf_op jit(solution)/shard_map/all_to_all | solution.py:29
  52.3 2.7 %stats.1 = (bf16[392,1024]{1,0:T(8,128)(2,1)S(1)}, bf16[392,1024]{1,0:T(8,128)(2,1)S(1)}, f32[8,16,128]{2,1,0:T(8,128)S(1)}) custom-call(f32[392,1024]{1,0:T(8,128)S(1)} %get-tuple-element.32.conv, f32[392,1024]{1,0:T(8,128)S(1)} %get-tuple-element.33.conv_other, f32[8,16,128]{2,1,0:T(8,128)S(1)} %all_to_all.35.moments, f32[1,2048]{1,0:T(1,128)S(1)} %bitcast.12, ...), custom_call_target="tpu_custom_call" | custom-call | tf_op jit(solution)/shard_map/stats/pallas_call | solution.py:282
  55.0 9.7 %all_to_all.36.stats = f32[8,16,128]{2,1,0:T(8,128)S(1)} all-to-all(f32[8,16,128]{2,1,0:T(8,128)S(1)} %get-tuple-element.38), channel_id=1, replica_groups=mesh['zh'=4,'zl'=2,'x'=4,'yh'=4,'yl'=2,'c'=2] {'yh','yl'}, dimensions={0} | all-to-all | bytes 131072 | tf_op jit(solution)/shard_map/all_to_all | solution.py:29
  64.7 2.4 %weight_partial.1 = (bf16[392,1024]{1,0:T(8,128)(2,1)S(1)}, bf16[392,1024]{1,0:T(8,128)(2,1)S(1)}, bf16[16,272,128]{2,1,0:T(8,128)(2,1)}) custom-call(f32[392,1024]{1,0:T(8,128)S(1)} %get-tuple-element.32.conv, f32[392,1024]{1,0:T(8,128)S(1)} %get-tuple-element.33.conv_other, f32[8,16,128]{2,1,0:T(8,128)S(1)} %all_to_all.35.moments, ...), custom_call_target="tpu_custom_call" | custom-call | tf_op jit(solution)/shard_map/weight_partial/pallas_call | solution.py:282
  67.1 1.0 act_grad.1
  68.2 4.2 %all-to-all-start.3 = ((bf16[16,272,128]{2,1,0:T(8,128)(2,1)}), bf16[16,272,128]{2,1,0:T(8,128)(2,1)S(1)}, u32[]{:S(2)}, u32[]{:S(2)}) async-start(bf16[16,272,128]{2,1,0:T(8,128)(2,1)} %get-tuple-element.45), calls=%async_computation.3 | async-start | bytes 2228224 | tf_op jit(solution)/shard_map/all_to_all | solution.py:29
  72.4 5.0 %collective-permute-start.3 = (bf16[392,512]{1,0:T(8,128)(2,1)S(1)}, bf16[392,512]{1,0:T(8,128)(2,1)S(1)}, u32[]{:S(2)}, u32[]{:S(2)}) collective-permute-start(bf16[392,512]{1,0:T(8,128)(2,1)S(1)} %get-tuple-element.47), channel_id=1, source_target_pairs={{0,1},{1,0},{2,3},{3,2},{4,5},{5,4},{6,7},{7,6},{8,9},{9,8},{10,11... | collective-permute-start | bytes 1204232 | tf_op jit(solution)/shard_map/ppermute | solution.py:25
  77.5 1.3 collective-permute-done.3
  78.8 0.9 add_convert_fusion
  79.7 8.6 %all-to-all-done.3.received = bf16[16,272,128]{2,1,0:T(8,128)(2,1)S(1)} async-done(((bf16[16,272,128]{2,1,0:T(8,128)(2,1)}), bf16[16,272,128]{2,1,0:T(8,128)(2,1)S(1)}, u32[]{:S(2)}, u32[]{:S(2)}) %all-to-all-start.3) | async-done | bytes 1114144 | tf_op jit(solution)/shard_map/all_to_all | solution.py:29
  88.3 0.2 near_sum.1
  88.5 21.4 %all_to_all.37.received = bf16[16,24,128]{2,1,0:T(8,128)(2,1)S(1)} all-to-all(bf16[16,24,128]{2,1,0:T(8,128)(2,1)S(1)} %near_sum.1), channel_id=1, replica_groups=mesh['zh'=4,'zl'=2,'x'=4,'yh'=4,'yl'=2,'c'=2] {'zh','yh'}, dimensions={0} | all-to-all | bytes 196608 | tf_op jit(solution)/shard_map/all_to_all | solution.py:29
  109.9 0.1 far_sum.1
  110.0 13.1 %all_to_all.38.parts = bf16[32,24,128]{2,1,0:T(8,128)(2,1)S(1)} all-to-all(bf16[32,24,128]{2,1,0:T(8,128)(2,1)S(1)} %far_sum.1), channel_id=1, replica_groups=mesh['zh'=4,'zl'=2,'x'=4,'yh'=4,'yl'=2,'c'=2] {'zh','zl','x'}, dimensions={0} | all-to-all | bytes 393216 | tf_op jit(solution)/shard_map/all_to_all | solution.py:29
  123.1 0.1 split.1
  123.2 7.5 %collective-permute-start.4 = (f32[40,1024]{1,0:T(8,128)S(1)}, f32[40,1024]{1,0:T(8,128)S(1)}, u32[]{:S(2)}, u32[]{:S(2)}) collective-permute-start(f32[40,1024]{1,0:T(8,128)S(1)} %get-tuple-element.51), channel_id=1, source_target_pairs={{0,1},{1,0},{2,3},{3,2},{4,5},{5,4},{6,7},{7,6},{8,9},{9,8},{10,11... | collective-permute-start | bytes 491528 | tf_op jit(solution)/shard_map/ppermute | solution.py:25
  130.7 10.6 %all_to_all.39.squares = f32[16,8,128]{2,1,0:T(8,128)S(1)} all-to-all(f32[16,8,128]{2,1,0:T(8,128)S(1)} %get-tuple-element.52), channel_id=1, replica_groups=mesh['zh'=4,'zl'=2,'x'=4,'yh'=4,'yl'=2,'c'=2] {'yh','yl','c'}, dimensions={0} | all-to-all | bytes 131072 | tf_op jit(solution)/shard_map/all_to_all | solution.py:29
  141.3 0.0 collective-permute-done.4.arrived
  141.4 0.8 step.1
  (15 shorter events, 0.0 us)
Async XLA Ops:
  2.7 38.3 %all-to-all-start = ((bf16[16,32,1024]{2,1,0:T(8,128)(2,1)}), bf16[16,32,1024]{2,1,0:T(8,128)(2,1)S(1)}, u32[]{:S(2)}, u32[]{:S(2)}) async-start(bf16[16,32,1024]{2,1,0:T(8,128)(2,1)} %bitcast.2), calls=%async_computation | async-start | bytes 2097152 | tf_op jit(solution)/shard_map/all_to_all | solution.py:29
  13.0 4.8 %copy-start = (bf16[392,2048]{1,0:T(8,128)(2,1)S(1)}, bf16[392,2048]{1,0:T(8,128)(2,1)}, u32[]{:S(2)}) copy-start(bf16[392,2048]{1,0:T(8,128)(2,1)} %block.1) | copy-start | bytes 4816900
  15.5 5.4 %copy-start.2 = (bf16[392,512]{1,0:T(8,128)(2,1)S(1)}, bf16[392,512]{1,0:T(8,128)(2,1)}, u32[]{:S(2)}) copy-start(bf16[392,512]{1,0:T(8,128)(2,1)} %acts.3) | copy-start | bytes 1204228
  15.5 36.8 %copy-start.5 = (f32[2048]{0:T(1024)S(1)}, f32[2048]{0:T(1024)}, u32[]{:S(2)}) copy-start(f32[2048]{0:T(1024)} %param.10) | copy-start | bytes 24580
  15.5 36.8 %copy-start.6 = (f32[2048]{0:T(1024)S(1)}, f32[2048]{0:T(1024)}, u32[]{:S(2)}) copy-start(f32[2048]{0:T(1024)} %param.11) | copy-start | bytes 24580
  15.5 26.9 %collective-permute-start.2 = (bf16[392,1024]{1,0:T(8,128)(2,1)}, bf16[392,1024]{1,0:T(8,128)(2,1)}, u32[]{:S(2)}, u32[]{:S(2)}) collective-permute-start(bf16[392,1024]{1,0:T(8,128)(2,1)} %slice_select_fusion), channel_id=1, source_target_pairs={{0,1},{1,0},{2,3},{3,2},{4,5},{5,4},{6,7},{7,6},{8,9},{9,8},{10,11... | collective-permute-start | bytes 2408456 | tf_op jit(solution)/shard_map/ppermute | solution.py:25
  18.7 23.7 %collective-permute-start.1 = (bf16[392,1024]{1,0:T(8,128)(2,1)}, bf16[392,1024]{1,0:T(8,128)(2,1)}, u32[]{:S(2)}, u32[]{:S(2)}) collective-permute-start(bf16[392,1024]{1,0:T(8,128)(2,1)} %slice_select_fusion.1), channel_id=1, source_target_pairs={{0,1},{1,0},{2,3},{3,2},{4,5},{5,4},{6,7},{7,6},{8,9},{9,8},{10,11... | collective-permute-start | bytes 2408456 | tf_op jit(solution)/shard_map/ppermute | solution.py:25
  20.9 3.6 %collective-permute-start = (bf16[392,512]{1,0:T(8,128)(2,1)S(1)}, bf16[392,512]{1,0:T(8,128)(2,1)S(1)}, u32[]{:S(2)}, u32[]{:S(2)}) collective-permute-start(bf16[392,512]{1,0:T(8,128)(2,1)S(1)} %copy-done.2), channel_id=1, source_target_pairs={{0,1},{1,0},{2,3},{3,2},{4,5},{5,4},{6,7},{7,6},{8,9},{9,8},{10,11... | collective-permute-start | bytes 1204232 | tf_op jit(solution)/shard_map/ppermute | solution.py:25
  41.0 11.3 %copy-start.1 = (bf16[392,2048]{1,0:T(8,128)(2,1)S(1)}, bf16[392,2048]{1,0:T(8,128)(2,1)}, u32[]{:S(2)}) copy-start(bf16[392,2048]{1,0:T(8,128)(2,1)} %out.1) | copy-start | bytes 4816900
  68.2 20.1 %all-to-all-start.3 = ((bf16[16,272,128]{2,1,0:T(8,128)(2,1)}), bf16[16,272,128]{2,1,0:T(8,128)(2,1)S(1)}, u32[]{:S(2)}, u32[]{:S(2)}) async-start(bf16[16,272,128]{2,1,0:T(8,128)(2,1)} %get-tuple-element.45), calls=%async_computation.3 | async-start | bytes 2228224 | tf_op jit(solution)/shard_map/all_to_all | solution.py:29
  72.4 6.4 %collective-permute-start.3 = (bf16[392,512]{1,0:T(8,128)(2,1)S(1)}, bf16[392,512]{1,0:T(8,128)(2,1)S(1)}, u32[]{:S(2)}, u32[]{:S(2)}) collective-permute-start(bf16[392,512]{1,0:T(8,128)(2,1)S(1)} %get-tuple-element.47), channel_id=1, source_target_pairs={{0,1},{1,0},{2,3},{3,2},{4,5},{5,4},{6,7},{7,6},{8,9},{9,8},{10,11... | collective-permute-start | bytes 1204232 | tf_op jit(solution)/shard_map/ppermute | solution.py:25
  79.7 61.7 %copy-start.3 = (bf16[32,2048]{1,0:T(8,128)(2,1)S(1)}, bf16[32,2048]{1,0:T(8,128)(2,1)}, u32[]{:S(2)}) copy-start(bf16[32,2048]{1,0:T(8,128)(2,1)} %weight.1) | copy-start | bytes 393220
  79.7 61.7 %copy-start.4 = (f32[32,2048]{1,0:T(8,128)S(1)}, f32[32,2048]{1,0:T(8,128)}, u32[]{:S(2)}) copy-start(f32[32,2048]{1,0:T(8,128)} %velocity.1) | copy-start | bytes 786436
  123.2 18.2 %collective-permute-start.4 = (f32[40,1024]{1,0:T(8,128)S(1)}, f32[40,1024]{1,0:T(8,128)S(1)}, u32[]{:S(2)}, u32[]{:S(2)}) collective-permute-start(f32[40,1024]{1,0:T(8,128)S(1)} %get-tuple-element.51), channel_id=1, source_target_pairs={{0,1},{1,0},{2,3},{3,2},{4,5},{5,4},{6,7},{7,6},{8,9},{9,8},{10,11... | collective-permute-start | bytes 491528 | tf_op jit(solution)/shard_map/ppermute | solution.py:25

commit v9 on v8

--- a/solution.py
+++ b/solution.py
@@ -51,6 +51,20 @@
     return [pl.ds(start, chunk) for start in range(0, width, chunk)]
 
 
+def pieces_kernel(weight, out, sems):
+    half = out.shape[2]
+    copies_out = [
+        pltpu.make_async_copy(
+            weight.at[:, pl.ds(i % 2 * half, half)], out.at[i], sems.at[i]
+        )
+        for i in range(out.shape[0])
+    ]
+    for copy in copies_out:
+        copy.start()
+    for copy in copies_out:
+        copy.wait()
+
+
 def moments_kernel(acts, acts_other, weight, conv, conv_other, moments):
     count = 2 * conv.shape[0]
     for j, cols in enumerate(columns(conv.shape[1])):
@@ -76,25 +90,58 @@
 
 
 def stats_kernel(
-    conv, conv_other, moments, gain, shift, block, block_other, out, out_other, grad, grad_other, stats
+    conv,
+    conv_other,
+    moments,
+    gain,
+    shift,
+    block,
+    out,
+    block_far,
+    out_far,
+    grad,
+    grad_other,
+    stats,
+    block_other,
+    out_other,
+    sems,
 ):
     rows, half = conv.shape
     core = lax.axis_index("c")
+    loads = [
+        pltpu.make_async_copy(block_far, block_other, sems.at[0]),
+        pltpu.make_async_copy(out_far, out_other, sems.at[1]),
+    ]
+    for load in loads:
+        load.start()
+    scales = []
     for j, cols in enumerate(columns(half)):
         place = pl.ds(pl.multiple_of(core * half + j * chunk, chunk), chunk)
         mean, inv_std = pooled(moments[:, 8 * j : 8 * j + 8], 2 * rows)
-        scale, bias = gain[:, place] * inv_std, shift[:, place]
-        sum_grad = sum_cross = 0.0
-        for of, added, incoming, result in (
-            (conv, block[:, place], out[:, place], grad),
-            (conv_other, block_other[:, cols], out_other[:, cols], grad_other),
-        ):
-            centered = of[:, cols] - mean
-            summed = centered * scale + bias + added.astype(f32)
-            value = jnp.where(summed > 0.0, incoming.astype(f32), 0.0)
-            result[:, cols] = value.astype(bf16)
-            sum_grad += jnp.sum(value, axis=0, keepdims=True)
-            sum_cross += jnp.sum(value * centered, axis=0, keepdims=True)
+        scales.append((cols, place, mean, inv_std, gain[:, place] * inv_std, shift[:, place]))
+
+    def sums(of, added, incoming, result, cols, mean, scale, bias):
+        centered = of[:, cols] - mean
+        summed = centered * scale + bias + added.astype(f32)
+        value = jnp.where(summed > 0.0, incoming.astype(f32), 0.0)
+        result[:, cols] = value.astype(bf16)
+        return (
+            jnp.sum(value, axis=0, keepdims=True),
+            jnp.sum(value * centered, axis=0, keepdims=True),
+        )
+
+    near_sums = [
+        sums(conv, block[:, place], out[:, place], grad, cols, mean, scale, bias)
+        for cols, place, mean, _, scale, bias in scales
+    ]
+    for load in loads:
+        load.wait()
+    for j, (cols, _, mean, inv_std, scale, bias) in enumerate(scales):
+        sum_grad, sum_cross = sums(
+            conv_other, block_other[:, cols], out_other[:, cols], grad_other, cols, mean, scale, bias
+        )
+        sum_grad += near_sums[j][0]
+        sum_cross += near_sums[j][1]
         tile = jnp.concatenate(fold(sum_grad) + fold(sum_cross * inv_std), axis=0)
         stats[:, 8 * j : 8 * j + 8] = jnp.broadcast_to(tile[None], (stats.shape[0], 8, lanes))
 
@@ -110,12 +157,18 @@
     grad_other,
     acts,
     acts_other,
+    weight,
+    act,
+    act_other,
+    squares,
+    result_out,
+    wide,
+    acts_t,
+    acts_t_other,
     grad_conv,
     grad_conv_other,
     out,
-    wide,
-    acts_t,
-    acts_t_other,
+    sems,
 ):
     nx, nyl, nyh = sizes
     core = lax.axis_index("c")
@@ -126,6 +179,7 @@
     length = groups * nyh * step
     acts_t[...] = acts[...].T
     acts_t_other[...] = acts_other[...].T
+    writes = []
     for j, cols in enumerate(columns(half)):
         place = pl.ds(pl.multiple_of(core * half + j * chunk, chunk), chunk)
         mean, inv_std = pooled(moments[:, 8 * j : 8 * j + 8], 2 * rows)
@@ -160,9 +214,10 @@
                 ]
                 out[piece, :length] = jnp.concatenate(rows_of, axis=0).astype(bf16)
                 out[piece, length:] = last.astype(bf16)
-
-
-def act_kernel(grad_conv, grad_conv_other, weight, act, act_other, squares):
+        ready = pl.ds(j * nx * nyl, nx * nyl)
+        writes.append(pltpu.make_async_copy(out.at[ready], result_out.at[ready], sems.at[j]))
+        writes[-1].start()
+
     dims = (((1,), (1,)), ((), ()))
     act[...] = lax.dot_general(grad_conv[...], weight[...], dims, preferred_element_type=f32)
     act_other[...] = lax.dot_general(
@@ -170,9 +225,11 @@
     ).astype(bf16)
     total = jnp.zeros((8, lanes), f32)
     for cols in columns(weight.shape[1]):
-        wide = weight[:, cols].astype(f32)
-        total += sum(fold(jnp.sum((wide * wide).reshape(-1, 8, chunk), axis=0)))
+        value = weight[:, cols].astype(f32)
+        total += sum(fold(jnp.sum((value * value).reshape(-1, 8, chunk), axis=0)))
     squares[...] = total
+    for write in writes:
+        write.wait()
 
 
 def near_kernel(nyh, received, out, total):
@@ -278,12 +335,19 @@
     return pltpu.CompilerParams(vmem_limit_bytes=mib << 20)
 
 
-def call(kernel, name, operands, outs, scratch=()):
+def call(kernel, name, operands, outs, scratch=(), loaded=0, written=None):
+    anywhere = pl.BlockSpec(memory_space=pl.ANY)
+    at = len(operands) - loaded
+    in_specs = [whole(value.shape) for value in operands[:at]] + [anywhere] * loaded
+    out_specs = [whole(out.shape) for out in outs]
+    if written is not None:
+        out_specs.append(anywhere)
+        outs = [*outs, pltpu.HBM(written.shape, written.dtype)]
     return pl.pallas_call(
         kernel,
         grid=(1,),
-        in_specs=[whole(value.shape) for value in operands],
-        out_specs=[whole(out.shape) for out in outs],
+        in_specs=in_specs,
+        out_specs=out_specs,
         out_shape=outs,
         scratch_shapes=scratch,
         compiler_params=params(),
@@ -305,8 +369,14 @@
     def other_half(value):
         return jnp.where(first_core, value[:, half:], value[:, :half])
 
-    pieces = jnp.stack([conv_weight[:, :half], conv_weight[:, half:]])
-    pieces = jnp.broadcast_to(pieces[None], (ny, 2, part, half)).reshape(members, part, half)
+    (pieces,) = call(
+        pieces_kernel,
+        "pieces",
+        (conv_weight,),
+        [],
+        [pltpu.SemaphoreType.DMA((members,))],
+        written=shape((members, part, half), bf16),
+    )
     weight = exchange(pieces, bn).reshape(cin, half)
     acts_other = swap(activations)
     block_other = swap(other_half(block_input))
@@ -324,27 +394,27 @@
     grad, grad_other, stats = call(
         stats_kernel,
         "stats",
-        (conv, conv_other, moments, gain, shift, block_input, block_other, out_grad, out_other),
+        (conv, conv_other, moments, gain, shift, block_input, out_grad, block_other, out_other),
         [narrow, narrow, sums],
+        [pltpu.VMEM((rows, half), bf16)] * 2 + [pltpu.SemaphoreType.DMA((2,))],
+        loaded=2,
     )
     stats = exchange(stats, y_axes)
     count = nzl * nx * nyl
     step = 2 * part // nx
     length = groups * nyh * step
-    grad_conv, grad_conv_other, partial = call(
+    act, act_other, weight_squares, partial = call(
         functools.partial(weight_kernel, (nx, nyl, nyh)),
         "weight_partial",
-        (conv, conv_other, moments, stats, gain, grad, grad_other, activations, acts_other),
-        [narrow, narrow, shape((count, length + 16, lanes), bf16)],
-        [pltpu.VMEM((cin, chunk), f32)] + [pltpu.VMEM((cin, rows), bf16)] * 2,
-    )
-    act, act_other, weight_squares = call(
-        act_kernel,
-        "act_grad",
-        (grad_conv, grad_conv_other, weight),
+        (conv, conv_other, moments, stats, gain, grad, grad_other, activations, acts_other, weight),
         [shape((rows, cin), f32), shape((rows, cin), bf16), shape((8, lanes), f32)],
-    )
-    partial, act_other = lax.optimization_barrier((partial, act_other))
+        [pltpu.VMEM((cin, chunk), f32)]
+        + [pltpu.VMEM((cin, rows), bf16)] * 2
+        + [pltpu.VMEM((rows, half), bf16)] * 2
+        + [pltpu.VMEM((count, length + 16, lanes), bf16)]
+        + [pltpu.SemaphoreType.DMA((half // chunk,))],
+        written=shape((count, length + 16, lanes), bf16),
+    )
     act_grad = (act + swap(act_other).astype(f32)).astype(bf16)
     partial, act_grad = lax.optimization_barrier((exchange(partial, near), act_grad))
 

time: 143 us -> 141 us (0.986)
  no operation moved by 1% of the time
where the time goes in v9:
time: 141 us; the launch traced here: 140 us
  blocking collectives  64.6 us (46%)
  starting transfers between devices  33.7 us (24%)
  waiting for transfers between devices  27.8 us (20%)
  Pallas kernels  8.16 us (6%)
  other arithmetic  4.33 us (3%)
    all_to_all x5, blocking collectives, exchange(): return lax.all_to_all(pieces, axis, 0, 0, tiled=True)  64.6 us
    all_to_all x2, waiting for transfers between devices, exchange(): return lax.all_to_all(pieces, axis, 0, 0, tiled=True)  25 us
    ppermute x5, starting transfers between devices, swap(): return lax.ppermute(value, 'c', [(0, 1), (1, 0)])  19.2 us
    all_to_all x2, starting transfers between devices, exchange(): return lax.all_to_all(pieces, axis, 0, 0, tiled=True)  14.6 us
    pallas_call x8, Pallas kernels, call(): pl.pallas_call(kernel, grid=(1,), in_specs=in_specs, out_specs=out_specs,...  8.16 us
    select_n x2, other arithmetic, other_half(): return jnp.where(first_core, value[:, half:], value[:, :half])  3.46 us
    ppermute x5, waiting for transfers between devices, swap(): return lax.ppermute(value, 'c', [(0, 1), (1, 0)])  2.83 us
  transfers between devices with their start and end apart: 7, of which 4 were waited for; matrix products, arithmetic and copies ran while one was open for 3% of the time, Pallas kernels for 1%

profile of v9, /device:TPU:1, one launch (start us, length us, event | category | flops | bytes accessed | tf_op | source)
XLA Modules:
  0.0 140.4 jit_solution(13444284805470403420)
XLA Ops:
  0.6 0.0 copy-start.3
  0.6 0.9 copy-done.3
  1.5 1.1 pieces.1
  2.7 10.3 %all-to-all-start = ((bf16[16,32,1024]{2,1,0:T(8,128)(2,1)}), bf16[16,32,1024]{2,1,0:T(8,128)(2,1)S(1)}, u32[]{:S(2)}, u32[]{:S(2)}) async-start(bf16[16,32,1024]{2,1,0:T(8,128)(2,1)} %pieces.1), calls=%async_computation | async-start | bytes 2097152 | tf_op jit(solution)/shard_map/all_to_all | solution.py:29
  13.0 2.5 %slice_select_fusion = bf16[392,1024]{1,0:T(8,128)(2,1)} fusion(bf16[392,2048]{1,0:T(8,128)(2,1)} %out.1, pred[]{:T(512)S(6)} %eq.3), kind=kLoop, calls=%fused_computation.1 | loop fusion | flops 401408 | bytes 2408449 | tf_op jit(solution)/shard_map/jit(_where)/select_n | solution.py:370
  15.5 2.3 %collective-permute-start.2 = (bf16[392,1024]{1,0:T(8,128)(2,1)}, bf16[392,1024]{1,0:T(8,128)(2,1)}, u32[]{:S(2)}, u32[]{:S(2)}) collective-permute-start(bf16[392,1024]{1,0:T(8,128)(2,1)} %slice_select_fusion), channel_id=1, source_target_pairs={{0,1},{1,0},{2,3},{3,2},{4,5},{5,4},{6,7},{7,6},{8,9},{9,8},{10,11... | collective-permute-start | bytes 2408456 | tf_op jit(solution)/shard_map/ppermute | solution.py:25
  17.8 1.0 slice_select_fusion.1
  18.8 2.2 %collective-permute-start.1 = (bf16[392,1024]{1,0:T(8,128)(2,1)}, bf16[392,1024]{1,0:T(8,128)(2,1)}, u32[]{:S(2)}, u32[]{:S(2)}) collective-permute-start(bf16[392,1024]{1,0:T(8,128)(2,1)} %slice_select_fusion.1), channel_id=1, source_target_pairs={{0,1},{1,0},{2,3},{3,2},{4,5},{5,4},{6,7},{7,6},{8,9},{9,8},{10,11... | collective-permute-start | bytes 2408456 | tf_op jit(solution)/shard_map/ppermute | solution.py:25
  21.0 2.1 %collective-permute-start = (bf16[392,512]{1,0:T(8,128)(2,1)S(1)}, bf16[392,512]{1,0:T(8,128)(2,1)S(1)}, u32[]{:S(2)}, u32[]{:S(2)}) collective-permute-start(bf16[392,512]{1,0:T(8,128)(2,1)S(1)} %copy-done.2), channel_id=1, source_target_pairs={{0,1},{1,0},{2,3},{3,2},{4,5},{5,4},{6,7},{7,6},{8,9},{9,8},{10,11... | collective-permute-start | bytes 1204232 | tf_op jit(solution)/shard_map/ppermute | solution.py:25
  23.1 1.5 %collective-permute-done.acts_other = bf16[392,512]{1,0:T(8,128)(2,1)S(1)} collective-permute-done((bf16[392,512]{1,0:T(8,128)(2,1)S(1)}, bf16[392,512]{1,0:T(8,128)(2,1)S(1)}, u32[]{:S(2)}, u32[]{:S(2)}) %collective-permute-start) | collective-permute-done | bytes 401440 | tf_op jit(solution)/shard_map/ppermute | solution.py:25
  24.6 16.4 %all-to-all-done = bf16[16,32,1024]{2,1,0:T(8,128)(2,1)S(1)} async-done(((bf16[16,32,1024]{2,1,0:T(8,128)(2,1)}), bf16[16,32,1024]{2,1,0:T(8,128)(2,1)S(1)}, u32[]{:S(2)}, u32[]{:S(2)}) %all-to-all-start) | async-done | bytes 1048608 | tf_op jit(solution)/shard_map/all_to_all | solution.py:29
  41.0 1.4 %moments.1 = (f32[392,1024]{1,0:T(8,128)S(1)}, f32[392,1024]{1,0:T(8,128)S(1)}, f32[8,16,128]{2,1,0:T(8,128)S(1)}) custom-call(bf16[392,512]{1,0:T(8,128)(2,1)S(1)} %copy-done.2, bf16[392,512]{1,0:T(8,128)(2,1)S(1)} %collective-permute-done.acts_other, bf16[512,1024]{1,0:T(8,128)(2,1)S(1)} %bitcast.5), custom_call_target="tpu_custom_call" | custom-call | tf_op jit(solution)/shard_map/moments/pallas_call | solution.py:346
  42.4 0.0 collective-permute-done.2.out_far
  42.4 0.0 collective-permute-done.1.block_far
  42.4 9.8 %all_to_all.35.moments = f32[8,16,128]{2,1,0:T(8,128)S(1)} all-to-all(f32[8,16,128]{2,1,0:T(8,128)S(1)} %get-tuple-element.31), channel_id=1, replica_groups=mesh['zh'=4,'zl'=2,'x'=4,'yh'=4,'yl'=2,'c'=2] {'yh','yl'}, dimensions={0} | all-to-all | bytes 131072 | tf_op jit(solution)/shard_map/all_to_all | solution.py:29
  52.3 2.0 %stats.1 = (bf16[392,1024]{1,0:T(8,128)(2,1)S(1)}, bf16[392,1024]{1,0:T(8,128)(2,1)S(1)}, f32[8,16,128]{2,1,0:T(8,128)S(1)}) custom-call(f32[392,1024]{1,0:T(8,128)S(1)} %get-tuple-element.28.conv, f32[392,1024]{1,0:T(8,128)S(1)} %get-tuple-element.29.conv_other, f32[8,16,128]{2,1,0:T(8,128)S(1)} %all_to_all.35.moments, f32[1,2048]{1,0:T(1,128)S(1)} %bitcast.7, ...), custom_call_target="tpu_custom_call" | custom-call | tf_op jit(solution)/shard_map/stats/pallas_call | solution.py:346
  54.3 9.7 %all_to_all.36.stats = f32[8,16,128]{2,1,0:T(8,128)S(1)} all-to-all(f32[8,16,128]{2,1,0:T(8,128)S(1)} %get-tuple-element.34), channel_id=1, replica_groups=mesh['zh'=4,'zl'=2,'x'=4,'yh'=4,'yl'=2,'c'=2] {'yh','yl'}, dimensions={0} | all-to-all | bytes 131072 | tf_op jit(solution)/shard_map/all_to_all | solution.py:29
  64.0 2.3 %weight_partial.1 = (f32[392,512]{1,0:T(8,128)S(1)}, bf16[392,512]{1,0:T(8,128)(2,1)S(1)}, f32[8,128]{1,0:T(8,128)S(1)}, bf16[16,272,128]{2,1,0:T(8,128)(2,1)}) custom-call(f32[392,1024]{1,0:T(8,128)S(1)} %get-tuple-element.28.conv, f32[392,1024]{1,0:T(8,128)S(1)} %get-tuple-element.29.conv_other, f32[8,16,128]{2,1,0:T(8,128)S(1)} %all_to_all.35.moments, ...), custom_call_target="tpu_custom_call" | custom-call | tf_op jit(solution)/shard_map/weight_partial/pallas_call | solution.py:346
  66.3 4.2 %all-to-all-start.3 = ((bf16[16,272,128]{2,1,0:T(8,128)(2,1)}), bf16[16,272,128]{2,1,0:T(8,128)(2,1)S(1)}, u32[]{:S(2)}, u32[]{:S(2)}) async-start(bf16[16,272,128]{2,1,0:T(8,128)(2,1)} %get-tuple-element.37), calls=%async_computation.3 | async-start | bytes 2228224 | tf_op jit(solution)/shard_map/all_to_all | solution.py:29
  70.5 5.1 %collective-permute-start.3 = (bf16[392,512]{1,0:T(8,128)(2,1)S(1)}, bf16[392,512]{1,0:T(8,128)(2,1)S(1)}, u32[]{:S(2)}, u32[]{:S(2)}) collective-permute-start(bf16[392,512]{1,0:T(8,128)(2,1)S(1)} %get-tuple-element.39), channel_id=1, source_target_pairs={{0,1},{1,0},{2,3},{3,2},{4,5},{5,4},{6,7},{7,6},{8,9},{9,8},{10,11... | collective-permute-start | bytes 1204232 | tf_op jit(solution)/shard_map/ppermute | solution.py:25
  75.6 1.3 collective-permute-done.3
  76.9 0.9 add_convert_fusion
  77.8 8.6 %all-to-all-done.3.received = bf16[16,272,128]{2,1,0:T(8,128)(2,1)S(1)} async-done(((bf16[16,272,128]{2,1,0:T(8,128)(2,1)}), bf16[16,272,128]{2,1,0:T(8,128)(2,1)S(1)}, u32[]{:S(2)}, u32[]{:S(2)}) %all-to-all-start.3) | async-done | bytes 1114144 | tf_op jit(solution)/shard_map/all_to_all | solution.py:29
  86.4 0.2 near_sum.1
  86.6 21.4 %all_to_all.37.received = bf16[16,24,128]{2,1,0:T(8,128)(2,1)S(1)} all-to-all(bf16[16,24,128]{2,1,0:T(8,128)(2,1)S(1)} %near_sum.1), channel_id=1, replica_groups=mesh['zh'=4,'zl'=2,'x'=4,'yh'=4,'yl'=2,'c'=2] {'zh','yh'}, dimensions={0} | all-to-all | bytes 196608 | tf_op jit(solution)/shard_map/all_to_all | solution.py:29
  108.0 0.1 far_sum.1
  108.1 13.1 %all_to_all.38.parts = bf16[32,24,128]{2,1,0:T(8,128)(2,1)S(1)} all-to-all(bf16[32,24,128]{2,1,0:T(8,128)(2,1)S(1)} %far_sum.1), channel_id=1, replica_groups=mesh['zh'=4,'zl'=2,'x'=4,'yh'=4,'yl'=2,'c'=2] {'zh','zl','x'}, dimensions={0} | all-to-all | bytes 393216 | tf_op jit(solution)/shard_map/all_to_all | solution.py:29
  121.2 0.1 split.1
  121.3 7.5 %collective-permute-start.4 = (f32[40,1024]{1,0:T(8,128)S(1)}, f32[40,1024]{1,0:T(8,128)S(1)}, u32[]{:S(2)}, u32[]{:S(2)}) collective-permute-start(f32[40,1024]{1,0:T(8,128)S(1)} %get-tuple-element.43), channel_id=1, source_target_pairs={{0,1},{1,0},{2,3},{3,2},{4,5},{5,4},{6,7},{7,6},{8,9},{9,8},{10,11... | collective-permute-start | bytes 491528 | tf_op jit(solution)/shard_map/ppermute | solution.py:25
  128.9 10.6 %all_to_all.39.squares = f32[16,8,128]{2,1,0:T(8,128)S(1)} all-to-all(f32[16,8,128]{2,1,0:T(8,128)S(1)} %get-tuple-element.44), channel_id=1, replica_groups=mesh['zh'=4,'zl'=2,'x'=4,'yh'=4,'yl'=2,'c'=2] {'yh','yl','c'}, dimensions={0} | all-to-all | bytes 131072 | tf_op jit(solution)/shard_map/all_to_all | solution.py:29
  139.5 0.0 collective-permute-done.4.arrived
  139.5 0.8 step.1
  (14 shorter events, 0.0 us)
Async XLA Ops:
  0.6 0.9 copy-start.3
  2.7 38.3 %all-to-all-start = ((bf16[16,32,1024]{2,1,0:T(8,128)(2,1)}), bf16[16,32,1024]{2,1,0:T(8,128)(2,1)S(1)}, u32[]{:S(2)}, u32[]{:S(2)}) async-start(bf16[16,32,1024]{2,1,0:T(8,128)(2,1)} %pieces.1), calls=%async_computation | async-start | bytes 2097152 | tf_op jit(solution)/shard_map/all_to_all | solution.py:29
  13.0 4.8 %copy-start = (bf16[392,2048]{1,0:T(8,128)(2,1)S(1)}, bf16[392,2048]{1,0:T(8,128)(2,1)}, u32[]{:S(2)}) copy-start(bf16[392,2048]{1,0:T(8,128)(2,1)} %block.1) | copy-start | bytes 4816900
  15.5 5.4 %copy-start.2 = (bf16[392,512]{1,0:T(8,128)(2,1)S(1)}, bf16[392,512]{1,0:T(8,128)(2,1)}, u32[]{:S(2)}) copy-start(bf16[392,512]{1,0:T(8,128)(2,1)} %acts.3) | copy-start | bytes 1204228
  15.5 36.8 %copy-start.6 = (f32[2048]{0:T(1024)S(1)}, f32[2048]{0:T(1024)}, u32[]{:S(2)}) copy-start(f32[2048]{0:T(1024)} %param.10) | copy-start | bytes 24580
  15.5 36.8 %copy-start.7 = (f32[2048]{0:T(1024)S(1)}, f32[2048]{0:T(1024)}, u32[]{:S(2)}) copy-start(f32[2048]{0:T(1024)} %param.11) | copy-start | bytes 24580
  15.5 26.9 %collective-permute-start.2 = (bf16[392,1024]{1,0:T(8,128)(2,1)}, bf16[392,1024]{1,0:T(8,128)(2,1)}, u32[]{:S(2)}, u32[]{:S(2)}) collective-permute-start(bf16[392,1024]{1,0:T(8,128)(2,1)} %slice_select_fusion), channel_id=1, source_target_pairs={{0,1},{1,0},{2,3},{3,2},{4,5},{5,4},{6,7},{7,6},{8,9},{9,8},{10,11... | collective-permute-start | bytes 2408456 | tf_op jit(solution)/shard_map/ppermute | solution.py:25
  18.8 23.7 %collective-permute-start.1 = (bf16[392,1024]{1,0:T(8,128)(2,1)}, bf16[392,1024]{1,0:T(8,128)(2,1)}, u32[]{:S(2)}, u32[]{:S(2)}) collective-permute-start(bf16[392,1024]{1,0:T(8,128)(2,1)} %slice_select_fusion.1), channel_id=1, source_target_pairs={{0,1},{1,0},{2,3},{3,2},{4,5},{5,4},{6,7},{7,6},{8,9},{9,8},{10,11... | collective-permute-start | bytes 2408456 | tf_op jit(solution)/shard_map/ppermute | solution.py:25
  21.0 3.6 %collective-permute-start = (bf16[392,512]{1,0:T(8,128)(2,1)S(1)}, bf16[392,512]{1,0:T(8,128)(2,1)S(1)}, u32[]{:S(2)}, u32[]{:S(2)}) collective-permute-start(bf16[392,512]{1,0:T(8,128)(2,1)S(1)} %copy-done.2), channel_id=1, source_target_pairs={{0,1},{1,0},{2,3},{3,2},{4,5},{5,4},{6,7},{7,6},{8,9},{9,8},{10,11... | collective-permute-start | bytes 1204232 | tf_op jit(solution)/shard_map/ppermute | solution.py:25
  41.0 11.3 %copy-start.1 = (bf16[392,2048]{1,0:T(8,128)(2,1)S(1)}, bf16[392,2048]{1,0:T(8,128)(2,1)}, u32[]{:S(2)}) copy-start(bf16[392,2048]{1,0:T(8,128)(2,1)} %out.1) | copy-start | bytes 4816900
  66.3 20.1 %all-to-all-start.3 = ((bf16[16,272,128]{2,1,0:T(8,128)(2,1)}), bf16[16,272,128]{2,1,0:T(8,128)(2,1)S(1)}, u32[]{:S(2)}, u32[]{:S(2)}) async-start(bf16[16,272,128]{2,1,0:T(8,128)(2,1)} %get-tuple-element.37), calls=%async_computation.3 | async-start | bytes 2228224 | tf_op jit(solution)/shard_map/all_to_all | solution.py:29
  70.5 6.4 %collective-permute-start.3 = (bf16[392,512]{1,0:T(8,128)(2,1)S(1)}, bf16[392,512]{1,0:T(8,128)(2,1)S(1)}, u32[]{:S(2)}, u32[]{:S(2)}) collective-permute-start(bf16[392,512]{1,0:T(8,128)(2,1)S(1)} %get-tuple-element.39), channel_id=1, source_target_pairs={{0,1},{1,0},{2,3},{3,2},{4,5},{5,4},{6,7},{7,6},{8,9},{9,8},{10,11... | collective-permute-start | bytes 1204232 | tf_op jit(solution)/shard_map/ppermute | solution.py:25
  77.8 61.7 %copy-start.4 = (bf16[32,2048]{1,0:T(8,128)(2,1)S(1)}, bf16[32,2048]{1,0:T(8,128)(2,1)}, u32[]{:S(2)}) copy-start(bf16[32,2048]{1,0:T(8,128)(2,1)} %weight.3) | copy-start | bytes 393220
  77.8 61.7 %copy-start.5 = (f32[32,2048]{1,0:T(8,128)S(1)}, f32[32,2048]{1,0:T(8,128)}, u32[]{:S(2)}) copy-start(f32[32,2048]{1,0:T(8,128)} %velocity.1) | copy-start | bytes 786436
  121.3 18.2 %collective-permute-start.4 = (f32[40,1024]{1,0:T(8,128)S(1)}, f32[40,1024]{1,0:T(8,128)S(1)}, u32[]{:S(2)}, u32[]{:S(2)}) collective-permute-start(f32[40,1024]{1,0:T(8,128)S(1)} %get-tuple-element.43), channel_id=1, source_target_pairs={{0,1},{1,0},{2,3},{3,2},{4,5},{5,4},{6,7},{7,6},{8,9},{9,8},{10,11... | collective-permute-start | bytes 491528 | tf_op jit(solution)/shard_map/ppermute | solution.py:25

commit v10 on v9

--- a/solution.py
+++ b/solution.py
@@ -233,64 +233,58 @@
 
 
 def near_kernel(nyh, received, out, total):
-    count, depth, _ = out.shape
-    step = depth - 8
     total[...] = jnp.sum(received[...].astype(f32), axis=0)
-    for zh in range(count // nyh):
-        base = count * step + zh
-        high, low = high_low(total[base : base + 1, :])
-        extra = jnp.concatenate([high, low, jnp.zeros((6, lanes), f32)], axis=0)
-        for yh in range(nyh):
-            at = (zh * nyh + yh) * step
-            tile = jnp.concatenate([total[at : at + step, :], extra], axis=0)
-            out[zh * nyh + yh] = tile.astype(bf16)
+    length = total.shape[0] - 16
+    step = length // (groups * nyh)
+    tail = high_low(total[length : length + groups, :])
+    for yh in range(nyh):
+        starts = [(q * nyh + yh) * step for q in range(groups)]
+        own = [total[at : at + step, :] for at in starts]
+        tile = jnp.concatenate([*own, *tail], axis=0).astype(bf16)
+        for zh in range(out.shape[0] // nyh):
+            out[zh * nyh + yh] = tile
 
 
 def far_kernel(received, out):
     total = jnp.sum(received[...].astype(f32), axis=0)
-    step = total.shape[0] - 8
-    value = total[:step]
+    at = total.shape[0] - 2 * groups
+    value = total[:at]
     square = jnp.sum(jnp.sum(value * value, axis=0, keepdims=True), axis=1, keepdims=True)
     square = jnp.broadcast_to(square, (1, lanes))
-    tail = total[step : step + 1] + total[step + 1 : step + 2]
-    tile = [value, *high_low(tail), *high_low(square), jnp.zeros((4, lanes), f32)]
+    tail = total[at : at + groups] + total[at + groups :]
+    tile = [value, *high_low(tail), *high_low(square), jnp.zeros((6, lanes), f32)]
     tile = jnp.concatenate(tile, axis=0).astype(bf16)
     out[...] = jnp.broadcast_to(tile[None], out.shape)
 
 
-def places(sizes):
-    nzh, nzl, nx = sizes
-    return [
-        ((zh * nzl + zl) * nx, pl.ds((zl * nzh + zh) * lanes, lanes))
-        for zh in range(nzh)
-        for zl in range(nzl)
-    ]
-
-
-def owned(parts, first, owner, count):
+def places(parts, nx):
+    for zl in range(parts.shape[0] // nx):
+        values = [parts[zl * nx + x].astype(f32) for x in range(nx)]
+        for q in range(groups):
+            yield zl * nx, q, pl.ds((zl * groups + q) * lanes, lanes), values
+
+
+def owned(parts, first, q, owner, count):
     values = [parts[first + owner * count + i].astype(f32) for i in range(count)]
-    return jnp.concatenate([v[: v.shape[0] - 8] for v in values], axis=0)
-
-
-def sums_of(parts, first, nx):
-    planes = []
-    for x in range(nx):
-        value = parts[first + x].astype(f32)
-        at = value.shape[0] - 8
-        planes.append(value[at : at + 1] + value[at + 1 : at + 2])
+    step = (values[0].shape[0] - 16) // groups
+    return jnp.concatenate([v[q * step : (q + 1) * step] for v in values], axis=0)
+
+
+def sums_of(values, q):
+    at = values[0].shape[0] - 16 + q
+    planes = [v[at : at + 1] + v[at + groups : at + groups + 1] for v in values]
     return planes[0] + planes[1], planes[2] + planes[3]
 
 
-def split_kernel(sizes, parts, weight_squares, theirs, squares):
-    nx = sizes[2]
+def split_kernel(nx, parts, weight_squares, theirs, squares):
     other = 1 - lax.axis_index("c")
     part = theirs.shape[0] - 8
-    for first, cols in places(sizes):
-        theirs[:part, cols] = owned(parts, first, other, nx // 2)
-        shift, gain = sums_of(parts, first, nx)
+    for first, q, cols, values in places(parts, nx):
+        theirs[:part, cols] = owned(parts, first, q, other, nx // 2)
+        shift, gain = sums_of(values, q)
         theirs[part:, cols] = jnp.concatenate([shift, gain, jnp.zeros((6, lanes), f32)], axis=0)
     total = jnp.sum(parts[...].astype(f32), axis=0)
-    at = total.shape[0] - 6
+    at = total.shape[0] - 8
     square = total[at : at + 1] + total[at + 1 : at + 2]
     weight_square = jnp.sum(weight_squares[...], axis=0, keepdims=True)
     weight_square = jnp.sum(weight_square, axis=1, keepdims=True)
@@ -299,8 +293,7 @@
     squares[...] = jnp.broadcast_to(tile[None], squares.shape)
 
 
-def step_kernel(sizes, parts, arrived, squares, weight, velocity, out, gain, shift):
-    nx = sizes[2]
+def step_kernel(nx, parts, arrived, squares, weight, velocity, out, gain, shift):
     core = lax.axis_index("c")
     part, cout = out.shape
     half = cout // 2
@@ -313,12 +306,12 @@
         decayed = weight_grad + weight_decay * weight[:, cols].astype(f32)
         out[:, cols] = momentum * velocity[:, cols] + ratio * decayed
 
-    for first, cols in places(sizes):
+    for first, q, cols, values in places(parts, nx):
         here = pl.ds(pl.multiple_of(core * half + cols.start, lanes), lanes)
         there = pl.ds(pl.multiple_of((1 - core) * half + cols.start, lanes), lanes)
-        update(here, owned(parts, first, core, nx // 2))
+        update(here, owned(parts, first, q, core, nx // 2))
         update(there, arrived[:part, cols])
-        shift[:, here], gain[:, here] = sums_of(parts, first, nx)
+        shift[:, here], gain[:, here] = sums_of(values, q)
         last = arrived[part:, cols]
         shift[:, there], gain[:, there] = last[:1], last[1:2]
 
@@ -359,7 +352,7 @@
     rows, cin = activations.shape
     part, cout = conv_weight.shape
     half = cout // 2
-    nzh, nzl, nx = sizes = tuple(lax.axis_size(a) for a in rep)
+    nzh, nzl, nx = (lax.axis_size(a) for a in rep)
     nyh, nyl = (lax.axis_size(a) for a in y_axes)
     ny = nyh * nyl
     members = 2 * ny
@@ -375,6 +368,7 @@
         (conv_weight,),
         [],
         [pltpu.SemaphoreType.DMA((members,))],
+        loaded=1,
         written=shape((members, part, half), bf16),
     )
     weight = exchange(pieces, bn).reshape(cin, half)
@@ -422,18 +416,18 @@
         functools.partial(near_kernel, nyh),
         "near_sum",
         (partial,),
-        [shape((nzh * nyh, step + 8, lanes), bf16)],
+        [shape((nzh * nyh, groups * (step + 2), lanes), bf16)],
         [pltpu.VMEM((length + 16, lanes), f32)],
     )
     (ready,) = call(
         far_kernel,
         "far_sum",
         (exchange(partial, far),),
-        [shape((nzh * nzl * nx, step + 8, lanes), bf16)],
-    )
-    ready = exchange(ready, rep)
+        [shape((nzl * nx, groups * step + 16, lanes), bf16)],
+    )
+    ready = exchange(ready, ("zl", "x"))
     theirs, squares = call(
-        functools.partial(split_kernel, sizes),
+        functools.partial(split_kernel, nx),
         "split",
         (ready, weight_squares),
         [shape((part + 8, half), f32), shape((members, 8, lanes), f32)],
@@ -441,7 +435,7 @@
     arrived = swap(theirs)
     squares = exchange(squares, bn)
     new_velocity, gain_grad, shift_grad = call(
-        functools.partial(step_kernel, sizes),
+        functools.partial(step_kernel, nx),
         "step",
         (ready, arrived, squares, conv_weight, velocity),
         [shape((part, cout), f32), shape((1, cout), f32), shape((1, cout), f32)],

time: 141 us -> 137 us (0.972)
  blocking collectives: 64.6 us -> 62.2 us
    all_to_all x5, blocking collectives: 64.6 us -> 62.2 us  [exchange(): return lax.all_to_all(pieces, axis, 0, 0, tiled=True)]
where the time goes in v10:
time: 137 us
  blocking collectives  62.2 us (45%)
  starting transfers between devices  32.5 us (24%)
  waiting for transfers between devices  27.8 us (20%)
  Pallas kernels  8.16 us (6%)
  other arithmetic  4.33 us (3%)
    all_to_all x5, blocking collectives, exchange(): return lax.all_to_all(pieces, axis, 0, 0, tiled=True)  62.2 us
    all_to_all x2, waiting for transfers between devices, exchange(): return lax.all_to_all(pieces, axis, 0, 0, tiled=True)  25 us
    ppermute x5, starting transfers between devices, swap(): return lax.ppermute(value, 'c', [(0, 1), (1, 0)])  17.9 us
    all_to_all x2, starting transfers between devices, exchange(): return lax.all_to_all(pieces, axis, 0, 0, tiled=True)  14.6 us
    pallas_call x8, Pallas kernels, call(): pl.pallas_call(kernel, grid=(1,), in_specs=in_specs, out_specs=out_specs,...  8.16 us
    select_n x2, other arithmetic, other_half(): return jnp.where(first_core, value[:, half:], value[:, :half])  3.46 us
    ppermute x5, waiting for transfers between devices, swap(): return lax.ppermute(value, 'c', [(0, 1), (1, 0)])  2.83 us
  transfers between devices with their start and end apart: 7, of which 4 were waited for; matrix products, arithmetic and copies ran while one was open for 3% of the time, Pallas kernels for 1%

profile of v10, /device:TPU:1, one launch (start us, length us, event | category | flops | bytes accessed | tf_op | source)
XLA Modules:
  0.0 136.6 jit_solution(16845510437569127633)
XLA Ops:
  0.6 0.0 copy-start.3
  0.6 0.9 copy-done.3
  1.5 1.1 pieces.1
  2.7 10.3 %all-to-all-start = ((bf16[16,32,1024]{2,1,0:T(8,128)(2,1)}), bf16[16,32,1024]{2,1,0:T(8,128)(2,1)S(1)}, u32[]{:S(2)}, u32[]{:S(2)}) async-start(bf16[16,32,1024]{2,1,0:T(8,128)(2,1)} %pieces.1), calls=%async_computation | async-start | bytes 2097152 | tf_op jit(solution)/shard_map/all_to_all | solution.py:29
  13.0 2.5 %slice_select_fusion = bf16[392,1024]{1,0:T(8,128)(2,1)} fusion(bf16[392,2048]{1,0:T(8,128)(2,1)} %out.1, pred[]{:T(512)S(6)} %eq.3), kind=kLoop, calls=%fused_computation.1 | loop fusion | flops 401408 | bytes 2408449 | tf_op jit(solution)/shard_map/jit(_where)/select_n | solution.py:363
  15.5 2.3 %collective-permute-start.2 = (bf16[392,1024]{1,0:T(8,128)(2,1)}, bf16[392,1024]{1,0:T(8,128)(2,1)}, u32[]{:S(2)}, u32[]{:S(2)}) collective-permute-start(bf16[392,1024]{1,0:T(8,128)(2,1)} %slice_select_fusion), channel_id=1, source_target_pairs={{0,1},{1,0},{2,3},{3,2},{4,5},{5,4},{6,7},{7,6},{8,9},{9,8},{10,11... | collective-permute-start | bytes 2408456 | tf_op jit(solution)/shard_map/ppermute | solution.py:25
  17.8 1.0 slice_select_fusion.1
  18.8 2.2 %collective-permute-start.1 = (bf16[392,1024]{1,0:T(8,128)(2,1)}, bf16[392,1024]{1,0:T(8,128)(2,1)}, u32[]{:S(2)}, u32[]{:S(2)}) collective-permute-start(bf16[392,1024]{1,0:T(8,128)(2,1)} %slice_select_fusion.1), channel_id=1, source_target_pairs={{0,1},{1,0},{2,3},{3,2},{4,5},{5,4},{6,7},{7,6},{8,9},{9,8},{10,11... | collective-permute-start | bytes 2408456 | tf_op jit(solution)/shard_map/ppermute | solution.py:25
  21.0 2.1 %collective-permute-start = (bf16[392,512]{1,0:T(8,128)(2,1)S(1)}, bf16[392,512]{1,0:T(8,128)(2,1)S(1)}, u32[]{:S(2)}, u32[]{:S(2)}) collective-permute-start(bf16[392,512]{1,0:T(8,128)(2,1)S(1)} %copy-done.2), channel_id=1, source_target_pairs={{0,1},{1,0},{2,3},{3,2},{4,5},{5,4},{6,7},{7,6},{8,9},{9,8},{10,11... | collective-permute-start | bytes 1204232 | tf_op jit(solution)/shard_map/ppermute | solution.py:25
  23.1 1.5 %collective-permute-done.acts_other = bf16[392,512]{1,0:T(8,128)(2,1)S(1)} collective-permute-done((bf16[392,512]{1,0:T(8,128)(2,1)S(1)}, bf16[392,512]{1,0:T(8,128)(2,1)S(1)}, u32[]{:S(2)}, u32[]{:S(2)}) %collective-permute-start) | collective-permute-done | bytes 401440 | tf_op jit(solution)/shard_map/ppermute | solution.py:25
  24.6 16.4 %all-to-all-done = bf16[16,32,1024]{2,1,0:T(8,128)(2,1)S(1)} async-done(((bf16[16,32,1024]{2,1,0:T(8,128)(2,1)}), bf16[16,32,1024]{2,1,0:T(8,128)(2,1)S(1)}, u32[]{:S(2)}, u32[]{:S(2)}) %all-to-all-start) | async-done | bytes 1048608 | tf_op jit(solution)/shard_map/all_to_all | solution.py:29
  41.0 1.4 %moments.1 = (f32[392,1024]{1,0:T(8,128)S(1)}, f32[392,1024]{1,0:T(8,128)S(1)}, f32[8,16,128]{2,1,0:T(8,128)S(1)}) custom-call(bf16[392,512]{1,0:T(8,128)(2,1)S(1)} %copy-done.2, bf16[392,512]{1,0:T(8,128)(2,1)S(1)} %collective-permute-done.acts_other, bf16[512,1024]{1,0:T(8,128)(2,1)S(1)} %bitcast.5), custom_call_target="tpu_custom_call" | custom-call | tf_op jit(solution)/shard_map/moments/pallas_call | solution.py:339
  42.4 0.0 collective-permute-done.2.out_far
  42.4 0.0 collective-permute-done.1.block_far
  42.4 9.8 %all_to_all.35.moments = f32[8,16,128]{2,1,0:T(8,128)S(1)} all-to-all(f32[8,16,128]{2,1,0:T(8,128)S(1)} %get-tuple-element.31), channel_id=1, replica_groups=mesh['zh'=4,'zl'=2,'x'=4,'yh'=4,'yl'=2,'c'=2] {'yh','yl'}, dimensions={0} | all-to-all | bytes 131072 | tf_op jit(solution)/shard_map/all_to_all | solution.py:29
  52.3 2.0 %stats.1 = (bf16[392,1024]{1,0:T(8,128)(2,1)S(1)}, bf16[392,1024]{1,0:T(8,128)(2,1)S(1)}, f32[8,16,128]{2,1,0:T(8,128)S(1)}) custom-call(f32[392,1024]{1,0:T(8,128)S(1)} %get-tuple-element.28.conv, f32[392,1024]{1,0:T(8,128)S(1)} %get-tuple-element.29.conv_other, f32[8,16,128]{2,1,0:T(8,128)S(1)} %all_to_all.35.moments, f32[1,2048]{1,0:T(1,128)S(1)} %bitcast.7, ...), custom_call_target="tpu_custom_call" | custom-call | tf_op jit(solution)/shard_map/stats/pallas_call | solution.py:339
  54.3 9.7 %all_to_all.36.stats = f32[8,16,128]{2,1,0:T(8,128)S(1)} all-to-all(f32[8,16,128]{2,1,0:T(8,128)S(1)} %get-tuple-element.34), channel_id=1, replica_groups=mesh['zh'=4,'zl'=2,'x'=4,'yh'=4,'yl'=2,'c'=2] {'yh','yl'}, dimensions={0} | all-to-all | bytes 131072 | tf_op jit(solution)/shard_map/all_to_all | solution.py:29
  64.0 2.3 %weight_partial.1 = (f32[392,512]{1,0:T(8,128)S(1)}, bf16[392,512]{1,0:T(8,128)(2,1)S(1)}, f32[8,128]{1,0:T(8,128)S(1)}, bf16[16,272,128]{2,1,0:T(8,128)(2,1)}) custom-call(f32[392,1024]{1,0:T(8,128)S(1)} %get-tuple-element.28.conv, f32[392,1024]{1,0:T(8,128)S(1)} %get-tuple-element.29.conv_other, f32[8,16,128]{2,1,0:T(8,128)S(1)} %all_to_all.35.moments, ...), custom_call_target="tpu_custom_call" | custom-call | tf_op jit(solution)/shard_map/weight_partial/pallas_call | solution.py:339
  66.3 4.2 %all-to-all-start.3 = ((bf16[16,272,128]{2,1,0:T(8,128)(2,1)}), bf16[16,272,128]{2,1,0:T(8,128)(2,1)S(1)}, u32[]{:S(2)}, u32[]{:S(2)}) async-start(bf16[16,272,128]{2,1,0:T(8,128)(2,1)} %get-tuple-element.37), calls=%async_computation.3 | async-start | bytes 2228224 | tf_op jit(solution)/shard_map/all_to_all | solution.py:29
  70.5 5.1 %collective-permute-start.3 = (bf16[392,512]{1,0:T(8,128)(2,1)S(1)}, bf16[392,512]{1,0:T(8,128)(2,1)S(1)}, u32[]{:S(2)}, u32[]{:S(2)}) collective-permute-start(bf16[392,512]{1,0:T(8,128)(2,1)S(1)} %get-tuple-element.39), channel_id=1, source_target_pairs={{0,1},{1,0},{2,3},{3,2},{4,5},{5,4},{6,7},{7,6},{8,9},{9,8},{10,11... | collective-permute-start | bytes 1204232 | tf_op jit(solution)/shard_map/ppermute | solution.py:25
  75.6 1.3 collective-permute-done.3
  76.9 0.9 add_convert_fusion
  77.8 8.6 %all-to-all-done.3.received = bf16[16,272,128]{2,1,0:T(8,128)(2,1)S(1)} async-done(((bf16[16,272,128]{2,1,0:T(8,128)(2,1)}), bf16[16,272,128]{2,1,0:T(8,128)(2,1)S(1)}, u32[]{:S(2)}, u32[]{:S(2)}) %all-to-all-start.3) | async-done | bytes 1114144 | tf_op jit(solution)/shard_map/all_to_all | solution.py:29
  86.4 0.2 near_sum.1
  86.6 23.2 %all_to_all.37.received = bf16[16,72,128]{2,1,0:T(8,128)(2,1)S(1)} all-to-all(bf16[16,72,128]{2,1,0:T(8,128)(2,1)S(1)} %near_sum.1), channel_id=1, replica_groups=mesh['zh'=4,'zl'=2,'x'=4,'yh'=4,'yl'=2,'c'=2] {'zh','yh'}, dimensions={0} | all-to-all | bytes 589824 | tf_op jit(solution)/shard_map/all_to_all | solution.py:29
  109.8 0.1 far_sum.1
  110.0 8.0 %all_to_all.38.parts = bf16[8,80,128]{2,1,0:T(8,128)(2,1)S(1)} all-to-all(bf16[8,80,128]{2,1,0:T(8,128)(2,1)S(1)} %far_sum.1), channel_id=1, replica_groups=mesh['zh'=4,'zl'=2,'x'=4,'yh'=4,'yl'=2,'c'=2] {'zl','x'}, dimensions={0} | all-to-all | bytes 327680 | tf_op jit(solution)/shard_map/all_to_all | solution.py:29
  118.0 0.1 split.1
  118.1 6.3 %collective-permute-start.4 = (f32[40,1024]{1,0:T(8,128)S(1)}, f32[40,1024]{1,0:T(8,128)S(1)}, u32[]{:S(2)}, u32[]{:S(2)}) collective-permute-start(f32[40,1024]{1,0:T(8,128)S(1)} %get-tuple-element.43), channel_id=1, source_target_pairs={{0,1},{1,0},{2,3},{3,2},{4,5},{5,4},{6,7},{7,6},{8,9},{9,8},{10,11... | collective-permute-start | bytes 491528 | tf_op jit(solution)/shard_map/ppermute | solution.py:25
  124.4 11.4 %all_to_all.39.squares = f32[16,8,128]{2,1,0:T(8,128)S(1)} all-to-all(f32[16,8,128]{2,1,0:T(8,128)S(1)} %get-tuple-element.44), channel_id=1, replica_groups=mesh['zh'=4,'zl'=2,'x'=4,'yh'=4,'yl'=2,'c'=2] {'yh','yl','c'}, dimensions={0} | all-to-all | bytes 131072 | tf_op jit(solution)/shard_map/all_to_all | solution.py:29
  135.8 0.0 collective-permute-done.4.arrived
  135.8 0.8 step.1
  (14 shorter events, 0.0 us)
Async XLA Ops:
  0.6 0.9 copy-start.3
  2.7 38.3 %all-to-all-start = ((bf16[16,32,1024]{2,1,0:T(8,128)(2,1)}), bf16[16,32,1024]{2,1,0:T(8,128)(2,1)S(1)}, u32[]{:S(2)}, u32[]{:S(2)}) async-start(bf16[16,32,1024]{2,1,0:T(8,128)(2,1)} %pieces.1), calls=%async_computation | async-start | bytes 2097152 | tf_op jit(solution)/shard_map/all_to_all | solution.py:29
  13.0 4.8 %copy-start = (bf16[392,2048]{1,0:T(8,128)(2,1)S(1)}, bf16[392,2048]{1,0:T(8,128)(2,1)}, u32[]{:S(2)}) copy-start(bf16[392,2048]{1,0:T(8,128)(2,1)} %block.1) | copy-start | bytes 4816900
  15.5 5.4 %copy-start.2 = (bf16[392,512]{1,0:T(8,128)(2,1)S(1)}, bf16[392,512]{1,0:T(8,128)(2,1)}, u32[]{:S(2)}) copy-start(bf16[392,512]{1,0:T(8,128)(2,1)} %acts.3) | copy-start | bytes 1204228
  15.5 36.8 %copy-start.6 = (f32[2048]{0:T(1024)S(1)}, f32[2048]{0:T(1024)}, u32[]{:S(2)}) copy-start(f32[2048]{0:T(1024)} %param.10) | copy-start | bytes 24580
  15.5 36.8 %copy-start.7 = (f32[2048]{0:T(1024)S(1)}, f32[2048]{0:T(1024)}, u32[]{:S(2)}) copy-start(f32[2048]{0:T(1024)} %param.11) | copy-start | bytes 24580
  15.5 26.9 %collective-permute-start.2 = (bf16[392,1024]{1,0:T(8,128)(2,1)}, bf16[392,1024]{1,0:T(8,128)(2,1)}, u32[]{:S(2)}, u32[]{:S(2)}) collective-permute-start(bf16[392,1024]{1,0:T(8,128)(2,1)} %slice_select_fusion), channel_id=1, source_target_pairs={{0,1},{1,0},{2,3},{3,2},{4,5},{5,4},{6,7},{7,6},{8,9},{9,8},{10,11... | collective-permute-start | bytes 2408456 | tf_op jit(solution)/shard_map/ppermute | solution.py:25
  18.8 23.7 %collective-permute-start.1 = (bf16[392,1024]{1,0:T(8,128)(2,1)}, bf16[392,1024]{1,0:T(8,128)(2,1)}, u32[]{:S(2)}, u32[]{:S(2)}) collective-permute-start(bf16[392,1024]{1,0:T(8,128)(2,1)} %slice_select_fusion.1), channel_id=1, source_target_pairs={{0,1},{1,0},{2,3},{3,2},{4,5},{5,4},{6,7},{7,6},{8,9},{9,8},{10,11... | collective-permute-start | bytes 2408456 | tf_op jit(solution)/shard_map/ppermute | solution.py:25
  21.0 3.6 %collective-permute-start = (bf16[392,512]{1,0:T(8,128)(2,1)S(1)}, bf16[392,512]{1,0:T(8,128)(2,1)S(1)}, u32[]{:S(2)}, u32[]{:S(2)}) collective-permute-start(bf16[392,512]{1,0:T(8,128)(2,1)S(1)} %copy-done.2), channel_id=1, source_target_pairs={{0,1},{1,0},{2,3},{3,2},{4,5},{5,4},{6,7},{7,6},{8,9},{9,8},{10,11... | collective-permute-start | bytes 1204232 | tf_op jit(solution)/shard_map/ppermute | solution.py:25
  41.0 11.3 %copy-start.1 = (bf16[392,2048]{1,0:T(8,128)(2,1)S(1)}, bf16[392,2048]{1,0:T(8,128)(2,1)}, u32[]{:S(2)}) copy-start(bf16[392,2048]{1,0:T(8,128)(2,1)} %out.1) | copy-start | bytes 4816900
  66.3 20.1 %all-to-all-start.3 = ((bf16[16,272,128]{2,1,0:T(8,128)(2,1)}), bf16[16,272,128]{2,1,0:T(8,128)(2,1)S(1)}, u32[]{:S(2)}, u32[]{:S(2)}) async-start(bf16[16,272,128]{2,1,0:T(8,128)(2,1)} %get-tuple-element.37), calls=%async_computation.3 | async-start | bytes 2228224 | tf_op jit(solution)/shard_map/all_to_all | solution.py:29
  70.5 6.4 %collective-permute-start.3 = (bf16[392,512]{1,0:T(8,128)(2,1)S(1)}, bf16[392,512]{1,0:T(8,128)(2,1)S(1)}, u32[]{:S(2)}, u32[]{:S(2)}) collective-permute-start(bf16[392,512]{1,0:T(8,128)(2,1)S(1)} %get-tuple-element.39), channel_id=1, source_target_pairs={{0,1},{1,0},{2,3},{3,2},{4,5},{5,4},{6,7},{7,6},{8,9},{9,8},{10,11... | collective-permute-start | bytes 1204232 | tf_op jit(solution)/shard_map/ppermute | solution.py:25
  77.8 58.0 %copy-start.4 = (bf16[32,2048]{1,0:T(8,128)(2,1)S(1)}, bf16[32,2048]{1,0:T(8,128)(2,1)}, u32[]{:S(2)}) copy-start(bf16[32,2048]{1,0:T(8,128)(2,1)} %weight.3) | copy-start | bytes 393220
  77.8 58.0 %copy-start.5 = (f32[32,2048]{1,0:T(8,128)S(1)}, f32[32,2048]{1,0:T(8,128)}, u32[]{:S(2)}) copy-start(f32[32,2048]{1,0:T(8,128)} %velocity.1) | copy-start | bytes 786436
  118.1 17.7 %collective-permute-start.4 = (f32[40,1024]{1,0:T(8,128)S(1)}, f32[40,1024]{1,0:T(8,128)S(1)}, u32[]{:S(2)}, u32[]{:S(2)}) collective-permute-start(f32[40,1024]{1,0:T(8,128)S(1)} %get-tuple-element.43), channel_id=1, source_target_pairs={{0,1},{1,0},{2,3},{3,2},{4,5},{5,4},{6,7},{7,6},{8,9},{9,8},{10,11... | collective-permute-start | bytes 491528 | tf_op jit(solution)/shard_map/ppermute | solution.py:25

commit v11 on v10

--- a/solution.py
+++ b/solution.py
@@ -51,21 +51,26 @@
     return [pl.ds(start, chunk) for start in range(0, width, chunk)]
 
 
-def pieces_kernel(weight, out, sems):
-    half = out.shape[2]
-    copies_out = [
-        pltpu.make_async_copy(
-            weight.at[:, pl.ds(i % 2 * half, half)], out.at[i], sems.at[i]
-        )
-        for i in range(out.shape[0])
-    ]
-    for copy in copies_out:
-        copy.start()
-    for copy in copies_out:
-        copy.wait()
-
-
-def moments_kernel(acts, acts_other, weight, conv, conv_other, moments):
+def eighth_kernel(nx, weight, out):
+    half = weight.shape[1] // 2
+    place = lax.axis_index("zl") * nx + lax.axis_index("x")
+    for c in range(2):
+        tile = weight[:, pl.ds(pl.multiple_of(c * half + place * lanes, lanes), lanes)]
+        for y in range(out.shape[0] // 2):
+            out[2 * y + c] = tile
+
+
+def copies_kernel(block, out, sems):
+    writes = [pltpu.make_async_copy(block, out.at[i], sems.at[i]) for i in range(out.shape[0])]
+    for write in writes:
+        write.start()
+    for write in writes:
+        write.wait()
+
+
+def moments_kernel(acts, acts_other, parts, weight, conv, conv_other, moments):
+    for i in range(parts.shape[0]):
+        weight[:, i * lanes : (i + 1) * lanes] = parts[i]
     count = 2 * conv.shape[0]
     for j, cols in enumerate(columns(conv.shape[1])):
         both = []
@@ -245,75 +250,55 @@
             out[zh * nyh + yh] = tile
 
 
-def far_kernel(received, out):
+def spread(value):
+    value = jnp.sum(jnp.sum(value, axis=0, keepdims=True), axis=1, keepdims=True)
+    return jnp.broadcast_to(value, (1, lanes))
+
+
+def far_kernel(received, weight_squares, out):
     total = jnp.sum(received[...].astype(f32), axis=0)
     at = total.shape[0] - 2 * groups
     value = total[:at]
-    square = jnp.sum(jnp.sum(value * value, axis=0, keepdims=True), axis=1, keepdims=True)
-    square = jnp.broadcast_to(square, (1, lanes))
     tail = total[at : at + groups] + total[at + groups :]
-    tile = [value, *high_low(tail), *high_low(square), jnp.zeros((6, lanes), f32)]
-    tile = jnp.concatenate(tile, axis=0).astype(bf16)
+    square, weight_square = spread(value * value), spread(weight_squares[...])
+    last = [*high_low(square), *high_low(weight_square), jnp.zeros((4, lanes), f32)]
+    tile = jnp.concatenate([value, *high_low(tail), *last], axis=0).astype(bf16)
     out[...] = jnp.broadcast_to(tile[None], out.shape)
 
 
-def places(parts, nx):
-    for zl in range(parts.shape[0] // nx):
-        values = [parts[zl * nx + x].astype(f32) for x in range(nx)]
-        for q in range(groups):
-            yield zl * nx, q, pl.ds((zl * groups + q) * lanes, lanes), values
-
-
-def owned(parts, first, q, owner, count):
-    values = [parts[first + owner * count + i].astype(f32) for i in range(count)]
-    step = (values[0].shape[0] - 16) // groups
-    return jnp.concatenate([v[q * step : (q + 1) * step] for v in values], axis=0)
-
-
-def sums_of(values, q):
-    at = values[0].shape[0] - 16 + q
-    planes = [v[at : at + 1] + v[at + groups : at + groups + 1] for v in values]
-    return planes[0] + planes[1], planes[2] + planes[3]
-
-
-def split_kernel(nx, parts, weight_squares, theirs, squares):
-    other = 1 - lax.axis_index("c")
-    part = theirs.shape[0] - 8
-    for first, q, cols, values in places(parts, nx):
-        theirs[:part, cols] = owned(parts, first, q, other, nx // 2)
-        shift, gain = sums_of(values, q)
-        theirs[part:, cols] = jnp.concatenate([shift, gain, jnp.zeros((6, lanes), f32)], axis=0)
+def squares_kernel(parts, squares):
     total = jnp.sum(parts[...].astype(f32), axis=0)
     at = total.shape[0] - 8
     square = total[at : at + 1] + total[at + 1 : at + 2]
-    weight_square = jnp.sum(weight_squares[...], axis=0, keepdims=True)
-    weight_square = jnp.sum(weight_square, axis=1, keepdims=True)
-    weight_square = jnp.broadcast_to(weight_square, (1, lanes))
+    weight_square = (total[at + 2 : at + 3] + total[at + 3 : at + 4]) / (parts.shape[0] // 2)
     tile = jnp.concatenate([square, weight_square, jnp.zeros((6, lanes), f32)], axis=0)
     squares[...] = jnp.broadcast_to(tile[None], squares.shape)
 
 
-def step_kernel(nx, parts, arrived, squares, weight, velocity, out, gain, shift):
+def step_kernel(nx, parts, squares, weight, velocity, out, gain, shift):
     core = lax.axis_index("c")
-    part, cout = out.shape
-    half = cout // 2
+    half = out.shape[1] // 2
     total = jnp.sum(squares[...], axis=0)
     grad_norm = jnp.sqrt(total[:1, :1])
-    weight_norm = jnp.sqrt(total[1:2, :1] / (squares.shape[0] // 2))
+    weight_norm = jnp.sqrt(total[1:2, :1] / squares.shape[0])
     ratio = weight_norm / (grad_norm + weight_decay * weight_norm)
-
-    def update(cols, weight_grad):
-        decayed = weight_grad + weight_decay * weight[:, cols].astype(f32)
-        out[:, cols] = momentum * velocity[:, cols] + ratio * decayed
-
-    for first, q, cols, values in places(parts, nx):
-        here = pl.ds(pl.multiple_of(core * half + cols.start, lanes), lanes)
-        there = pl.ds(pl.multiple_of((1 - core) * half + cols.start, lanes), lanes)
-        update(here, owned(parts, first, q, core, nx // 2))
-        update(there, arrived[:part, cols])
-        shift[:, here], gain[:, here] = sums_of(values, q)
-        last = arrived[part:, cols]
-        shift[:, there], gain[:, there] = last[:1], last[1:2]
+    count = nx // 2
+    for zl in range(parts.shape[0] // (2 * nx)):
+        for c in range(2):
+            values = [parts[(zl * nx + x) * 2 + c].astype(f32) for x in range(nx)]
+            own = [
+                parts[(zl * nx + core * count + i) * 2 + c].astype(f32) for i in range(count)
+            ]
+            step = (own[0].shape[0] - 16) // groups
+            for q in range(groups):
+                cols = pl.ds(c * half + (zl * groups + q) * lanes, lanes)
+                weight_grad = jnp.concatenate([v[q * step : (q + 1) * step] for v in own], axis=0)
+                decayed = weight_grad + weight_decay * weight[:, cols].astype(f32)
+                out[:, cols] = momentum * velocity[:, cols] + ratio * decayed
+                at = groups * step + q
+                planes = [v[at : at + 1] + v[at + groups : at + groups + 1] for v in values]
+                shift[:, cols] = planes[0] + planes[1]
+                gain[:, cols] = planes[2] + planes[3]
 
 
 def shape(dims, dtype):
@@ -362,26 +347,35 @@
     def other_half(value):
         return jnp.where(first_core, value[:, half:], value[:, :half])
 
-    (pieces,) = call(
-        pieces_kernel,
-        "pieces",
+    (eighth,) = call(
+        functools.partial(eighth_kernel, nx),
+        "eighth",
         (conv_weight,),
+        [shape((members, part, lanes), bf16)],
+    )
+    eighth = exchange(eighth, bn).reshape(cin, lanes)
+    (spread_out,) = call(
+        copies_kernel,
+        "weight_copies",
+        (eighth,),
         [],
-        [pltpu.SemaphoreType.DMA((members,))],
-        loaded=1,
-        written=shape((members, part, half), bf16),
-    )
-    weight = exchange(pieces, bn).reshape(cin, half)
+        [pltpu.SemaphoreType.DMA((nzl * nx,))],
+        written=shape((nzl * nx, cin, lanes), bf16),
+    )
+    weight_parts = exchange(spread_out, ("zl", "x"))
     acts_other = swap(activations)
     block_other = swap(other_half(block_input))
     out_other = swap(other_half(out_grad))
-    weight, acts_other = lax.optimization_barrier((weight, acts_other))
+    weight_parts, acts_other = lax.optimization_barrier((weight_parts, acts_other))
 
     wide = shape((rows, half), f32)
     narrow = shape((rows, half), bf16)
     sums = shape((ny, 2 * half // lanes, lanes), f32)
-    conv, conv_other, moments = call(
-        moments_kernel, "moments", (activations, acts_other, weight), [wide, wide, sums]
+    weight, conv, conv_other, moments = call(
+        moments_kernel,
+        "moments",
+        (activations, acts_other, weight_parts),
+        [shape((cin, half), bf16), wide, wide, sums],
     )
     moments, block_other, out_other = lax.optimization_barrier((moments, block_other, out_other))
     moments = exchange(moments, y_axes)
@@ -422,22 +416,16 @@
     (ready,) = call(
         far_kernel,
         "far_sum",
-        (exchange(partial, far),),
-        [shape((nzl * nx, groups * step + 16, lanes), bf16)],
-    )
-    ready = exchange(ready, ("zl", "x"))
-    theirs, squares = call(
-        functools.partial(split_kernel, nx),
-        "split",
-        (ready, weight_squares),
-        [shape((part + 8, half), f32), shape((members, 8, lanes), f32)],
-    )
-    arrived = swap(theirs)
-    squares = exchange(squares, bn)
+        (exchange(partial, far), weight_squares),
+        [shape((2 * nzl * nx, groups * step + 16, lanes), bf16)],
+    )
+    ready = exchange(ready, ("zl", "x", "c"))
+    (squares,) = call(squares_kernel, "squares", (ready,), [shape((ny, 8, lanes), f32)])
+    squares = exchange(squares, y_axes)
     new_velocity, gain_grad, shift_grad = call(
         functools.partial(step_kernel, nx),
         "step",
-        (ready, arrived, squares, conv_weight, velocity),
+        (ready, squares, conv_weight, velocity),
         [shape((part, cout), f32), shape((1, cout), f32), shape((1, cout), f32)],
     )
     return (act_grad, gain_grad.reshape(cout), shift_grad.reshape(cout), new_velocity)

time: 137 us -> 138 us (level)
  blocking collectives: 62.2 us -> 84.4 us
  starting transfers between devices: 32.5 us -> 19.8 us
  waiting for transfers between devices: 27.8 us -> 16.2 us
  local copies, waits for them, and re-layouts: 0.93 us -> 3.67 us
  other arithmetic: 4.33 us -> 2.89 us
    all_to_all x5 -> x6, blocking collectives: 62.2 us -> 84.4 us  [exchange(): return lax.all_to_all(pieces, axis, 0, 0, tiled=True)]
    all_to_all x2, waiting for transfers between devices: 25 us -> 13.1 us  [exchange(): return lax.all_to_all(pieces, axis, 0, 0, tiled=True)]
    ppermute x5 -> x4, starting transfers between devices: 17.9 us -> 11.2 us  [swap(): return lax.ppermute(value, 'c', [(0, 1), (1, 0)])]
    all_to_all x2, starting transfers between devices: 14.6 us -> 8.63 us  [exchange(): return lax.all_to_all(pieces, axis, 0, 0, tiled=True)]
    unnamed x16 -> x22, local copies, waits for them, and re-layouts: 0.93 us -> 3.67 us
    select_n x2, other arithmetic: 3.46 us -> 2 us  [other_half(): return jnp.where(first_core, value[:, half:], value[:, :half])]
    pallas_call x8 -> x9, Pallas kernels: 8.16 us -> 9.26 us  [call(): pl.pallas_call(kernel, grid=(1,), in_specs=in_specs, out_specs=out_specs,...]
    ppermute x5 -> x4, waiting for transfers between devices: 2.83 us -> 3.04 us  [swap(): return lax.ppermute(value, 'c', [(0, 1), (1, 0)])]
  transfers between devices with their start and end apart: 7 -> 6, of which waited for: 4 -> 4; matrix products, arithmetic and copies ran while one was open for 3% -> 2% of each run, Pallas kernels for 1% -> 2%
where the time goes in v11:
time: 138 us; the launch traced here: 137 us
  blocking collectives  84.4 us (61%)
  starting transfers between devices  19.8 us (14%)
  waiting for transfers between devices  16.2 us (12%)
  Pallas kernels  9.26 us (7%)
  local copies, waits for them, and re-layouts  3.67 us (3%)
  other arithmetic  2.89 us (2%)
    all_to_all x6, blocking collectives, exchange(): return lax.all_to_all(pieces, axis, 0, 0, tiled=True)  84.4 us
    all_to_all x2, waiting for transfers between devices, exchange(): return lax.all_to_all(pieces, axis, 0, 0, tiled=True)  13.1 us
    ppermute x4, starting transfers between devices, swap(): return lax.ppermute(value, 'c', [(0, 1), (1, 0)])  11.2 us
    pallas_call x9, Pallas kernels, call(): pl.pallas_call(kernel, grid=(1,), in_specs=in_specs, out_specs=out_specs,...  9.26 us
    all_to_all x2, starting transfers between devices, exchange(): return lax.all_to_all(pieces, axis, 0, 0, tiled=True)  8.63 us
    unnamed x22, local copies, waits for them, and re-layouts  3.67 us
    ppermute x4, waiting for transfers between devices, swap(): return lax.ppermute(value, 'c', [(0, 1), (1, 0)])  3.04 us
  transfers between devices with their start and end apart: 6, of which 4 were waited for; matrix products, arithmetic and copies ran while one was open for 2% of the time, Pallas kernels for 2%

profile of v11, /device:TPU:1, one launch (start us, length us, event | category | flops | bytes accessed | tf_op | source)
XLA Modules:
  0.0 137.0 jit_solution(5481730132272417378)
XLA Ops:
  0.6 0.0 copy-start.6
  0.6 0.9 copy-done.6
  1.6 18.5 %all_to_all.40 = bf16[16,32,128]{2,1,0:T(8,128)(2,1)S(1)} all-to-all(bf16[16,32,128]{2,1,0:T(8,128)(2,1)S(1)} %eighth.1), channel_id=1, replica_groups=mesh['zh'=4,'zl'=2,'x'=4,'yh'=4,'yl'=2,'c'=2] {'yh','yl','c'}, dimensions={0} | all-to-all | bytes 262144 | tf_op jit(solution)/shard_map/all_to_all | solution.py:29
  20.1 1.0 weight_copies.1
  21.1 4.9 %all-to-all-start.1 = ((bf16[8,512,128]{2,1,0:T(8,128)(2,1)}), bf16[8,512,128]{2,1,0:T(8,128)(2,1)}, u32[]{:S(2)}, u32[]{:S(2)}) async-start(bf16[8,512,128]{2,1,0:T(8,128)(2,1)} %weight_copies.1), calls=%async_computation.1 | async-start | bytes 2097152 | tf_op jit(solution)/shard_map/all_to_all | solution.py:29
  26.0 1.0 slice_select_fusion
  27.1 2.0 %collective-permute-start.2 = (bf16[392,1024]{1,0:T(8,128)(2,1)}, bf16[392,1024]{1,0:T(8,128)(2,1)}, u32[]{:S(2)}, u32[]{:S(2)}) collective-permute-start(bf16[392,1024]{1,0:T(8,128)(2,1)} %slice_select_fusion), channel_id=1, source_target_pairs={{0,1},{1,0},{2,3},{3,2},{4,5},{5,4},{6,7},{7,6},{8,9},{9,8},{10,11... | collective-permute-start | bytes 2408456 | tf_op jit(solution)/shard_map/ppermute | solution.py:25
  29.1 1.0 slice_select_fusion.1
  30.1 2.4 %collective-permute-start.1 = (bf16[392,1024]{1,0:T(8,128)(2,1)}, bf16[392,1024]{1,0:T(8,128)(2,1)}, u32[]{:S(2)}, u32[]{:S(2)}) collective-permute-start(bf16[392,1024]{1,0:T(8,128)(2,1)} %slice_select_fusion.1), channel_id=1, source_target_pairs={{0,1},{1,0},{2,3},{3,2},{4,5},{5,4},{6,7},{7,6},{8,9},{9,8},{10,11... | collective-permute-start | bytes 2408456 | tf_op jit(solution)/shard_map/ppermute | solution.py:25
  32.5 1.9 %collective-permute-start = (bf16[392,512]{1,0:T(8,128)(2,1)S(1)}, bf16[392,512]{1,0:T(8,128)(2,1)S(1)}, u32[]{:S(2)}, u32[]{:S(2)}) collective-permute-start(bf16[392,512]{1,0:T(8,128)(2,1)S(1)} %copy-done.2), channel_id=1, source_target_pairs={{0,1},{1,0},{2,3},{3,2},{4,5},{5,4},{6,7},{7,6},{8,9},{9,8},{10,11... | collective-permute-start | bytes 1204232 | tf_op jit(solution)/shard_map/ppermute | solution.py:25
  34.5 1.7 %collective-permute-done.acts_other = bf16[392,512]{1,0:T(8,128)(2,1)S(1)} collective-permute-done((bf16[392,512]{1,0:T(8,128)(2,1)S(1)}, bf16[392,512]{1,0:T(8,128)(2,1)S(1)}, u32[]{:S(2)}, u32[]{:S(2)}) %collective-permute-start) | collective-permute-done | bytes 401440 | tf_op jit(solution)/shard_map/ppermute | solution.py:25
  36.2 0.7 copy-done.4
  36.9 4.3 %all-to-all-done.1.parts = bf16[8,512,128]{2,1,0:T(8,128)(2,1)} async-done(((bf16[8,512,128]{2,1,0:T(8,128)(2,1)}), bf16[8,512,128]{2,1,0:T(8,128)(2,1)}, u32[]{:S(2)}, u32[]{:S(2)}) %all-to-all-start.1) | async-done | bytes 1048608 | tf_op jit(solution)/shard_map/all_to_all | solution.py:29
  41.2 1.0 copy-done.3
  42.2 1.0 copy-done.5
  43.2 2.7 %moments.1 = (bf16[512,1024]{1,0:T(8,128)(2,1)S(1)}, f32[392,1024]{1,0:T(8,128)S(1)}, f32[392,1024]{1,0:T(8,128)S(1)}, f32[8,16,128]{2,1,0:T(8,128)S(1)}) custom-call(bf16[392,512]{1,0:T(8,128)(2,1)S(1)} %copy-done.3, bf16[392,512]{1,0:T(8,128)(2,1)S(1)} %copy-done.5, bf16[8,512,128]{2,1,0:T(8,128)(2,1)} %all-to-all-done.1.parts), custom_call_target="tpu_custom_call" | custom-call | tf_op jit(solution)/shard_map/moments/pallas_call | solution.py:324
  45.9 0.0 collective-permute-done.2.out_far
  45.9 9.6 %all_to_all.41.moments = f32[8,16,128]{2,1,0:T(8,128)S(1)} all-to-all(f32[8,16,128]{2,1,0:T(8,128)S(1)} %get-tuple-element.30), channel_id=1, replica_groups=mesh['zh'=4,'zl'=2,'x'=4,'yh'=4,'yl'=2,'c'=2] {'yh','yl'}, dimensions={0} | all-to-all | bytes 131072 | tf_op jit(solution)/shard_map/all_to_all | solution.py:29
  55.6 2.0 %stats.1 = (bf16[392,1024]{1,0:T(8,128)(2,1)S(1)}, bf16[392,1024]{1,0:T(8,128)(2,1)S(1)}, f32[8,16,128]{2,1,0:T(8,128)S(1)}) custom-call(f32[392,1024]{1,0:T(8,128)S(1)} %get-tuple-element.27.conv, f32[392,1024]{1,0:T(8,128)S(1)} %get-tuple-element.28.conv_other, f32[8,16,128]{2,1,0:T(8,128)S(1)} %all_to_all.41.moments, f32[1,2048]{1,0:T(1,128)S(1)} %bitcast.6, ...), custom_call_target="tpu_custom_call" | custom-call | tf_op jit(solution)/shard_map/stats/pallas_call | solution.py:324
  57.6 9.7 %all_to_all.42.stats = f32[8,16,128]{2,1,0:T(8,128)S(1)} all-to-all(f32[8,16,128]{2,1,0:T(8,128)S(1)} %get-tuple-element.33), channel_id=1, replica_groups=mesh['zh'=4,'zl'=2,'x'=4,'yh'=4,'yl'=2,'c'=2] {'yh','yl'}, dimensions={0} | all-to-all | bytes 131072 | tf_op jit(solution)/shard_map/all_to_all | solution.py:29
  67.3 2.3 %weight_partial.1 = (f32[392,512]{1,0:T(8,128)S(1)}, bf16[392,512]{1,0:T(8,128)(2,1)S(1)}, f32[8,128]{1,0:T(8,128)S(1)}, bf16[16,272,128]{2,1,0:T(8,128)(2,1)}) custom-call(f32[392,1024]{1,0:T(8,128)S(1)} %get-tuple-element.27.conv, f32[392,1024]{1,0:T(8,128)S(1)} %get-tuple-element.28.conv_other, f32[8,16,128]{2,1,0:T(8,128)S(1)} %all_to_all.41.moments, ...), custom_call_target="tpu_custom_call" | custom-call | tf_op jit(solution)/shard_map/weight_partial/pallas_call | solution.py:324
  69.6 3.7 %all-to-all-start.4 = ((bf16[16,272,128]{2,1,0:T(8,128)(2,1)}), bf16[16,272,128]{2,1,0:T(8,128)(2,1)S(1)}, u32[]{:S(2)}, u32[]{:S(2)}) async-start(bf16[16,272,128]{2,1,0:T(8,128)(2,1)} %get-tuple-element.37), calls=%async_computation.4 | async-start | bytes 2228224 | tf_op jit(solution)/shard_map/all_to_all | solution.py:29
  73.3 4.8 %collective-permute-start.3 = (bf16[392,512]{1,0:T(8,128)(2,1)S(1)}, bf16[392,512]{1,0:T(8,128)(2,1)S(1)}, u32[]{:S(2)}, u32[]{:S(2)}) collective-permute-start(bf16[392,512]{1,0:T(8,128)(2,1)S(1)} %get-tuple-element.39), channel_id=1, source_target_pairs={{0,1},{1,0},{2,3},{3,2},{4,5},{5,4},{6,7},{7,6},{8,9},{9,8},{10,11... | collective-permute-start | bytes 1204232 | tf_op jit(solution)/shard_map/ppermute | solution.py:25
  78.1 1.3 collective-permute-done.3
  79.4 0.9 add_convert_fusion
  80.3 8.9 %all-to-all-done.4.received = bf16[16,272,128]{2,1,0:T(8,128)(2,1)S(1)} async-done(((bf16[16,272,128]{2,1,0:T(8,128)(2,1)}), bf16[16,272,128]{2,1,0:T(8,128)(2,1)S(1)}, u32[]{:S(2)}, u32[]{:S(2)}) %all-to-all-start.4) | async-done | bytes 1114144 | tf_op jit(solution)/shard_map/all_to_all | solution.py:29
  89.2 0.2 near_sum.1
  89.4 23.5 %all_to_all.43.received = bf16[16,72,128]{2,1,0:T(8,128)(2,1)S(1)} all-to-all(bf16[16,72,128]{2,1,0:T(8,128)(2,1)S(1)} %near_sum.1), channel_id=1, replica_groups=mesh['zh'=4,'zl'=2,'x'=4,'yh'=4,'yl'=2,'c'=2] {'zh','yh'}, dimensions={0} | all-to-all | bytes 589824 | tf_op jit(solution)/shard_map/all_to_all | solution.py:29
  112.9 0.1 far_sum.1
  113.1 13.1 %all_to_all.44.parts = bf16[16,80,128]{2,1,0:T(8,128)(2,1)S(1)} all-to-all(bf16[16,80,128]{2,1,0:T(8,128)(2,1)S(1)} %far_sum.1), channel_id=1, replica_groups=mesh['zh'=4,'zl'=2,'x'=4,'yh'=4,'yl'=2,'c'=2] {'zl','x','c'}, dimensions={0} | all-to-all | bytes 655360 | tf_op jit(solution)/shard_map/all_to_all | solution.py:29
  126.2 10.0 %all_to_all.45.squares = f32[8,8,128]{2,1,0:T(8,128)S(1)} all-to-all(f32[8,8,128]{2,1,0:T(8,128)S(1)} %squares.1), channel_id=1, replica_groups=mesh['zh'=4,'zl'=2,'x'=4,'yh'=4,'yl'=2,'c'=2] {'yh','yl'}, dimensions={0} | all-to-all | bytes 65536 | tf_op jit(solution)/shard_map/all_to_all | solution.py:29
  136.2 0.8 step.1
  (20 shorter events, 0.1 us)
Async XLA Ops:
  0.6 0.9 copy-start.6
  20.1 6.0 %copy-start.1 = (bf16[392,2048]{1,0:T(8,128)(2,1)S(1)}, bf16[392,2048]{1,0:T(8,128)(2,1)}, u32[]{:S(2)}) copy-start(bf16[392,2048]{1,0:T(8,128)(2,1)} %out.1) | copy-start | bytes 4816900
  21.1 20.1 %all-to-all-start.1 = ((bf16[8,512,128]{2,1,0:T(8,128)(2,1)}), bf16[8,512,128]{2,1,0:T(8,128)(2,1)}, u32[]{:S(2)}, u32[]{:S(2)}) async-start(bf16[8,512,128]{2,1,0:T(8,128)(2,1)} %weight_copies.1), calls=%async_computation.1 | async-start | bytes 2097152 | tf_op jit(solution)/shard_map/all_to_all | solution.py:29
  26.0 3.1 %copy-start = (bf16[392,2048]{1,0:T(8,128)(2,1)S(1)}, bf16[392,2048]{1,0:T(8,128)(2,1)}, u32[]{:S(2)}) copy-start(bf16[392,2048]{1,0:T(8,128)(2,1)} %block.1) | copy-start | bytes 4816900
  27.0 5.5 %copy-start.2 = (bf16[392,512]{1,0:T(8,128)(2,1)S(1)}, bf16[392,512]{1,0:T(8,128)(2,1)}, u32[]{:S(2)}) copy-start(bf16[392,512]{1,0:T(8,128)(2,1)} %acts.3) | copy-start | bytes 1204228
  27.0 28.5 %copy-start.9 = (f32[2048]{0:T(1024)S(1)}, f32[2048]{0:T(1024)}, u32[]{:S(2)}) copy-start(f32[2048]{0:T(1024)} %param.10) | copy-start | bytes 24580
  27.1 28.5 %copy-start.10 = (f32[2048]{0:T(1024)S(1)}, f32[2048]{0:T(1024)}, u32[]{:S(2)}) copy-start(f32[2048]{0:T(1024)} %param.11) | copy-start | bytes 24580
  27.1 18.9 %collective-permute-start.2 = (bf16[392,1024]{1,0:T(8,128)(2,1)}, bf16[392,1024]{1,0:T(8,128)(2,1)}, u32[]{:S(2)}, u32[]{:S(2)}) collective-permute-start(bf16[392,1024]{1,0:T(8,128)(2,1)} %slice_select_fusion), channel_id=1, source_target_pairs={{0,1},{1,0},{2,3},{3,2},{4,5},{5,4},{6,7},{7,6},{8,9},{9,8},{10,11... | collective-permute-start | bytes 2408456 | tf_op jit(solution)/shard_map/ppermute | solution.py:25
  30.1 15.8 %collective-permute-start.1 = (bf16[392,1024]{1,0:T(8,128)(2,1)}, bf16[392,1024]{1,0:T(8,128)(2,1)}, u32[]{:S(2)}, u32[]{:S(2)}) collective-permute-start(bf16[392,1024]{1,0:T(8,128)(2,1)} %slice_select_fusion.1), channel_id=1, source_target_pairs={{0,1},{1,0},{2,3},{3,2},{4,5},{5,4},{6,7},{7,6},{8,9},{9,8},{10,11... | collective-permute-start | bytes 2408456 | tf_op jit(solution)/shard_map/ppermute | solution.py:25
  32.5 3.6 %collective-permute-start = (bf16[392,512]{1,0:T(8,128)(2,1)S(1)}, bf16[392,512]{1,0:T(8,128)(2,1)S(1)}, u32[]{:S(2)}, u32[]{:S(2)}) collective-permute-start(bf16[392,512]{1,0:T(8,128)(2,1)S(1)} %copy-done.2), channel_id=1, source_target_pairs={{0,1},{1,0},{2,3},{3,2},{4,5},{5,4},{6,7},{7,6},{8,9},{9,8},{10,11... | collective-permute-start | bytes 1204232 | tf_op jit(solution)/shard_map/ppermute | solution.py:25
  36.2 0.7 copy-start.4
  41.2 1.0 copy-start.3
  42.2 1.0 copy-start.5
  69.6 19.7 %all-to-all-start.4 = ((bf16[16,272,128]{2,1,0:T(8,128)(2,1)}), bf16[16,272,128]{2,1,0:T(8,128)(2,1)S(1)}, u32[]{:S(2)}, u32[]{:S(2)}) async-start(bf16[16,272,128]{2,1,0:T(8,128)(2,1)} %get-tuple-element.37), calls=%async_computation.4 | async-start | bytes 2228224 | tf_op jit(solution)/shard_map/all_to_all | solution.py:29
  73.3 6.2 %collective-permute-start.3 = (bf16[392,512]{1,0:T(8,128)(2,1)S(1)}, bf16[392,512]{1,0:T(8,128)(2,1)S(1)}, u32[]{:S(2)}, u32[]{:S(2)}) collective-permute-start(bf16[392,512]{1,0:T(8,128)(2,1)S(1)} %get-tuple-element.39), channel_id=1, source_target_pairs={{0,1},{1,0},{2,3},{3,2},{4,5},{5,4},{6,7},{7,6},{8,9},{9,8},{10,11... | collective-permute-start | bytes 1204232 | tf_op jit(solution)/shard_map/ppermute | solution.py:25
  80.3 55.9 %copy-start.7 = (bf16[32,2048]{1,0:T(8,128)(2,1)S(1)}, bf16[32,2048]{1,0:T(8,128)(2,1)}, u32[]{:S(2)}) copy-start(bf16[32,2048]{1,0:T(8,128)(2,1)} %weight.3) | copy-start | bytes 393220
  80.3 55.9 %copy-start.8 = (f32[32,2048]{1,0:T(8,128)S(1)}, f32[32,2048]{1,0:T(8,128)}, u32[]{:S(2)}) copy-start(f32[32,2048]{1,0:T(8,128)} %velocity.1) | copy-start | bytes 786436

commit v12 on v11

--- a/solution.py
+++ b/solution.py
@@ -100,13 +100,15 @@
     moments,
     gain,
     shift,
-    block,
-    out,
+    block_in,
+    out_in,
     block_far,
     out_far,
     grad,
     grad_other,
     stats,
+    block,
+    out,
     block_other,
     out_other,
     sems,
@@ -114,8 +116,10 @@
     rows, half = conv.shape
     core = lax.axis_index("c")
     loads = [
-        pltpu.make_async_copy(block_far, block_other, sems.at[0]),
-        pltpu.make_async_copy(out_far, out_other, sems.at[1]),
+        pltpu.make_async_copy(block_in, block, sems.at[0]),
+        pltpu.make_async_copy(out_in, out, sems.at[1]),
+        pltpu.make_async_copy(block_far, block_other, sems.at[2]),
+        pltpu.make_async_copy(out_far, out_other, sems.at[3]),
     ]
     for load in loads:
         load.start()
@@ -123,7 +127,7 @@
     for j, cols in enumerate(columns(half)):
         place = pl.ds(pl.multiple_of(core * half + j * chunk, chunk), chunk)
         mean, inv_std = pooled(moments[:, 8 * j : 8 * j + 8], 2 * rows)
-        scales.append((cols, place, mean, inv_std, gain[:, place] * inv_std, shift[:, place]))
+        scales.append((cols, mean, inv_std, gain[:, place] * inv_std, shift[:, place]))
 
     def sums(of, added, incoming, result, cols, mean, scale, bias):
         centered = of[:, cols] - mean
@@ -135,13 +139,15 @@
             jnp.sum(value * centered, axis=0, keepdims=True),
         )
 
+    for load in loads[:2]:
+        load.wait()
     near_sums = [
-        sums(conv, block[:, place], out[:, place], grad, cols, mean, scale, bias)
-        for cols, place, mean, _, scale, bias in scales
+        sums(conv, block[:, cols], out[:, cols], grad, cols, mean, scale, bias)
+        for cols, mean, _, scale, bias in scales
     ]
-    for load in loads:
+    for load in loads[2:]:
         load.wait()
-    for j, (cols, _, mean, inv_std, scale, bias) in enumerate(scales):
+    for j, (cols, mean, inv_std, scale, bias) in enumerate(scales):
         sum_grad, sum_cross = sums(
             conv_other, block_other[:, cols], out_other[:, cols], grad_other, cols, mean, scale, bias
         )
@@ -344,8 +350,9 @@
     first_core = lax.axis_index("c") == 0
     gain, shift = bn_gain.reshape(1, cout), bn_shift.reshape(1, cout)
 
-    def other_half(value):
-        return jnp.where(first_core, value[:, half:], value[:, :half])
+    def halves(value):
+        low, high = value[:, :half], value[:, half:]
+        return jnp.where(first_core, low, high), jnp.where(first_core, high, low)
 
     (eighth,) = call(
         functools.partial(eighth_kernel, nx),
@@ -364,9 +371,12 @@
     )
     weight_parts = exchange(spread_out, ("zl", "x"))
     acts_other = swap(activations)
-    block_other = swap(other_half(block_input))
-    out_other = swap(other_half(out_grad))
-    weight_parts, acts_other = lax.optimization_barrier((weight_parts, acts_other))
+    block, block_other = halves(block_input)
+    out, out_other = halves(out_grad)
+    block_other, out_other = swap(block_other), swap(out_other)
+    weight_parts, acts_other, block, out = lax.optimization_barrier(
+        (weight_parts, acts_other, block, out)
+    )
 
     wide = shape((rows, half), f32)
     narrow = shape((rows, half), bf16)
@@ -382,10 +392,10 @@
     grad, grad_other, stats = call(
         stats_kernel,
         "stats",
-        (conv, conv_other, moments, gain, shift, block_input, out_grad, block_other, out_other),
+        (conv, conv_other, moments, gain, shift, block, out, block_other, out_other),
         [narrow, narrow, sums],
-        [pltpu.VMEM((rows, half), bf16)] * 2 + [pltpu.SemaphoreType.DMA((2,))],
-        loaded=2,
+        [pltpu.VMEM((rows, half), bf16)] * 4 + [pltpu.SemaphoreType.DMA((4,))],
+        loaded=4,
     )
     stats = exchange(stats, y_axes)
     count = nzl * nx * nyl

time: 138 us -> 135 us (0.978)
  local copies, waits for them, and re-layouts: 3.67 us -> 0.92 us
  other arithmetic: 2.89 us -> 4.38 us
    unnamed x22 -> x14, local copies, waits for them, and re-layouts: 3.67 us -> 0.92 us
    select_n x2, other arithmetic: 2 us -> 3.49 us  [halves(): return (jnp.where(first_core, low, high), jnp.where(first_core, high, low))]
  transfers between devices with their start and end apart: 6 -> 6, of which waited for: 4 -> 4; matrix products, arithmetic and copies ran while one was open for 2% -> 3% of each run, Pallas kernels for 2% -> 1%
where the time goes in v12:
time: 135 us; the launch traced here: 134 us
  blocking collectives  84.4 us (63%)
  starting transfers between devices  20 us (15%)
  waiting for transfers between devices  15.2 us (11%)
  Pallas kernels  8.23 us (6%)
  other arithmetic  4.38 us (3%)
    all_to_all x6, blocking collectives, exchange(): return lax.all_to_all(pieces, axis, 0, 0, tiled=True)  84.4 us
    all_to_all x2, waiting for transfers between devices, exchange(): return lax.all_to_all(pieces, axis, 0, 0, tiled=True)  12.2 us
    ppermute x4, starting transfers between devices, swap(): return lax.ppermute(value, 'c', [(0, 1), (1, 0)])  11.3 us
    all_to_all x2, starting transfers between devices, exchange(): return lax.all_to_all(pieces, axis, 0, 0, tiled=True)  8.63 us
    pallas_call x9, Pallas kernels, call(): pl.pallas_call(kernel, grid=(1,), in_specs=in_specs, out_specs=out_specs,...  8.23 us
    select_n x2, other arithmetic, halves(): return (jnp.where(first_core, low, high), jnp.where(first_core, high, low))  3.49 us
    ppermute x4, waiting for transfers between devices, swap(): return lax.ppermute(value, 'c', [(0, 1), (1, 0)])  3.04 us
  transfers between devices with their start and end apart: 6, of which 4 were waited for; matrix products, arithmetic and copies ran while one was open for 3% of the time, Pallas kernels for 1%

profile of v12, /device:TPU:1, one launch (start us, length us, event | category | flops | bytes accessed | tf_op | source)
XLA Modules:
  0.0 133.9 jit_solution(5807796308505334359)
XLA Ops:
  0.6 0.0 copy-start.1
  0.6 0.9 copy-done.1
  1.6 18.5 %all_to_all.40 = bf16[16,32,128]{2,1,0:T(8,128)(2,1)S(1)} all-to-all(bf16[16,32,128]{2,1,0:T(8,128)(2,1)S(1)} %eighth.1), channel_id=1, replica_groups=mesh['zh'=4,'zl'=2,'x'=4,'yh'=4,'yl'=2,'c'=2] {'yh','yl','c'}, dimensions={0} | all-to-all | bytes 262144 | tf_op jit(solution)/shard_map/all_to_all | solution.py:29
  20.1 1.1 weight_copies.1
  21.1 4.9 %all-to-all-start.1 = ((bf16[8,512,128]{2,1,0:T(8,128)(2,1)}), bf16[8,512,128]{2,1,0:T(8,128)(2,1)S(1)}, u32[]{:S(2)}, u32[]{:S(2)}) async-start(bf16[8,512,128]{2,1,0:T(8,128)(2,1)} %weight_copies.1), calls=%async_computation.1 | async-start | bytes 2097152 | tf_op jit(solution)/shard_map/all_to_all | solution.py:29
  26.1 2.5 %broadcast_select_fusion.1 = (bf16[392,1024]{1,0:T(8,128)(2,1)}, bf16[392,1024]{1,0:T(8,128)(2,1)S(1)}) fusion(pred[]{:T(512)S(6)} %eq.3, bf16[392,2048]{1,0:T(8,128)(2,1)} %param.7), kind=kLoop, calls=%fused_computation.2 | loop fusion | flops 802816 | bytes 3211265 | tf_op jit(solution)/shard_map/jit(_where)/select_n | solution.py:355
  28.6 2.0 %collective-permute-start.1 = (bf16[392,1024]{1,0:T(8,128)(2,1)}, bf16[392,1024]{1,0:T(8,128)(2,1)}, u32[]{:S(2)}, u32[]{:S(2)}) collective-permute-start(bf16[392,1024]{1,0:T(8,128)(2,1)} %get-tuple-element.52), channel_id=1, source_target_pairs={{0,1},{1,0},{2,3},{3,2},{4,5},{5,4},{6,7},{7,6},{8,9},{9,8},{10,11... | collective-permute-start | bytes 2408456 | tf_op jit(solution)/shard_map/ppermute | solution.py:25
  30.6 1.0 broadcast_select_fusion
  31.6 2.5 %collective-permute-start.2 = (bf16[392,1024]{1,0:T(8,128)(2,1)}, bf16[392,1024]{1,0:T(8,128)(2,1)}, u32[]{:S(2)}, u32[]{:S(2)}) collective-permute-start(bf16[392,1024]{1,0:T(8,128)(2,1)} %get-tuple-element.50), channel_id=1, source_target_pairs={{0,1},{1,0},{2,3},{3,2},{4,5},{5,4},{6,7},{7,6},{8,9},{9,8},{10,11... | collective-permute-start | bytes 2408456 | tf_op jit(solution)/shard_map/ppermute | solution.py:25
  34.2 1.9 %collective-permute-start = (bf16[392,512]{1,0:T(8,128)(2,1)S(1)}, bf16[392,512]{1,0:T(8,128)(2,1)S(1)}, u32[]{:S(2)}, u32[]{:S(2)}) collective-permute-start(bf16[392,512]{1,0:T(8,128)(2,1)S(1)} %copy-done), channel_id=1, source_target_pairs={{0,1},{1,0},{2,3},{3,2},{4,5},{5,4},{6,7},{7,6},{8,9},{9,8},{10,11... | collective-permute-start | bytes 1204232 | tf_op jit(solution)/shard_map/ppermute | solution.py:25
  36.1 1.7 %collective-permute-done.acts_other = bf16[392,512]{1,0:T(8,128)(2,1)S(1)} collective-permute-done((bf16[392,512]{1,0:T(8,128)(2,1)S(1)}, bf16[392,512]{1,0:T(8,128)(2,1)S(1)}, u32[]{:S(2)}, u32[]{:S(2)}) %collective-permute-start) | collective-permute-done | bytes 401440 | tf_op jit(solution)/shard_map/ppermute | solution.py:25
  37.8 3.3 %all-to-all-done.1.parts = bf16[8,512,128]{2,1,0:T(8,128)(2,1)S(1)} async-done(((bf16[8,512,128]{2,1,0:T(8,128)(2,1)}), bf16[8,512,128]{2,1,0:T(8,128)(2,1)S(1)}, u32[]{:S(2)}, u32[]{:S(2)}) %all-to-all-start.1) | async-done | bytes 1048608 | tf_op jit(solution)/shard_map/all_to_all | solution.py:29
  41.1 1.5 %moments.1 = (bf16[512,1024]{1,0:T(8,128)(2,1)S(1)}, f32[392,1024]{1,0:T(8,128)S(1)}, f32[392,1024]{1,0:T(8,128)S(1)}, f32[8,16,128]{2,1,0:T(8,128)S(1)}) custom-call(bf16[392,512]{1,0:T(8,128)(2,1)S(1)} %copy-done, bf16[392,512]{1,0:T(8,128)(2,1)S(1)} %collective-permute-done.acts_other, bf16[8,512,128]{2,1,0:T(8,128)(2,1)S(1)} %all-to-all-done.1.parts), custom_call_target="tpu_custom_call" | custom-call | tf_op jit(solution)/shard_map/moments/pallas_call | solution.py:330
  42.6 0.0 collective-permute-done.1.block_far
  42.6 0.0 collective-permute-done.2.out_far
  42.6 9.6 %all_to_all.41.moments = f32[8,16,128]{2,1,0:T(8,128)S(1)} all-to-all(f32[8,16,128]{2,1,0:T(8,128)S(1)} %get-tuple-element.32), channel_id=1, replica_groups=mesh['zh'=4,'zl'=2,'x'=4,'yh'=4,'yl'=2,'c'=2] {'yh','yl'}, dimensions={0} | all-to-all | bytes 131072 | tf_op jit(solution)/shard_map/all_to_all | solution.py:29
  52.3 0.0 copy-done.5
  52.3 2.2 %stats.1 = (bf16[392,1024]{1,0:T(8,128)(2,1)S(1)}, bf16[392,1024]{1,0:T(8,128)(2,1)S(1)}, f32[8,16,128]{2,1,0:T(8,128)S(1)}) custom-call(f32[392,1024]{1,0:T(8,128)S(1)} %get-tuple-element.29.conv, f32[392,1024]{1,0:T(8,128)S(1)} %get-tuple-element.30.conv_other, f32[8,16,128]{2,1,0:T(8,128)S(1)} %all_to_all.41.moments, f32[1,2048]{1,0:T(1,128)S(1)} %bitcast.6, ...), custom_call_target="tpu_custom_call" | custom-call | tf_op jit(solution)/shard_map/stats/pallas_call | solution.py:330
  54.5 9.7 %all_to_all.42.stats = f32[8,16,128]{2,1,0:T(8,128)S(1)} all-to-all(f32[8,16,128]{2,1,0:T(8,128)S(1)} %get-tuple-element.37), channel_id=1, replica_groups=mesh['zh'=4,'zl'=2,'x'=4,'yh'=4,'yl'=2,'c'=2] {'yh','yl'}, dimensions={0} | all-to-all | bytes 131072 | tf_op jit(solution)/shard_map/all_to_all | solution.py:29
  64.2 2.2 %weight_partial.1 = (f32[392,512]{1,0:T(8,128)S(1)}, bf16[392,512]{1,0:T(8,128)(2,1)S(1)}, f32[8,128]{1,0:T(8,128)S(1)}, bf16[16,272,128]{2,1,0:T(8,128)(2,1)}) custom-call(f32[392,1024]{1,0:T(8,128)S(1)} %get-tuple-element.29.conv, f32[392,1024]{1,0:T(8,128)S(1)} %get-tuple-element.30.conv_other, f32[8,16,128]{2,1,0:T(8,128)S(1)} %all_to_all.41.moments, ...), custom_call_target="tpu_custom_call" | custom-call | tf_op jit(solution)/shard_map/weight_partial/pallas_call | solution.py:330
  66.4 3.7 %all-to-all-start.4 = ((bf16[16,272,128]{2,1,0:T(8,128)(2,1)}), bf16[16,272,128]{2,1,0:T(8,128)(2,1)S(1)}, u32[]{:S(2)}, u32[]{:S(2)}) async-start(bf16[16,272,128]{2,1,0:T(8,128)(2,1)} %get-tuple-element.41), calls=%async_computation.4 | async-start | bytes 2228224 | tf_op jit(solution)/shard_map/all_to_all | solution.py:29
  70.1 4.8 %collective-permute-start.3 = (bf16[392,512]{1,0:T(8,128)(2,1)S(1)}, bf16[392,512]{1,0:T(8,128)(2,1)S(1)}, u32[]{:S(2)}, u32[]{:S(2)}) collective-permute-start(bf16[392,512]{1,0:T(8,128)(2,1)S(1)} %get-tuple-element.43), channel_id=1, source_target_pairs={{0,1},{1,0},{2,3},{3,2},{4,5},{5,4},{6,7},{7,6},{8,9},{9,8},{10,11... | collective-permute-start | bytes 1204232 | tf_op jit(solution)/shard_map/ppermute | solution.py:25
  75.0 1.3 %collective-permute-done.3 = bf16[392,512]{1,0:T(8,128)(2,1)S(1)} collective-permute-done((bf16[392,512]{1,0:T(8,128)(2,1)S(1)}, bf16[392,512]{1,0:T(8,128)(2,1)S(1)}, u32[]{:S(2)}, u32[]{:S(2)}) %collective-permute-start.3) | collective-permute-done | bytes 401440 | tf_op jit(solution)/shard_map/ppermute | solution.py:25
  76.3 0.9 add_convert_fusion
  77.2 8.9 %all-to-all-done.4.received = bf16[16,272,128]{2,1,0:T(8,128)(2,1)S(1)} async-done(((bf16[16,272,128]{2,1,0:T(8,128)(2,1)}), bf16[16,272,128]{2,1,0:T(8,128)(2,1)S(1)}, u32[]{:S(2)}, u32[]{:S(2)}) %all-to-all-start.4) | async-done | bytes 1114144 | tf_op jit(solution)/shard_map/all_to_all | solution.py:29
  86.1 0.2 near_sum.1
  86.3 23.5 %all_to_all.43.received = bf16[16,72,128]{2,1,0:T(8,128)(2,1)S(1)} all-to-all(bf16[16,72,128]{2,1,0:T(8,128)(2,1)S(1)} %near_sum.1), channel_id=1, replica_groups=mesh['zh'=4,'zl'=2,'x'=4,'yh'=4,'yl'=2,'c'=2] {'zh','yh'}, dimensions={0} | all-to-all | bytes 589824 | tf_op jit(solution)/shard_map/all_to_all | solution.py:29
  109.8 0.1 far_sum.1
  109.9 13.1 %all_to_all.44.parts = bf16[16,80,128]{2,1,0:T(8,128)(2,1)S(1)} all-to-all(bf16[16,80,128]{2,1,0:T(8,128)(2,1)S(1)} %far_sum.1), channel_id=1, replica_groups=mesh['zh'=4,'zl'=2,'x'=4,'yh'=4,'yl'=2,'c'=2] {'zl','x','c'}, dimensions={0} | all-to-all | bytes 655360 | tf_op jit(solution)/shard_map/all_to_all | solution.py:29
  123.1 10.0 %all_to_all.45.squares = f32[8,8,128]{2,1,0:T(8,128)S(1)} all-to-all(f32[8,8,128]{2,1,0:T(8,128)S(1)} %squares.1), channel_id=1, replica_groups=mesh['zh'=4,'zl'=2,'x'=4,'yh'=4,'yl'=2,'c'=2] {'yh','yl'}, dimensions={0} | all-to-all | bytes 65536 | tf_op jit(solution)/shard_map/all_to_all | solution.py:29
  133.1 0.0 copy-done.3
  133.1 0.8 step.1
  (12 shorter events, 0.1 us)
Async XLA Ops:
  0.6 0.9 copy-start.1
  21.1 20.0 %all-to-all-start.1 = ((bf16[8,512,128]{2,1,0:T(8,128)(2,1)}), bf16[8,512,128]{2,1,0:T(8,128)(2,1)S(1)}, u32[]{:S(2)}, u32[]{:S(2)}) async-start(bf16[8,512,128]{2,1,0:T(8,128)(2,1)} %weight_copies.1), calls=%async_computation.1 | async-start | bytes 2097152 | tf_op jit(solution)/shard_map/all_to_all | solution.py:29
  26.0 4.6 %copy-start.6 = (bf16[392,2048]{1,0:T(8,128)(2,1)S(1)}, bf16[392,2048]{1,0:T(8,128)(2,1)}, u32[]{:S(2)}) copy-start(bf16[392,2048]{1,0:T(8,128)(2,1)} %param.12) | copy-start | bytes 4816900
  28.6 5.6 %copy-start = (bf16[392,512]{1,0:T(8,128)(2,1)S(1)}, bf16[392,512]{1,0:T(8,128)(2,1)}, u32[]{:S(2)}) copy-start(bf16[392,512]{1,0:T(8,128)(2,1)} %acts.3) | copy-start | bytes 1204228
  28.6 14.1 %collective-permute-start.1 = (bf16[392,1024]{1,0:T(8,128)(2,1)}, bf16[392,1024]{1,0:T(8,128)(2,1)}, u32[]{:S(2)}, u32[]{:S(2)}) collective-permute-start(bf16[392,1024]{1,0:T(8,128)(2,1)} %get-tuple-element.52), channel_id=1, source_target_pairs={{0,1},{1,0},{2,3},{3,2},{4,5},{5,4},{6,7},{7,6},{8,9},{9,8},{10,11... | collective-permute-start | bytes 2408456 | tf_op jit(solution)/shard_map/ppermute | solution.py:25
  31.6 20.7 %copy-start.4 = (f32[2048]{0:T(1024)S(1)}, f32[2048]{0:T(1024)}, u32[]{:S(2)}) copy-start(f32[2048]{0:T(1024)} %param.10) | copy-start | bytes 24580
  31.6 20.7 %copy-start.5 = (f32[2048]{0:T(1024)S(1)}, f32[2048]{0:T(1024)}, u32[]{:S(2)}) copy-start(f32[2048]{0:T(1024)} %param.11) | copy-start | bytes 24580
  31.6 11.0 %collective-permute-start.2 = (bf16[392,1024]{1,0:T(8,128)(2,1)}, bf16[392,1024]{1,0:T(8,128)(2,1)}, u32[]{:S(2)}, u32[]{:S(2)}) collective-permute-start(bf16[392,1024]{1,0:T(8,128)(2,1)} %get-tuple-element.50), channel_id=1, source_target_pairs={{0,1},{1,0},{2,3},{3,2},{4,5},{5,4},{6,7},{7,6},{8,9},{9,8},{10,11... | collective-permute-start | bytes 2408456 | tf_op jit(solution)/shard_map/ppermute | solution.py:25
  34.2 3.6 %collective-permute-start = (bf16[392,512]{1,0:T(8,128)(2,1)S(1)}, bf16[392,512]{1,0:T(8,128)(2,1)S(1)}, u32[]{:S(2)}, u32[]{:S(2)}) collective-permute-start(bf16[392,512]{1,0:T(8,128)(2,1)S(1)} %copy-done), channel_id=1, source_target_pairs={{0,1},{1,0},{2,3},{3,2},{4,5},{5,4},{6,7},{7,6},{8,9},{9,8},{10,11... | collective-permute-start | bytes 1204232 | tf_op jit(solution)/shard_map/ppermute | solution.py:25
  66.4 19.7 %all-to-all-start.4 = ((bf16[16,272,128]{2,1,0:T(8,128)(2,1)}), bf16[16,272,128]{2,1,0:T(8,128)(2,1)S(1)}, u32[]{:S(2)}, u32[]{:S(2)}) async-start(bf16[16,272,128]{2,1,0:T(8,128)(2,1)} %get-tuple-element.41), calls=%async_computation.4 | async-start | bytes 2228224 | tf_op jit(solution)/shard_map/all_to_all | solution.py:29
  70.1 6.2 %collective-permute-start.3 = (bf16[392,512]{1,0:T(8,128)(2,1)S(1)}, bf16[392,512]{1,0:T(8,128)(2,1)S(1)}, u32[]{:S(2)}, u32[]{:S(2)}) collective-permute-start(bf16[392,512]{1,0:T(8,128)(2,1)S(1)} %get-tuple-element.43), channel_id=1, source_target_pairs={{0,1},{1,0},{2,3},{3,2},{4,5},{5,4},{6,7},{7,6},{8,9},{9,8},{10,11... | collective-permute-start | bytes 1204232 | tf_op jit(solution)/shard_map/ppermute | solution.py:25
  77.2 55.9 %copy-start.2 = (bf16[32,2048]{1,0:T(8,128)(2,1)S(1)}, bf16[32,2048]{1,0:T(8,128)(2,1)}, u32[]{:S(2)}) copy-start(bf16[32,2048]{1,0:T(8,128)(2,1)} %weight.3) | copy-start | bytes 393220
  77.2 55.9 %copy-start.3 = (f32[32,2048]{1,0:T(8,128)S(1)}, f32[32,2048]{1,0:T(8,128)}, u32[]{:S(2)}) copy-start(f32[32,2048]{1,0:T(8,128)} %velocity.1) | copy-start | bytes 786436

commit v13 on v12

--- a/solution.py
+++ b/solution.py
@@ -100,15 +100,13 @@
     moments,
     gain,
     shift,
-    block_in,
-    out_in,
+    block,
+    out,
     block_far,
     out_far,
     grad,
     grad_other,
     stats,
-    block,
-    out,
     block_other,
     out_other,
     sems,
@@ -116,10 +114,8 @@
     rows, half = conv.shape
     core = lax.axis_index("c")
     loads = [
-        pltpu.make_async_copy(block_in, block, sems.at[0]),
-        pltpu.make_async_copy(out_in, out, sems.at[1]),
-        pltpu.make_async_copy(block_far, block_other, sems.at[2]),
-        pltpu.make_async_copy(out_far, out_other, sems.at[3]),
+        pltpu.make_async_copy(block_far, block_other, sems.at[0]),
+        pltpu.make_async_copy(out_far, out_other, sems.at[1]),
     ]
     for load in loads:
         load.start()
@@ -139,13 +135,11 @@
             jnp.sum(value * centered, axis=0, keepdims=True),
         )
 
-    for load in loads[:2]:
-        load.wait()
     near_sums = [
         sums(conv, block[:, cols], out[:, cols], grad, cols, mean, scale, bias)
         for cols, mean, _, scale, bias in scales
     ]
-    for load in loads[2:]:
+    for load in loads:
         load.wait()
     for j, (cols, mean, inv_std, scale, bias) in enumerate(scales):
         sum_grad, sum_cross = sums(
@@ -394,8 +388,8 @@
         "stats",
         (conv, conv_other, moments, gain, shift, block, out, block_other, out_other),
         [narrow, narrow, sums],
-        [pltpu.VMEM((rows, half), bf16)] * 4 + [pltpu.SemaphoreType.DMA((4,))],
-        loaded=4,
+        [pltpu.VMEM((rows, half), bf16)] * 2 + [pltpu.SemaphoreType.DMA((2,))],
+        loaded=2,
     )
     stats = exchange(stats, y_axes)
     count = nzl * nx * nyl

time: 135 us -> 134 us (level)
  no operation moved by 1% of the time
where the time goes in v13:
time: 134 us
  blocking collectives  84.4 us (63%)
  starting transfers between devices  20 us (15%)
  waiting for transfers between devices  15.2 us (11%)
  Pallas kernels  8.07 us (6%)
  other arithmetic  4.38 us (3%)
    all_to_all x6, blocking collectives, exchange(): return lax.all_to_all(pieces, axis, 0, 0, tiled=True)  84.4 us
    all_to_all x2, waiting for transfers between devices, exchange(): return lax.all_to_all(pieces, axis, 0, 0, tiled=True)  12.2 us
    ppermute x4, starting transfers between devices, swap(): return lax.ppermute(value, 'c', [(0, 1), (1, 0)])  11.3 us
    all_to_all x2, starting transfers between devices, exchange(): return lax.all_to_all(pieces, axis, 0, 0, tiled=True)  8.63 us
    pallas_call x9, Pallas kernels, call(): pl.pallas_call(kernel, grid=(1,), in_specs=in_specs, out_specs=out_specs,...  8.07 us
    select_n x2, other arithmetic, halves(): return (jnp.where(first_core, low, high), jnp.where(first_core, high, low))  3.49 us
    ppermute x4, waiting for transfers between devices, swap(): return lax.ppermute(value, 'c', [(0, 1), (1, 0)])  3.04 us
  transfers between devices with their start and end apart: 6, of which 4 were waited for; matrix products, arithmetic and copies ran while one was open for 3% of the time, Pallas kernels for 1%

profile of v13, /device:TPU:1, one launch (start us, length us, event | category | flops | bytes accessed | tf_op | source)
XLA Modules:
  0.0 133.7 jit_solution(5581999263683398285)
XLA Ops:
  0.6 0.0 copy-start.1
  0.6 0.9 copy-done.1
  1.6 18.5 %all_to_all.40 = bf16[16,32,128]{2,1,0:T(8,128)(2,1)S(1)} all-to-all(bf16[16,32,128]{2,1,0:T(8,128)(2,1)S(1)} %eighth.1), channel_id=1, replica_groups=mesh['zh'=4,'zl'=2,'x'=4,'yh'=4,'yl'=2,'c'=2] {'yh','yl','c'}, dimensions={0} | all-to-all | bytes 262144 | tf_op jit(solution)/shard_map/all_to_all | solution.py:29
  20.1 1.1 weight_copies.1
  21.1 4.9 %all-to-all-start.1 = ((bf16[8,512,128]{2,1,0:T(8,128)(2,1)}), bf16[8,512,128]{2,1,0:T(8,128)(2,1)S(1)}, u32[]{:S(2)}, u32[]{:S(2)}) async-start(bf16[8,512,128]{2,1,0:T(8,128)(2,1)} %weight_copies.1), calls=%async_computation.1 | async-start | bytes 2097152 | tf_op jit(solution)/shard_map/all_to_all | solution.py:29
  26.1 2.5 %broadcast_select_fusion.1 = (bf16[392,1024]{1,0:T(8,128)(2,1)}, bf16[392,1024]{1,0:T(8,128)(2,1)S(1)}) fusion(pred[]{:T(512)S(6)} %eq.3, bf16[392,2048]{1,0:T(8,128)(2,1)} %param.7), kind=kLoop, calls=%fused_computation.2 | loop fusion | flops 802816 | bytes 3211265 | tf_op jit(solution)/shard_map/jit(_where)/select_n | solution.py:349
  28.6 2.0 %collective-permute-start.1 = (bf16[392,1024]{1,0:T(8,128)(2,1)}, bf16[392,1024]{1,0:T(8,128)(2,1)}, u32[]{:S(2)}, u32[]{:S(2)}) collective-permute-start(bf16[392,1024]{1,0:T(8,128)(2,1)} %get-tuple-element.52), channel_id=1, source_target_pairs={{0,1},{1,0},{2,3},{3,2},{4,5},{5,4},{6,7},{7,6},{8,9},{9,8},{10,11... | collective-permute-start | bytes 2408456 | tf_op jit(solution)/shard_map/ppermute | solution.py:25
  30.6 1.0 broadcast_select_fusion
  31.6 2.5 %collective-permute-start.2 = (bf16[392,1024]{1,0:T(8,128)(2,1)}, bf16[392,1024]{1,0:T(8,128)(2,1)}, u32[]{:S(2)}, u32[]{:S(2)}) collective-permute-start(bf16[392,1024]{1,0:T(8,128)(2,1)} %get-tuple-element.50), channel_id=1, source_target_pairs={{0,1},{1,0},{2,3},{3,2},{4,5},{5,4},{6,7},{7,6},{8,9},{9,8},{10,11... | collective-permute-start | bytes 2408456 | tf_op jit(solution)/shard_map/ppermute | solution.py:25
  34.2 1.9 %collective-permute-start = (bf16[392,512]{1,0:T(8,128)(2,1)S(1)}, bf16[392,512]{1,0:T(8,128)(2,1)S(1)}, u32[]{:S(2)}, u32[]{:S(2)}) collective-permute-start(bf16[392,512]{1,0:T(8,128)(2,1)S(1)} %copy-done), channel_id=1, source_target_pairs={{0,1},{1,0},{2,3},{3,2},{4,5},{5,4},{6,7},{7,6},{8,9},{9,8},{10,11... | collective-permute-start | bytes 1204232 | tf_op jit(solution)/shard_map/ppermute | solution.py:25
  36.1 1.7 %collective-permute-done.acts_other = bf16[392,512]{1,0:T(8,128)(2,1)S(1)} collective-permute-done((bf16[392,512]{1,0:T(8,128)(2,1)S(1)}, bf16[392,512]{1,0:T(8,128)(2,1)S(1)}, u32[]{:S(2)}, u32[]{:S(2)}) %collective-permute-start) | collective-permute-done | bytes 401440 | tf_op jit(solution)/shard_map/ppermute | solution.py:25
  37.8 3.3 %all-to-all-done.1.parts = bf16[8,512,128]{2,1,0:T(8,128)(2,1)S(1)} async-done(((bf16[8,512,128]{2,1,0:T(8,128)(2,1)}), bf16[8,512,128]{2,1,0:T(8,128)(2,1)S(1)}, u32[]{:S(2)}, u32[]{:S(2)}) %all-to-all-start.1) | async-done | bytes 1048608 | tf_op jit(solution)/shard_map/all_to_all | solution.py:29
  41.1 1.5 %moments.1 = (bf16[512,1024]{1,0:T(8,128)(2,1)S(1)}, f32[392,1024]{1,0:T(8,128)S(1)}, f32[392,1024]{1,0:T(8,128)S(1)}, f32[8,16,128]{2,1,0:T(8,128)S(1)}) custom-call(bf16[392,512]{1,0:T(8,128)(2,1)S(1)} %copy-done, bf16[392,512]{1,0:T(8,128)(2,1)S(1)} %collective-permute-done.acts_other, bf16[8,512,128]{2,1,0:T(8,128)(2,1)S(1)} %all-to-all-done.1.parts), custom_call_target="tpu_custom_call" | custom-call | tf_op jit(solution)/shard_map/moments/pallas_call | solution.py:324
  42.6 0.0 collective-permute-done.1.block_far
  42.6 0.0 collective-permute-done.2.out_far
  42.6 9.6 %all_to_all.41.moments = f32[8,16,128]{2,1,0:T(8,128)S(1)} all-to-all(f32[8,16,128]{2,1,0:T(8,128)S(1)} %get-tuple-element.32), channel_id=1, replica_groups=mesh['zh'=4,'zl'=2,'x'=4,'yh'=4,'yl'=2,'c'=2] {'yh','yl'}, dimensions={0} | all-to-all | bytes 131072 | tf_op jit(solution)/shard_map/all_to_all | solution.py:29
  52.3 0.0 copy-done.5
  52.3 2.0 %stats.1 = (bf16[392,1024]{1,0:T(8,128)(2,1)S(1)}, bf16[392,1024]{1,0:T(8,128)(2,1)S(1)}, f32[8,16,128]{2,1,0:T(8,128)S(1)}) custom-call(f32[392,1024]{1,0:T(8,128)S(1)} %get-tuple-element.29.conv, f32[392,1024]{1,0:T(8,128)S(1)} %get-tuple-element.30.conv_other, f32[8,16,128]{2,1,0:T(8,128)S(1)} %all_to_all.41.moments, f32[1,2048]{1,0:T(1,128)S(1)} %bitcast.6, ...), custom_call_target="tpu_custom_call" | custom-call | tf_op jit(solution)/shard_map/stats/pallas_call | solution.py:324
  54.3 9.7 %all_to_all.42.stats = f32[8,16,128]{2,1,0:T(8,128)S(1)} all-to-all(f32[8,16,128]{2,1,0:T(8,128)S(1)} %get-tuple-element.37), channel_id=1, replica_groups=mesh['zh'=4,'zl'=2,'x'=4,'yh'=4,'yl'=2,'c'=2] {'yh','yl'}, dimensions={0} | all-to-all | bytes 131072 | tf_op jit(solution)/shard_map/all_to_all | solution.py:29
  64.0 2.2 %weight_partial.1 = (f32[392,512]{1,0:T(8,128)S(1)}, bf16[392,512]{1,0:T(8,128)(2,1)S(1)}, f32[8,128]{1,0:T(8,128)S(1)}, bf16[16,272,128]{2,1,0:T(8,128)(2,1)}) custom-call(f32[392,1024]{1,0:T(8,128)S(1)} %get-tuple-element.29.conv, f32[392,1024]{1,0:T(8,128)S(1)} %get-tuple-element.30.conv_other, f32[8,16,128]{2,1,0:T(8,128)S(1)} %all_to_all.41.moments, ...), custom_call_target="tpu_custom_call" | custom-call | tf_op jit(solution)/shard_map/weight_partial/pallas_call | solution.py:324
  66.3 3.7 %all-to-all-start.4 = ((bf16[16,272,128]{2,1,0:T(8,128)(2,1)}), bf16[16,272,128]{2,1,0:T(8,128)(2,1)S(1)}, u32[]{:S(2)}, u32[]{:S(2)}) async-start(bf16[16,272,128]{2,1,0:T(8,128)(2,1)} %get-tuple-element.41), calls=%async_computation.4 | async-start | bytes 2228224 | tf_op jit(solution)/shard_map/all_to_all | solution.py:29
  70.0 4.8 %collective-permute-start.3 = (bf16[392,512]{1,0:T(8,128)(2,1)S(1)}, bf16[392,512]{1,0:T(8,128)(2,1)S(1)}, u32[]{:S(2)}, u32[]{:S(2)}) collective-permute-start(bf16[392,512]{1,0:T(8,128)(2,1)S(1)} %get-tuple-element.43), channel_id=1, source_target_pairs={{0,1},{1,0},{2,3},{3,2},{4,5},{5,4},{6,7},{7,6},{8,9},{9,8},{10,11... | collective-permute-start | bytes 1204232 | tf_op jit(solution)/shard_map/ppermute | solution.py:25
  74.8 1.3 %collective-permute-done.3 = bf16[392,512]{1,0:T(8,128)(2,1)S(1)} collective-permute-done((bf16[392,512]{1,0:T(8,128)(2,1)S(1)}, bf16[392,512]{1,0:T(8,128)(2,1)S(1)}, u32[]{:S(2)}, u32[]{:S(2)}) %collective-permute-start.3) | collective-permute-done | bytes 401440 | tf_op jit(solution)/shard_map/ppermute | solution.py:25
  76.2 0.9 add_convert_fusion
  77.0 8.9 %all-to-all-done.4.received = bf16[16,272,128]{2,1,0:T(8,128)(2,1)S(1)} async-done(((bf16[16,272,128]{2,1,0:T(8,128)(2,1)}), bf16[16,272,128]{2,1,0:T(8,128)(2,1)S(1)}, u32[]{:S(2)}, u32[]{:S(2)}) %all-to-all-start.4) | async-done | bytes 1114144 | tf_op jit(solution)/shard_map/all_to_all | solution.py:29
  85.9 0.2 near_sum.1
  86.1 23.5 %all_to_all.43.received = bf16[16,72,128]{2,1,0:T(8,128)(2,1)S(1)} all-to-all(bf16[16,72,128]{2,1,0:T(8,128)(2,1)S(1)} %near_sum.1), channel_id=1, replica_groups=mesh['zh'=4,'zl'=2,'x'=4,'yh'=4,'yl'=2,'c'=2] {'zh','yh'}, dimensions={0} | all-to-all | bytes 589824 | tf_op jit(solution)/shard_map/all_to_all | solution.py:29
  109.6 0.1 far_sum.1
  109.8 13.1 %all_to_all.44.parts = bf16[16,80,128]{2,1,0:T(8,128)(2,1)S(1)} all-to-all(bf16[16,80,128]{2,1,0:T(8,128)(2,1)S(1)} %far_sum.1), channel_id=1, replica_groups=mesh['zh'=4,'zl'=2,'x'=4,'yh'=4,'yl'=2,'c'=2] {'zl','x','c'}, dimensions={0} | all-to-all | bytes 655360 | tf_op jit(solution)/shard_map/all_to_all | solution.py:29
  122.9 10.0 %all_to_all.45.squares = f32[8,8,128]{2,1,0:T(8,128)S(1)} all-to-all(f32[8,8,128]{2,1,0:T(8,128)S(1)} %squares.1), channel_id=1, replica_groups=mesh['zh'=4,'zl'=2,'x'=4,'yh'=4,'yl'=2,'c'=2] {'yh','yl'}, dimensions={0} | all-to-all | bytes 65536 | tf_op jit(solution)/shard_map/all_to_all | solution.py:29
  132.9 0.0 copy-done.2
  132.9 0.8 step.1
  (12 shorter events, 0.1 us)
Async XLA Ops:
  0.6 0.9 copy-start.1
  21.1 20.0 %all-to-all-start.1 = ((bf16[8,512,128]{2,1,0:T(8,128)(2,1)}), bf16[8,512,128]{2,1,0:T(8,128)(2,1)S(1)}, u32[]{:S(2)}, u32[]{:S(2)}) async-start(bf16[8,512,128]{2,1,0:T(8,128)(2,1)} %weight_copies.1), calls=%async_computation.1 | async-start | bytes 2097152 | tf_op jit(solution)/shard_map/all_to_all | solution.py:29
  26.0 4.6 %copy-start.6 = (bf16[392,2048]{1,0:T(8,128)(2,1)S(1)}, bf16[392,2048]{1,0:T(8,128)(2,1)}, u32[]{:S(2)}) copy-start(bf16[392,2048]{1,0:T(8,128)(2,1)} %param.12) | copy-start | bytes 4816900
  28.6 5.6 %copy-start = (bf16[392,512]{1,0:T(8,128)(2,1)S(1)}, bf16[392,512]{1,0:T(8,128)(2,1)}, u32[]{:S(2)}) copy-start(bf16[392,512]{1,0:T(8,128)(2,1)} %acts.3) | copy-start | bytes 1204228
  28.6 14.1 %collective-permute-start.1 = (bf16[392,1024]{1,0:T(8,128)(2,1)}, bf16[392,1024]{1,0:T(8,128)(2,1)}, u32[]{:S(2)}, u32[]{:S(2)}) collective-permute-start(bf16[392,1024]{1,0:T(8,128)(2,1)} %get-tuple-element.52), channel_id=1, source_target_pairs={{0,1},{1,0},{2,3},{3,2},{4,5},{5,4},{6,7},{7,6},{8,9},{9,8},{10,11... | collective-permute-start | bytes 2408456 | tf_op jit(solution)/shard_map/ppermute | solution.py:25
  31.6 20.7 %copy-start.4 = (f32[2048]{0:T(1024)S(1)}, f32[2048]{0:T(1024)}, u32[]{:S(2)}) copy-start(f32[2048]{0:T(1024)} %param.10) | copy-start | bytes 24580
  31.6 20.7 %copy-start.5 = (f32[2048]{0:T(1024)S(1)}, f32[2048]{0:T(1024)}, u32[]{:S(2)}) copy-start(f32[2048]{0:T(1024)} %param.11) | copy-start | bytes 24580
  31.6 11.0 %collective-permute-start.2 = (bf16[392,1024]{1,0:T(8,128)(2,1)}, bf16[392,1024]{1,0:T(8,128)(2,1)}, u32[]{:S(2)}, u32[]{:S(2)}) collective-permute-start(bf16[392,1024]{1,0:T(8,128)(2,1)} %get-tuple-element.50), channel_id=1, source_target_pairs={{0,1},{1,0},{2,3},{3,2},{4,5},{5,4},{6,7},{7,6},{8,9},{9,8},{10,11... | collective-permute-start | bytes 2408456 | tf_op jit(solution)/shard_map/ppermute | solution.py:25
  34.2 3.6 %collective-permute-start = (bf16[392,512]{1,0:T(8,128)(2,1)S(1)}, bf16[392,512]{1,0:T(8,128)(2,1)S(1)}, u32[]{:S(2)}, u32[]{:S(2)}) collective-permute-start(bf16[392,512]{1,0:T(8,128)(2,1)S(1)} %copy-done), channel_id=1, source_target_pairs={{0,1},{1,0},{2,3},{3,2},{4,5},{5,4},{6,7},{7,6},{8,9},{9,8},{10,11... | collective-permute-start | bytes 1204232 | tf_op jit(solution)/shard_map/ppermute | solution.py:25
  66.3 19.7 %all-to-all-start.4 = ((bf16[16,272,128]{2,1,0:T(8,128)(2,1)}), bf16[16,272,128]{2,1,0:T(8,128)(2,1)S(1)}, u32[]{:S(2)}, u32[]{:S(2)}) async-start(bf16[16,272,128]{2,1,0:T(8,128)(2,1)} %get-tuple-element.41), calls=%async_computation.4 | async-start | bytes 2228224 | tf_op jit(solution)/shard_map/all_to_all | solution.py:29
  70.0 6.2 %collective-permute-start.3 = (bf16[392,512]{1,0:T(8,128)(2,1)S(1)}, bf16[392,512]{1,0:T(8,128)(2,1)S(1)}, u32[]{:S(2)}, u32[]{:S(2)}) collective-permute-start(bf16[392,512]{1,0:T(8,128)(2,1)S(1)} %get-tuple-element.43), channel_id=1, source_target_pairs={{0,1},{1,0},{2,3},{3,2},{4,5},{5,4},{6,7},{7,6},{8,9},{9,8},{10,11... | collective-permute-start | bytes 1204232 | tf_op jit(solution)/shard_map/ppermute | solution.py:25
  77.0 55.9 %copy-start.2 = (bf16[32,2048]{1,0:T(8,128)(2,1)S(1)}, bf16[32,2048]{1,0:T(8,128)(2,1)}, u32[]{:S(2)}) copy-start(bf16[32,2048]{1,0:T(8,128)(2,1)} %weight.3) | copy-start | bytes 393220
  77.0 55.9 %copy-start.3 = (f32[32,2048]{1,0:T(8,128)S(1)}, f32[32,2048]{1,0:T(8,128)}, u32[]{:S(2)}) copy-start(f32[32,2048]{1,0:T(8,128)} %velocity.1) | copy-start | bytes 786436
